TPU v7x, 128 devices: a whole 4x4x4 slice. The times are simulated.
128 devices in a mesh: grp: 2 (over core), dp: 64 (over x, y, z).
Axes of the slice: x: 4, y: 4, z: 4, core: 2. Of those that a mesh axis runs over, the one named last changes fastest.
Arguments:
- tokens: bfloat16 [2, 64, 576, 768], P('grp', 'dp'), may hold values from -6 to 6
- cotangent: bfloat16 [2, 64, 576, 768], P('grp', 'dp'), may hold values from -6 to 6
- counts: int32 [2, 64, 2], P('grp', 'dp'), may hold values from 0 to 576, as said below
- patch_row: int32 [2, 64, 576], P('grp', 'dp'), may hold values from 0 to 23, as said below
- patch_col: int32 [2, 64, 576], P('grp', 'dp'), may hold values from 0 to 23, as said below
- w_qkv: float32 [768, 2304], P('dp'), may hold values from -0.21650635 to 0.21650635
- w_proj: float32 [768, 768], P('dp'), may hold values from -4 to 4
- w_fc1: float32 [768, 3072], P('dp'), may hold values from -0.21875 to 0.21875
- w_fc2: float32 [3072, 768], P('dp'), may hold values from -0.109375 to 0.109375
- vectors: float32 [14, 768], P(None, 'dp')
- m_qkv: float32 [768, 2304], P('dp'), may hold values from -0.00061035156 to 0.00061035156
- v_qkv: float32 [768, 2304], P('dp'), may hold values from 8.182106e-09 to 3.244628e-08
- m_proj: float32 [768, 768], P('dp'), may hold values from -6.1035156e-05 to 6.1035156e-05
- v_proj: float32 [768, 768], P('dp'), may hold values from 9.02853e-11 to 3.5267697e-10
- m_fc1: float32 [768, 3072], P('dp'), may hold values from -3.8146973e-05 to 3.8146973e-05
- v_fc1: float32 [768, 3072], P('dp'), may hold values from 3.808911e-11 to 1.4953504e-10
- m_fc2: float32 [3072, 768], P('dp'), may hold values from -7.6293945e-05 to 7.6293945e-05
- v_fc2: float32 [3072, 768], P('dp'), may hold values from 1.4107078e-10 to 5.5017607e-10
- m_vectors: float32 [14, 768], P(None, 'dp'), may hold values from -0.0024414062 to 0.0024414062
- v_vectors: float32 [14, 768], P(None, 'dp'), may hold values from 1.1849946e-07 to 4.796407e-07
Outputs:
- mixed_out: bfloat16 [2, 64, 576, 768], P('grp', 'dp')
- grad_tokens: float32 [2, 64, 576, 768], P('grp', 'dp')
- grad_norm: float32 [], replicated
- qkv_new: float32 [768, 2304], P('dp')
- qkv_first: float32 [768, 2304], P('dp')
- qkv_second: float32 [768, 2304], P('dp')
- proj_new: float32 [768, 768], P('dp')
- proj_first: float32 [768, 768], P('dp')
- proj_second: float32 [768, 768], P('dp')
- fc1_new: float32 [768, 3072], P('dp')
- fc1_first: float32 [768, 3072], P('dp')
- fc1_second: float32 [768, 3072], P('dp')
- fc2_new: float32 [3072, 768], P('dp')
- fc2_first: float32 [3072, 768], P('dp')
- fc2_second: float32 [3072, 768], P('dp')
- vectors_new: float32 [14, 768], P(None, 'dp')
- vectors_first: float32 [14, 768], P(None, 'dp')
- vectors_second: float32 [14, 768], P(None, 'dp')
- bias_proj_grad: float32 [768], P('dp')
Inputs may be any that keep to these rules, and one draw needn't show every extreme that they name: counts[0, f, i] is the number of kept patches of image i of a first-group frame, 98 to 196; counts[1, f, 0] that of the one image of a second-group frame, 288 to 576; counts[1, f, 1] is 0. Kept patches fill their image's first slots. `patch_row`: the kept patches of one image sit at distinct grid positions (rows below 14 in the first group, 24 in the second); other slots hold any position. `patch_col`: column of the same positions.
All inputs are finite; a program needn't handle non-finite values.
Results may differ from a plain program's by a relative error of at most 0.023.
The roundings to bfloat16 on the way count: a program that leaves them out, or rounds other values in their place, can miss the bound.
Values may be sent and summed in bfloat16 or wider, within the bound.
No kernel may reach another device: no remote copies, remote signals or barrier semaphores. Data moves between devices by JAX's collectives and lax.ppermute only.
A program may use at most 192 MiB of HBM per device.

v0:
```python
import jax
import jax.numpy as jnp
from jax import lax
from jax.experimental import pallas as pl
from jax.experimental.pallas import tpu as pltpu
from jax.sharding import PartitionSpec as P

D = 768
H = 12
HD = 64
FF = 3072
STEP = 10
A = 196
S = 576

CORES = 2
HC = H // CORES
DC = D // CORES
FC = FF // CORES
PAIRS = HC // 2
T = CORES * S

WIN = 208
WINDOWS = (0, 192)

EPS_NORM = 1e-06
BETA_ONE = 0.9
BETA_TWO = 0.95
ADAM_EPS = 1e-08
DECAY_RATE = 0.05
RATE_VECTOR = 0.8
CLIP_LIMIT = 1.0
NEG = -1e30

bf16 = jnp.bfloat16
f32 = jnp.float32
VMEM_LIMIT = 56 * 1024 * 1024


SIDE = 4
CHIPS = SIDE**3
PLANE = SIDE * SIDE
KR = D // CHIPS
FR = FC // CHIPS
BLOCK = SIDE * KR
QUARTER = PLANE * KR
BOTH = ("grp", "dp")


def device(core, x, y, z):
    return ((core * SIDE + x) * SIDE + y) * SIDE + z


def lines():
    r = range(SIDE)
    return [[device(0, a, g, z) for a in r] for g in r for z in r] + [
        [device(1, g, a, z) for a in r] for g in r for z in r
    ]


def planes():
    r = range(SIDE)
    return [[device(0, a, g, z) for g in r for z in r] for a in r] + [
        [device(1, g, a, z) for g in r for z in r] for a in r
    ]


def shift(value, d):
    pairs = [(group[i], group[(i + d) % SIDE]) for group in lines() for i in range(SIDE)]
    return lax.ppermute(value, BOTH, pairs)


def plane_swap(value):
    return lax.all_to_all(value, BOTH, 0, 0, axis_index_groups=planes())


def natural(core, a, g):
    return jnp.where(core == 0, SIDE * a + g, SIDE * g + a)


def lay_out(place_ref, pieces, full_ref):
    core, me = place_ref[0], place_ref[1]
    for d, piece in enumerate(pieces):
        a = (me + SIDE - d) & (SIDE - 1)
        for g in range(SIDE):
            at = pl.multiple_of(natural(core, a, g) * BLOCK, BLOCK)
            full_ref[pl.ds(at, BLOCK), :] = piece[g * BLOCK : (g + 1) * BLOCK, :]


def usable_rows(place_ref, group, rows, base=0):
    slot = lax.broadcasted_iota(jnp.int32, (rows, 1), 0) + base
    first = ((slot < A) & (slot < place_ref[2])) | ((slot >= A) & (slot < 2 * A) & (slot - A < place_ref[3]))
    first = first.astype(f32)
    second = (slot < place_ref[4]).astype(f32)
    if isinstance(group, int):
        return second if group else first
    return jnp.where(group == 0, first, second)


def own_rows(win):
    row = lax.broadcasted_iota(jnp.int32, (WIN, 1), 0) + (WINDOWS[win] - win * A)
    return ((row >= 0) & (row < A)).astype(f32)


def key_bias(place_ref, win=None):
    if win is None:
        key = lax.broadcasted_iota(jnp.int32, (1, S), 1)
        return jnp.where(key < place_ref[4], 0.0, NEG)
    key = lax.broadcasted_iota(jnp.int32, (1, WIN), 1) + (WINDOWS[win] - win * A)
    return jnp.where((key >= 0) & (key < place_ref[2 + win]), 0.0, NEG)


def exact_dot(a, b):
    high = a.astype(bf16)
    rest = a - high.astype(f32)
    mid = rest.astype(bf16)
    low = (rest - mid.astype(f32)).astype(bf16)
    b = b.astype(bf16)
    return dot(high, b) + dot(mid, b) + dot(low, b)


def spots(core, shape, full, part):
    l = lax.broadcasted_iota(jnp.int32, shape, full)
    m = lax.broadcasted_iota(jnp.int32, shape, part)
    q = (m * 2731) >> 16
    return l == m + FR * (q + core)


def spots_t(core):
    return spots(core, (DC, D), 1, 0)


def params(**kw):
    return pltpu.CompilerParams(vmem_limit_bytes=VMEM_LIMIT, **kw)


def cost(flops, bytes_accessed, transcendentals=0):
    return pl.CostEstimate(
        flops=int(flops), bytes_accessed=int(bytes_accessed), transcendentals=int(transcendentals)
    )


def dot(a, b):
    return jnp.dot(a, b, preferred_element_type=f32)


def dot_t(a, b):
    return lax.dot_general(a, b, (((1,), (1,)), ((), ())), preferred_element_type=f32)


def t_dot(a, b):
    return lax.dot_general(a, b, (((0,), (0,)), ((), ())), preferred_element_type=f32)


def stats(z):
    mean_val = jnp.mean(z, axis=-1, keepdims=True)
    centred = z - mean_val
    variance = jnp.mean(centred * centred, axis=-1, keepdims=True)
    inv_std = lax.rsqrt(variance + EPS_NORM)
    return centred * inv_std, inv_std


def norm_back(grad, normed, inv_std, gain):
    e = grad * gain
    return inv_std * (
        e
        - jnp.mean(e, axis=-1, keepdims=True)
        - normed * jnp.mean(e * normed, axis=-1, keepdims=True)
    )


def swap_halves(u):
    lanes = u.shape[1]
    lane = lax.broadcasted_iota(jnp.int32, u.shape, 1)
    up = pltpu.roll(u, lanes - HD // 2, 1)
    down = pltpu.roll(u, HD // 2, 1)
    return jnp.where((lane & (HD - 1)) < HD // 2, up, down)


TURN = 1.5707963267948966


def sin_cos(a):
    k = jnp.floor(a * (1.0 / TURN) + 0.5)
    r = ((a - k * 1.5703125) - k * 4.837512969970703125e-4) - k * 7.54978995489188216e-8
    z = r * r
    s = ((-1.9515295891e-4 * z + 8.3321608736e-3) * z - 1.6666654611e-1) * z * r + r
    c = ((2.443315711809948e-5 * z - 1.388731625493765e-3) * z + 4.166664568298827e-2) * z * z - 0.5 * z + 1.0
    quarter = k.astype(jnp.int32)
    odd = (quarter & 1) == 1
    sine = jnp.where(odd, c, s)
    cosine = jnp.where(odd, s, c)
    sine = jnp.where((quarter & 2) == 0, sine, -sine)
    cosine = jnp.where(((quarter + 1) & 2) == 0, cosine, -cosine)
    return sine, cosine


def share_kernel(place_ref, w_ref, v_ref, out_ref):
    core = place_ref[0]
    w = w_ref[...].astype(bf16)
    cols = []
    for p in range(PAIRS):
        for i in range(3):
            at = i * D + p * 128
            cols.append(jnp.where(core == 0, w[:, at : at + 128], w[:, at + DC : at + DC + 128]))
    v = jnp.concatenate([v_ref[...], jnp.zeros((128 - v_ref.shape[0], KR), f32)], axis=0)
    v = jnp.concatenate([v, jnp.zeros((128, 128 - KR), f32)], axis=1)
    cols.append(v.T[:KR, :].astype(bf16))
    share = jnp.concatenate(cols, axis=1)
    for n in range(PLANE):
        out_ref[n] = share


def share_call(place, w, vectors):
    whole = lambda a: pl.BlockSpec(a.shape, lambda i, c: (0, 0))
    return pl.pallas_call(
        share_kernel,
        grid_spec=pltpu.PrefetchScalarGridSpec(
            num_scalar_prefetch=1,
            grid=(1,),
            in_specs=[whole(w), whole(vectors)],
            out_specs=pl.BlockSpec((PLANE, KR, 3 * DC + 128), lambda i, c: (0, 0, 0)),
        ),
        out_shape=jax.ShapeDtypeStruct((PLANE, KR, 3 * DC + 128), bf16),
        compiler_params=params(),
        cost_estimate=cost(KR * D * 3, 1e6),
    )(place, w, vectors)


def gy_kernel(place_ref, c_ref, co_ref, gy_ref):
    i = pl.program_id(0)
    keep = usable_rows(place_ref, i ^ place_ref[0], S)
    gy_ref[...] = (jnp.where(i == 0, c_ref[...], co_ref[...]).astype(f32) * keep).astype(bf16)


def gy_call(place, c, co):
    whole = pl.BlockSpec((S, D), lambda i, c: (0, 0))
    return pl.pallas_call(
        gy_kernel,
        grid_spec=pltpu.PrefetchScalarGridSpec(
            num_scalar_prefetch=1,
            grid=(CORES,),
            in_specs=[whole, whole],
            out_specs=pl.BlockSpec((S, D), lambda i, c: (i, 0)),
        ),
        out_shape=jax.ShapeDtypeStruct((T, D), bf16),
        compiler_params=params(),
        cost_estimate=cost(4 * T * D, T * D * 4),
    )(place, c, co)


def qkv_kernel(
    place_ref, x_ref, xo_ref, ints_ref, w0, w1, w2, w3, v0, v1, v2, v3,
    vec_ref, ht_ref, cos_ref, sin_ref, q_out, k_out, v_out, b1_ref, pos_ref,
    w_s, full_s, rows_s, freq_s,
):
    core = place_ref[0]

    @pl.when(pl.program_id(0) == 0)
    def _():
        lay_out(place_ref, (w0, w1, w2, w3), w_s)
        lay_out(place_ref, (v0, v1, v2, v3), full_s)
        rows_s[...] = full_s[...].astype(f32).T[:16, :]
        vec_ref[...] = rows_s[...]
        late = rows_s[8:16, :].astype(bf16)
        units = dot(late, spots(core, (D, DC), 0, 1).astype(bf16))
        for r in range(FC // DC):
            b1_ref[:, r * DC : (r + 1) * DC] = units[2 + r : 3 + r, :]
        src = lax.broadcasted_iota(jnp.int32, (D, DC), 0)
        dst = lax.broadcasted_iota(jnp.int32, (D, DC), 1)
        want = core * (DC // 2) + (dst // HD) * (HD // 2) + (dst & (HD // 2 - 1))
        freq_s[0:8, :] = dot(late, (src == want).astype(bf16))
        freq_s[8:16, :] = dot(late, (src == want + D // 2).astype(bf16))

    i = pl.program_id(0)
    x = jnp.where(i < pl.num_programs(0) // CORES, x_ref[...], xo_ref[...])
    h = stats(x.astype(f32))[0] * rows_s[0:1, :] + rows_s[1:2, :]
    pos = ints_ref[...].astype(f32).T
    pos_ref[...] = pos
    ht_ref[...] = h.T.astype(bf16)
    acc = dot(h.astype(bf16), w_s[...])
    angle = pos[:, 1:2] * freq_s[1:2, :] + pos[:, 0:1] * freq_s[9:10, :]
    lane = lax.broadcasted_iota(jnp.int32, (1, DC), 1)
    sign = jnp.where((lane & (HD - 1)) < HD // 2, -1.0, 1.0)
    small = jnp.max(jnp.abs(angle)) < 8000.0

    @pl.when(small)
    def _():
        sine, cosine = sin_cos(angle)
        cos_ref[...] = cosine
        sin_ref[...] = sine * sign

    @pl.when(jnp.logical_not(small))
    def _():
        cos_ref[...] = jnp.cos(angle)
        sin_ref[...] = jnp.sin(angle) * sign

    cosine, sine = cos_ref[...], sin_ref[...]
    at = pl.ds(pl.multiple_of(core * DC, DC), DC)
    part = lambda i: jnp.concatenate([acc[:, (3 * p + i) * 128 : (3 * p + i + 1) * 128] for p in range(PAIRS)], axis=1)
    q = part(0) + rows_s[4:5, at]
    k = part(1) + rows_s[5:6, at]
    q_out[...] = ((q * cosine + swap_halves(q) * sine) * HD ** (-0.5)).astype(bf16)
    k_out[...] = (k * cosine + swap_halves(k) * sine).astype(bf16)
    v_out[...] = (part(2) + rows_s[6:7, at]).astype(bf16)


def qkv_call(place, x, xo, ints, pieces):
    rows = S
    tile = lambda n: pl.BlockSpec((rows, n), lambda i, c: (i, 0))
    keep = lambda *n: pl.BlockSpec(n, lambda i, c: (0,) * len(n))
    return pl.pallas_call(
        qkv_kernel,
        grid_spec=pltpu.PrefetchScalarGridSpec(
            num_scalar_prefetch=1,
            grid=(CORES,),
            in_specs=[keep(S, D), keep(S, D), pl.BlockSpec((None, 8, S), lambda i, c: (i, 0, 0))]
            + [keep(QUARTER, 3 * DC)] * 4
            + [pl.BlockSpec((QUARTER, 128), lambda i, c: (0, 3 * DC // 128))] * 4,
            out_specs=[keep(16, D), pl.BlockSpec((None, D, rows), lambda i, c: (i, 0, 0))]
            + [tile(DC)] * 5
            + [keep(1, FC), tile(8)],
            scratch_shapes=[
                pltpu.VMEM((D, 3 * DC), bf16),
                pltpu.VMEM((D, 128), bf16),
                pltpu.VMEM((16, D), f32),
                pltpu.VMEM((16, DC), f32),
            ],
        ),
        out_shape=[
            jax.ShapeDtypeStruct((16, D), f32),
            jax.ShapeDtypeStruct((CORES, D, S), bf16),
            jax.ShapeDtypeStruct((T, DC), f32),
            jax.ShapeDtypeStruct((T, DC), f32),
            *[jax.ShapeDtypeStruct((T, DC), bf16)] * 3,
            jax.ShapeDtypeStruct((1, FC), f32),
            jax.ShapeDtypeStruct((T, 8), f32),
        ],
        compiler_params=params(),
        cost_estimate=cost(2 * T * D * 3 * DC + 60 * T * DC, T * D * 6 + D * 3 * DC * 2 + T * DC * 14),
    )(place, x, xo, ints, *pieces, *pieces)


def softmax_head(q, k, v, mine, bias):
    s = dot_t(jnp.where(mine, q, jnp.zeros_like(q)), k) + bias
    e = jnp.exp(s - jnp.max(s, axis=-1, keepdims=True))
    p = e * (1.0 / jnp.sum(e, axis=-1, keepdims=True))
    return p


def attn_fwd_kernel(
    place_ref, q0, k0, v0, q1, k1, v1, o_ref, p0_ref, p1_ref
):
    lane = lax.broadcasted_iota(jnp.int32, (1, 2 * HD), 1)
    low = lane < HD
    q, k, v = q1[0], k1[0], v1[0]
    mixes = []
    bias = key_bias(place_ref)
    for head, mine in ((0, low), (1, ~low)):
        p = softmax_head(q, k, v, mine, bias).astype(bf16)
        p1_ref[head] = p
        mixes.append(dot(p, v))
    mix = jnp.where(low, mixes[0], mixes[1])
    o_ref[1] = jnp.where(usable_rows(place_ref, 1, S) > 0, mix, v.astype(f32)).astype(bf16)
    o_ref[0] = v0[0]
    for win, base in enumerate(WINDOWS):
        q, k, v = (r[0, base : base + WIN, :] for r in (q0, k0, v0))
        own = own_rows(win)
        bias = key_bias(place_ref, win)
        mixes = []
        for head, mine in ((0, low), (1, ~low)):
            p = softmax_head(q, k, v, mine, bias)
            p = (p * own).astype(bf16)
            p0_ref[head, win] = p
            mixes.append(dot(p, v))
        mix = jnp.where(low, mixes[0], mixes[1])
        use = (own * usable_rows(place_ref, 0, WIN, base)) > 0
        before = o_ref[0, base : base + WIN, :].astype(f32)
        o_ref[0, base : base + WIN, :] = jnp.where(use, mix, before).astype(bf16)


def attn_fwd_call(place, q, k, v):
    block = lambda g: pl.BlockSpec((1, S, 2 * HD), lambda p, c: (g ^ c[0], 0, p))
    q, k, v = (a.reshape(CORES, S, DC) for a in (q, k, v))
    return pl.pallas_call(
        attn_fwd_kernel,
        grid_spec=pltpu.PrefetchScalarGridSpec(
            num_scalar_prefetch=1,
            grid=(PAIRS,),
            in_specs=[block(0)] * 3 + [block(1)] * 3,
            out_specs=[
                pl.BlockSpec((CORES, S, 2 * HD), lambda p, c: (0, 0, p)),
                pl.BlockSpec((2, 2, WIN, WIN), lambda p, c: (p, 0, 0, 0)),
                pl.BlockSpec((2, S, S), lambda p, c: (p, 0, 0)),
            ],
        ),
        out_shape=[
            jax.ShapeDtypeStruct((CORES, S, DC), bf16),
            jax.ShapeDtypeStruct((HC, 2, WIN, WIN), bf16),
            jax.ShapeDtypeStruct((HC, S, S), bf16),
        ],
        compiler_params=params(),
        cost_estimate=cost(4 * HC * (S * S + 2 * WIN * WIN) * 128, 12e6, HC * S * S),
    )(place, q, k, v, q, k, v)


def proj_kernel(place_ref, mine_ref, other_ref, x_ref, xo_ref, w0, w1, w2, w3, v_ref, after_ref, n2_ref, r2_ref, h2_ref, w_s):
    @pl.when(pl.program_id(0) == 0)
    def _():
        lay_out(place_ref, (w0, w1, w2, w3), w_s)

    core = place_ref[0]
    at = lambda c: pl.ds(pl.multiple_of(c * DC, DC), DC)
    branch = dot(mine_ref[0], w_s[at(core), :]) + dot(other_ref[0], w_s[at(1 - core), :])
    x = jnp.where(pl.program_id(0) < pl.num_programs(0) // CORES, x_ref[...], xo_ref[...])
    after = x.astype(f32) + (branch + v_ref[7:8, :])
    normed, inv_std = stats(after)
    n2_ref[...] = normed
    r2_ref[...] = jnp.broadcast_to(inv_std, r2_ref.shape)

    @pl.when(pl.program_id(0) < pl.num_programs(0) // CORES)
    def _():
        after_ref[...] = after

    h2_ref[...] = (normed * v_ref[2:3, :] + v_ref[3:4, :]).astype(bf16)


def proj_call(place, mine, other, x, xo, pieces, vec):
    rows = 288
    half = S // rows
    tile = lambda n: pl.BlockSpec((rows, n), lambda i, c: (i, 0))
    whole = lambda a: pl.BlockSpec(a.shape, lambda i, c: (0,) * a.ndim)
    return pl.pallas_call(
        proj_kernel,
        grid_spec=pltpu.PrefetchScalarGridSpec(
            num_scalar_prefetch=1,
            grid=(T // rows,),
            in_specs=[
                pl.BlockSpec((1, rows, DC), lambda i, c: ((i // half) ^ c[0], i % half, 0)),
                pl.BlockSpec((1, rows, DC), lambda i, c: ((i // half) ^ c[0], i % half, 0)),
                pl.BlockSpec((rows, D), lambda i, c: (jnp.minimum(i, half - 1), 0)),
                pl.BlockSpec((rows, D), lambda i, c: (jnp.maximum(i - half, 0), 0)),
            ]
            + [pl.BlockSpec((QUARTER, D), lambda i, c: (0, FC // D))] * 4
            + [whole(vec)],
            out_specs=[pl.BlockSpec((rows, D), lambda i, c: (jnp.minimum(i, half - 1), 0)), tile(D), tile(8), tile(D)],
            scratch_shapes=[pltpu.VMEM((D, D), bf16)],
        ),
        out_shape=[
            jax.ShapeDtypeStruct((S, D), f32),
            jax.ShapeDtypeStruct((T, D), f32),
            jax.ShapeDtypeStruct((T, 8), f32),
            jax.ShapeDtypeStruct((T, D), bf16),
        ],
        compiler_params=params(),
        cost_estimate=cost(2 * T * D * D, T * D * 10 + D * D * 2),
    )(place, mine, other, x, xo, *pieces, vec)


PACK = 4 * DC + 128
K0 = (2.0 / 3.141592653589793) ** 0.5
FT = 768


def gelu_slope(u):
    sq = u * u
    th = jnp.tanh(u * (K0 + (K0 * 0.044715) * sq))
    half = 0.5 + 0.5 * th
    return u * half, half + (u * (half - half * half)) * (2 * K0 + (6 * K0 * 0.044715) * sq)


def mlp_kernel(
    place_ref, h2_ref, gy_ref, w10, w11, w12, w13, w2_ref, b1_ref, mlp_ref, mlpo_ref, gh2b_ref, act_ref, gup_ref, gb1_ref, w1_s
):
    i = pl.program_id(0)

    @pl.when(i == 0)
    def _():
        lay_out(place_ref, (w10, w11, w12, w13), w1_s)
        gb1_ref[...] = jnp.zeros_like(gb1_ref)

    for f in range(FC // FT):
        c = slice(f * FT, (f + 1) * FT)
        act, slope = gelu_slope(dot(h2_ref[...], w1_s[:, c]) + b1_ref[:, c])
        act_ref[:, c] = act.astype(bf16)
        gup = (dot_t(gy_ref[...], w2_ref[c, :]) * slope).astype(bf16)
        gup_ref[:, c] = gup
        gb1_ref[:, c] += jnp.sum(gup.astype(f32), axis=0, keepdims=True)
    gh2b_ref[...] = dot_t(gup_ref[...], w1_s[...]).astype(bf16)
    mlp = dot(act_ref[...], w2_ref[...])
    half = pl.num_programs(0) // CORES

    @pl.when(i < half)
    def _():
        mlp_ref[...] = mlp

    @pl.when(i >= half)
    def _():
        mlpo_ref[...] = mlp


def mlp_call(place, h2, gy, pieces, w2, b1):
    rows = 288
    half = S // rows
    tile = lambda n: pl.BlockSpec((rows, n), lambda i, c: (i, 0))
    whole = lambda a: pl.BlockSpec(a.shape, lambda i, c: (0,) * a.ndim)
    return pl.pallas_call(
        mlp_kernel,
        grid_spec=pltpu.PrefetchScalarGridSpec(
            num_scalar_prefetch=1,
            grid=(T // rows,),
            in_specs=[tile(D), tile(D)]
            + [pl.BlockSpec((QUARTER, FC), lambda i, c: (0, 0))] * 4
            + [whole(w2), whole(b1)],
            out_specs=[
                pl.BlockSpec((rows, D), lambda i, c: (jnp.minimum(i, half - 1), 0)),
                pl.BlockSpec((rows, D), lambda i, c: (jnp.maximum(i - half, 0), 0)),
                tile(D),
                tile(FC),
                tile(FC),
                pl.BlockSpec((1, FC), lambda i, c: (0, 0)),
            ],
            scratch_shapes=[pltpu.VMEM((D, FC), bf16)],
        ),
        out_shape=[
            jax.ShapeDtypeStruct((S, D), f32),
            jax.ShapeDtypeStruct((S, D), f32),
            jax.ShapeDtypeStruct((T, D), bf16),
            jax.ShapeDtypeStruct((T, FC), bf16),
            jax.ShapeDtypeStruct((T, FC), bf16),
            jax.ShapeDtypeStruct((1, FC), f32),
        ],
        compiler_params=params(),
        cost_estimate=cost(8 * T * D * FC, 30e6, T * FC),
    )(place, h2, gy, *pieces, w2, b1)


def by_line(place_ref, value, block, out_ref):
    core = place_ref[0]
    for n in range(PLANE):
        to = jnp.where(core == 0, n, (n % SIDE) * SIDE + n // SIDE)
        out_ref[pl.ds(pl.multiple_of(to * block, block), block), :] = value[n * block : (n + 1) * block, :].astype(bf16)


def fc_grad_kernel(place_ref, h2_ref, gup_ref, act_ref, gy_ref, gw1_ref, gw2_ref):
    by_line(place_ref, t_dot(act_ref[...], gy_ref[...]), SIDE * FR, gw2_ref)
    by_line(place_ref, t_dot(h2_ref[...], gup_ref[...]), BLOCK, gw1_ref)


def fc_grad_call(place, h2, gup, act, gy):
    whole = lambda a: pl.BlockSpec(a.shape, lambda i, c: (0, 0))
    return pl.pallas_call(
        fc_grad_kernel,
        grid_spec=pltpu.PrefetchScalarGridSpec(
            num_scalar_prefetch=1,
            grid=(2,),
            in_specs=[
                whole(h2),
                pl.BlockSpec((T, FC // 2), lambda i, c: (0, i)),
                whole(act),
                pl.BlockSpec((T, DC), lambda i, c: (0, i)),
            ],
            out_specs=[
                pl.BlockSpec((D, FC // 2), lambda i, c: (0, i)),
                pl.BlockSpec((FC, DC), lambda i, c: (0, i)),
            ],
        ),
        out_shape=[jax.ShapeDtypeStruct((D, FC), bf16), jax.ShapeDtypeStruct((FC, D), bf16)],
        compiler_params=params(),
        cost_estimate=cost(4 * T * D * FC, T * (D + FC) * 4 + D * FC * 4),
    )(place, h2, gup, act, gy)


def mid_kernel(place_ref, n2_ref, r2_ref, gy_ref, gh2_ref, other_ref, v_ref, ga_ref, gab_ref, sums_ref):
    i = pl.program_id(0)
    normed, inv_std = n2_ref[...], r2_ref[:, 0:1]
    gh2 = gh2_ref[...].astype(f32) + other_ref[...].astype(f32)
    gy = gy_ref[...].astype(f32)
    ga = gy + norm_back(gh2, normed, inv_std, v_ref[2:3, :])
    gab = ga.astype(bf16)
    gab_ref[...] = gab

    @pl.when(i == 0)
    def _():
        sums_ref[...] = jnp.zeros_like(sums_ref)

    @pl.when(i < pl.num_programs(0) // CORES)
    def _():
        ga_ref[...] = ga
        sums_ref[0:1, :] += jnp.sum(gh2 * normed, axis=0, keepdims=True)
        sums_ref[1:2, :] += jnp.sum(gh2, axis=0, keepdims=True)
        sums_ref[2:3, :] += jnp.sum(gab.astype(f32), axis=0, keepdims=True)
        sums_ref[3:4, :] += jnp.sum(gy, axis=0, keepdims=True)


def mid_call(place, n2, r2, gy, gh2, other, vec):
    rows = 288
    half = S // rows
    tile = lambda n: pl.BlockSpec((rows, n), lambda i, c: (i, 0))
    flipped = pl.BlockSpec((rows, D), lambda i, c: ((i + half) % (2 * half), 0))
    whole = lambda a: pl.BlockSpec(a.shape, lambda i, c: (0,) * a.ndim)
    return pl.pallas_call(
        mid_kernel,
        grid_spec=pltpu.PrefetchScalarGridSpec(
            num_scalar_prefetch=1,
            grid=(T // rows,),
            in_specs=[tile(D), tile(8), tile(D), tile(D), flipped, whole(vec)],
            out_specs=[
                pl.BlockSpec((rows, D), lambda i, c: (jnp.minimum(i, half - 1), 0)),
                tile(D),
                pl.BlockSpec((8, D), lambda i, c: (0, 0)),
            ],
        ),
        out_shape=[
            jax.ShapeDtypeStruct((S, D), f32),
            jax.ShapeDtypeStruct((T, D), bf16),
            jax.ShapeDtypeStruct((8, D), f32),
        ],
        compiler_params=params(),
        cost_estimate=cost(30 * T * D, T * D * 14),
    )(place, n2, r2, gy, gh2, other, vec)


def back_head(q_t, k, v, do, do_t, delta, p, mine, head):
    gp = dot_t(jnp.where(mine, do, jnp.zeros_like(do)), v)
    gs = (p.astype(f32) * (gp - delta)).astype(bf16)
    at = slice(head * HD, (head + 1) * HD)
    return dot(gs, k), dot(q_t[at, :], gs), dot(do_t[at, :], p)


def deltas(do, o, low):
    prod = do.astype(f32) * o.astype(f32)
    d0 = jnp.sum(jnp.where(low, prod, 0.0), axis=-1, keepdims=True)
    d1 = jnp.sum(jnp.where(low, 0.0, prod), axis=-1, keepdims=True)
    return d0, d1


def attn_bwd_kernel(
    place_ref,
    q0, k0, v0, o0, p0, cos0, sin0, pos0,
    q1, k1, v1, o1, p1, cos1, sin1, pos1,
    h1t_ref, ga_ref, cols_ref, mine_ref, other_ref, y0, y1, y2, y3, w0, w1, w2, w3,
    x_ref, xo_ref, mid_ref, gb1_ref,
    gw0, gw1, gw2, gw3, gh_ref, gho_ref,
    gq_s, gk_s, gv_s, gw_s, y_s, do_s, gqkv_s, att_s, rows_s, full_s, w_s,
):
    lane = lax.broadcasted_iota(jnp.int32, (1, 2 * HD), 1)
    low = lane < HD
    pair = pl.program_id(0)
    core = place_ref[0]

    @pl.when(pair == 0)
    def _():
        lay_out(place_ref, (y0, y1, y2, y3), y_s)

    wy = y_s[pl.ds(pl.multiple_of(core * DC + pair * 2 * HD, 2 * HD), 2 * HD), :]
    for frame in range(CORES):
        do_s[frame] = dot_t(ga_ref[frame], wy).astype(bf16)

    def finish(frame, q, k, cos_ref, sin_ref, pos_ref):
        cosine, sine = cos_ref[0], sin_ref[0]
        gq = gq_s[...] * HD ** (-0.5)
        gk = gk_s[...]
        sq, sk = swap_halves(gq), swap_halves(gk)
        turn = (q.astype(f32) * HD**0.5) * sq + k.astype(f32) * sk
        gq = (gq * cosine - sq * sine).astype(bf16)
        gk = (gk * cosine - sk * sine).astype(bf16)
        gv = gv_s[...].astype(bf16)
        for i, g in enumerate((gq, gk, gv)):
            gqkv_s[frame ^ core, :, pl.ds(pl.multiple_of(pair * 6 * HD + i * 2 * HD, 2 * HD), 2 * HD)] = g
        pos = pos_ref[0]
        col = jnp.sum(turn * pos[:, 1:2], axis=0, keepdims=True)
        row = jnp.sum(turn * pos[:, 0:1], axis=0, keepdims=True)
        bias = [jnp.sum(g.astype(f32), axis=0, keepdims=True) for g in (gq, gk, gv)]
        return jnp.concatenate([col, row] + bias, axis=0)

    q, k, v, do = q1[0], k1[0], v1[0], do_s[1 ^ core]
    d = deltas(do, o1[0], low)
    q_t, do_t = q.astype(f32).T.astype(bf16), do.astype(f32).T.astype(bf16)
    out = [
        back_head(q_t, k, v, do, do_t, d[head], p1[head], mine, head)
        for head, mine in ((0, low), (1, ~low))
    ]
    gq_s[...] = jnp.where(low, out[0][0], out[1][0])
    gk_s[...] = jnp.concatenate([out[0][1], out[1][1]], axis=0).T
    gv_s[...] = jnp.concatenate([out[0][2], out[1][2]], axis=0).T
    sums1 = finish(1, q, k, cos1, sin1, pos1)
    gq_s[...] = jnp.zeros_like(gq_s)
    gk_s[...] = jnp.zeros_like(gk_s)
    gv_s[...] = jnp.zeros_like(gv_s)
    for win, base in enumerate(WINDOWS):
        at = pl.ds(base, WIN)
        q, k, v, o = (r[0, at, :] for r in (q0, k0, v0, o0))
        do = do_s[core, at, :]
        d = deltas(do, o, low)
        q_t, do_t = q.astype(f32).T.astype(bf16), do.astype(f32).T.astype(bf16)
        out = [
            back_head(q_t, k, v, do, do_t, d[head], p0[head, win], mine, head)
            for head, mine in ((0, low), (1, ~low))
        ]
        gq_s[at, :] += jnp.where(low, out[0][0], out[1][0])
        gk_s[at, :] += jnp.concatenate([out[0][1], out[1][1]], axis=0).T
        gv_s[at, :] += jnp.concatenate([out[0][2], out[1][2]], axis=0).T
    sums0 = finish(0, q0[0], k0[0], cos0, sin0, pos0)
    att_s[pair, 0:5, :] = sums0 + sums1

    gw = jnp.zeros((D, 6 * HD), f32)
    gw_mine = jnp.zeros((2 * HD, DC), f32)
    gw_other = jnp.zeros((2 * HD, DC), f32)
    for frame in range(CORES):
        cols = cols_ref[frame].astype(f32).T.astype(bf16)
        gw_mine += dot(cols, mine_ref[frame ^ core])
        gw_other += dot(cols, other_ref[frame ^ core])
        gw += dot(h1t_ref[frame], gqkv_s[frame, :, pl.ds(pl.multiple_of(pair * 6 * HD, 6 * HD), 6 * HD)])
    gw_s[:, : 6 * HD] = gw.astype(bf16)
    at = lambda c: pl.ds(pl.multiple_of(c * DC, DC), DC)
    gw_s[at(core), 6 * HD :] = gw_mine.T.astype(bf16)
    gw_s[at(1 - core), 6 * HD :] = gw_other.T.astype(bf16)
    to_chips(place_ref, gw_s, (gw0, gw1, gw2, gw3), pl.ds(pl.multiple_of(pair * 8 * HD, 8 * HD), 8 * HD))

    @pl.when(pair == PAIRS - 1)
    def _():
        lay_out(place_ref, (w0, w1, w2, w3), w_s)
        rows_s[...] = jnp.zeros_like(rows_s)
        for frame, x, out in ((0, x_ref, gh_ref), (1, xo_ref, gho_ref)):
            for half in range(2):
                at = slice(half * (S // 2), (half + 1) * (S // 2))
                gh = dot_t(gqkv_s[frame, at, :], w_s[...])
                out[at, :] = gh
                normed, _ = stats(x[at, :].astype(f32))
                rows_s[0:1, :] += jnp.sum(gh * normed, axis=0, keepdims=True)
                rows_s[1:2, :] += jnp.sum(gh, axis=0, keepdims=True)
        rows_s[2:4, :] = mid_ref[0:2, :]
        rows_s[7:9, :] = mid_ref[2:4, :]
        att = jnp.concatenate([att_s[p] for p in range(PAIRS)], axis=1)
        rows_s[4:7, pl.ds(pl.multiple_of(core * DC, DC), DC)] = att[2:5, :]
        src = lax.broadcasted_iota(jnp.int32, (DC, D), 0)
        dst = lax.broadcasted_iota(jnp.int32, (DC, D), 1)
        want = core * (DC // 2) + (src // HD) * (HD // 2) + (src & (HD // 2 - 1))
        side = lax.broadcasted_iota(jnp.int32, (1, DC), 1)
        turn = jnp.where((side & (HD - 1)) < HD // 2, att, -att)
        rows_s[9:10, :] = exact_dot(turn, dst == want)[0:1, :] + exact_dot(turn, dst == want + D // 2)[1:2, :]
        gb1 = jnp.concatenate([gb1_ref[:, r * DC : (r + 1) * DC] for r in range(FC // DC)] * 2, axis=0)
        rows_s[10:14, :] = exact_dot(gb1, spots_t(core))[:4, :]
        full_s[...] = rows_s[...].T.astype(bf16)
        to_chips(place_ref, full_s, (gw0, gw1, gw2, gw3), slice(4 * DC, PACK))


def to_chips(place_ref, full_ref, outs, cols):
    for d, out in enumerate(outs):
        a = (place_ref[1] + d) & (SIDE - 1)
        for g in range(SIDE):
            at = pl.multiple_of(natural(place_ref[0], a, g) * BLOCK, BLOCK)
            out[g * BLOCK : (g + 1) * BLOCK, cols] = full_ref[pl.ds(at, BLOCK), :]


def attn_bwd_call(
    place, q, k, v, ga, mine, other, p0, p1, cosine, sine, pos, h1t, pieces, proj_pieces, x, xo, mid, gb1
):
    q, k, v, cosine, sine, pos, ga = (a.reshape(CORES, S, -1) for a in (q, k, v, cosine, sine, pos, ga))
    block = lambda g: pl.BlockSpec((1, S, 2 * HD), lambda p, c: (g ^ c[0], 0, p))
    own = lambda g: pl.BlockSpec((1, S, 2 * HD), lambda p, c: (g, 0, p))
    at = lambda g: pl.BlockSpec((1, S, 8), lambda p, c: (g ^ c[0], 0, 0))
    whole = lambda a: pl.BlockSpec(a.shape, lambda p, c: (0,) * a.ndim)
    keep = lambda *n: pl.BlockSpec(n, lambda p, c: (0,) * len(n))
    return pl.pallas_call(
        attn_bwd_kernel,
        grid_spec=pltpu.PrefetchScalarGridSpec(
            num_scalar_prefetch=1,
            grid=(PAIRS,),
            in_specs=[block(0)] * 3
            + [own(0), pl.BlockSpec((2, 2, WIN, WIN), lambda p, c: (p, 0, 0, 0))]
            + [block(0)] * 2
            + [at(0)]
            + [block(1)] * 3
            + [own(1), pl.BlockSpec((2, S, S), lambda p, c: (p, 0, 0))]
            + [block(1)] * 2
            + [at(1)]
            + [whole(h1t), whole(ga)]
            + [pl.BlockSpec((CORES, S, 2 * HD), lambda p, c: (0, 0, PAIRS * c[0] + p))]
            + [whole(mine), whole(other)]
            + [pl.BlockSpec((QUARTER, D), lambda p, c: (0, FC // D))] * 4
            + [keep(QUARTER, 3 * DC)] * 4
            + [whole(a) for a in (x, xo, mid, gb1)],
            out_specs=[keep(QUARTER, PACK)] * 4 + [keep(S, D)] * 2,
            scratch_shapes=[pltpu.VMEM((S, 2 * HD), f32)] * 3
            + [pltpu.VMEM((D, 8 * HD), bf16), pltpu.VMEM((D, D), bf16), pltpu.VMEM((CORES, S, 2 * HD), bf16)]
            + [pltpu.VMEM((CORES, S, 3 * DC), bf16), pltpu.VMEM((PAIRS, 8, 2 * HD), f32)]
            + [pltpu.VMEM((128, D), f32), pltpu.VMEM((D, 128), bf16), pltpu.VMEM((D, 3 * DC), bf16)],
        ),
        out_shape=[
            *[jax.ShapeDtypeStruct((QUARTER, PACK), bf16)] * 4,
            *[jax.ShapeDtypeStruct((S, D), f32)] * 2,
        ],
        compiler_params=params(),
        cost_estimate=cost(10 * HC * S * S * 128 + 4 * T * D * 4 * DC, 36e6),
    )(
        place,
        q, k, v, mine, p0, cosine, sine, pos,
        q, k, v, mine, p1, cosine, sine, pos,
        h1t, ga, ga, mine, other, *proj_pieces, *pieces, x, xo, mid, gb1,
    )


def last_kernel(x_ref, ga_ref, gh_ref, other_ref, after_ref, mlp_ref, mlpo_ref, v_ref, gt_ref, out_ref):
    normed, inv_std = stats(x_ref[...].astype(f32))
    gt_ref[...] = ga_ref[...] + norm_back(gh_ref[...] + other_ref[...], normed, inv_std, v_ref[0:1, :])
    out_ref[...] = (after_ref[...] + (mlp_ref[...] + mlpo_ref[...] + v_ref[8:9, :])).astype(bf16)


def last_call(x, ga, gh, other, after, mlp, mlp_other, vec):
    rows = 288
    tile = lambda n: pl.BlockSpec((rows, n), lambda i: (i, 0))
    return pl.pallas_call(
        last_kernel,
        grid=(S // rows,),
        in_specs=[tile(D)] * 7 + [pl.BlockSpec(vec.shape, lambda i: (0, 0))],
        out_specs=[tile(D), tile(D)],
        out_shape=[jax.ShapeDtypeStruct((S, D), f32), jax.ShapeDtypeStruct((S, D), bf16)],
        compiler_params=params(),
        cost_estimate=cost(30 * S * D, S * D * 28),
    )(x, ga, gh, other, after, mlp, mlp_other, vec)


WIDE = PACK + FC


def pack_kernel(q0, q1, q2, q3, f_ref, out_ref):
    total = q0[...].astype(f32) + q1[...].astype(f32) + q2[...].astype(f32) + q3[...].astype(f32)
    fc1 = f_ref[...].astype(f32)
    for n in range(PLANE):
        at = slice(n * KR, (n + 1) * KR)
        out_ref[n, :, :PACK] = total[at, :].astype(bf16)
        out_ref[n, :, PACK:] = fc1[at, :].astype(bf16)


def pack_call(parts, fc1):
    return pl.pallas_call(
        pack_kernel,
        out_shape=jax.ShapeDtypeStruct((PLANE, KR, WIDE), bf16),
        compiler_params=params(),
        cost_estimate=cost(QUARTER * PACK * 4, QUARTER * PACK * 10),
    )(*parts, fc1)


def sum_kernel(in_ref, out_ref):
    total = in_ref[0].astype(f32)
    for n in range(1, PLANE):
        total += in_ref[n].astype(f32)
    out_ref[...] = total


def sum_call(packed):
    return pl.pallas_call(
        sum_kernel,
        out_shape=jax.ShapeDtypeStruct(packed.shape[1:], f32),
        compiler_params=params(),
        cost_estimate=cost(packed.size, packed.size * 2),
    )(packed)


def fc2_kernel(place_ref, mine_ref, other_ref, out_ref, sq_ref):
    first = place_ref[0] == 0
    a, b = mine_ref[...], other_ref[...]
    out_ref[:FR, :] = jnp.where(first, a, b)
    out_ref[FR:, :] = jnp.where(first, b, a)
    total = jnp.sum(a * a + b * b, axis=(0, 1), keepdims=True)
    sq_ref[...] = jnp.broadcast_to(total, sq_ref.shape)


def fc2_call(place, mine, other):
    whole = lambda a: pl.BlockSpec(a.shape, lambda i, c: (0,) * len(a.shape))
    shapes = [jax.ShapeDtypeStruct(s, f32) for s in ((2 * FR, D), (8, 128))]
    return pl.pallas_call(
        fc2_kernel,
        grid_spec=pltpu.PrefetchScalarGridSpec(
            num_scalar_prefetch=1,
            grid=(1,),
            in_specs=[whole(mine), whole(other)],
            out_specs=[whole(a) for a in shapes],
        ),
        out_shape=shapes,
        compiler_params=params(),
        cost_estimate=cost(6 * FR * D, FR * D * 16),
    )(place, mine, other)


def norm_kernel(g_ref, o_ref, sq_ref, out_ref):
    g, o = g_ref[...], o_ref[...]
    part = jnp.sum(g * g + o * o, axis=(0, 1), keepdims=True)
    cross = g[:, 4 * DC : PACK] * o[:, 4 * DC : PACK]
    part += 2.0 * jnp.sum(cross, axis=(0, 1), keepdims=True)
    out_ref[...] = jnp.broadcast_to((part + sq_ref[0:1, 0:1])[None], out_ref.shape)


def norm_call(g, o, squares):
    return pl.pallas_call(
        norm_kernel,
        out_shape=jax.ShapeDtypeStruct((CHIPS, 8, 128), f32),
        compiler_params=params(),
        cost_estimate=cost(4 * KR * PACK, 1e6),
    )(g, o, squares)


RATES = (D ** (-0.5), max(1, 2 * D // S) ** (-0.5), D ** (-0.5), FF ** (-0.5), RATE_VECTOR)


def adam_kernel(place_ref, norm_ref, mine_ref, other_ref, g2_ref, *refs):
    masters, firsts, seconds = refs[0:5], refs[5:10], refs[10:15]
    outs = refs[15:30]
    norm_out, bias_out = refs[30:32]
    core = place_ref[0]
    mine, other = mine_ref[...], other_ref[...]
    g0 = jnp.where(core == 0, mine, other)
    g1 = jnp.where(core == 0, other, mine)
    total = jnp.sum(jnp.sum(norm_ref[...], axis=0)[0:1, 0:1], axis=(0, 1), keepdims=True)
    grad_norm = jnp.sqrt(total)
    norm_out[...] = jnp.broadcast_to(grad_norm, norm_out.shape)
    clip = jnp.minimum(1.0, CLIP_LIMIT / (grad_norm + 1e-06))

    def update(i, at, grad):
        clipped = grad * clip
        master = masters[i][at]
        first = BETA_ONE * firsts[i][at] + (1.0 - BETA_ONE) * clipped
        second = BETA_TWO * seconds[i][at] + (1.0 - BETA_TWO) * clipped * clipped
        first_hat = first / (1.0 - BETA_ONE**STEP)
        second_hat = second / (1.0 - BETA_TWO**STEP)
        decay = 0.0 if i == 4 else DECAY_RATE
        outs[3 * i][at] = master - RATES[i] * (first_hat / (jnp.sqrt(second_hat) + ADAM_EPS) + decay * master)
        outs[3 * i + 1][at] = first
        outs[3 * i + 2][at] = second

    rows = slice(None)
    for c, g in ((0, g0), (1, g1)):
        for p in range(PAIRS):
            for i in range(3):
                col = i * D + c * DC + p * 128
                update(0, (rows, slice(col, col + 128)), g[:, (4 * p + i) * 128 : (4 * p + i + 1) * 128])
            col = c * DC + p * 128
            update(1, (rows, slice(col, col + 128)), g[:, (4 * p + 3) * 128 : (4 * p + 4) * 128])
    for r in range(FC // DC):
        at = slice(PACK + r * DC, PACK + (r + 1) * DC)
        part = exact_dot(g0[:, at], spots_t(0)) + exact_dot(g1[:, at], spots_t(1))
        update(2, (rows, slice(r * D, (r + 1) * D)), part)
    update(3, (rows, rows), g2_ref[...])
    vec = (g0 + g1)[:, 4 * DC : 4 * DC + 128]
    vec = jnp.concatenate([vec, jnp.zeros((16 - KR, 128), f32)], axis=0).T[:16, :KR]
    update(4, (rows, rows), vec[: masters[4].shape[0], :])
    bias_out[...] = vec[7:8, :] * clip


def adam_call(place, norm, mine, other, g2, masters, firsts, seconds):
    whole = lambda a: pl.BlockSpec(a.shape, lambda i, c: (0,) * len(a.shape))
    args = [norm, mine, other, g2, *masters, *firsts, *seconds]
    shapes = [jax.ShapeDtypeStruct(m.shape, f32) for m in masters for _ in range(3)]
    shapes += [jax.ShapeDtypeStruct((1, 128), f32), jax.ShapeDtypeStruct((1, KR), f32)]
    return pl.pallas_call(
        adam_kernel,
        grid_spec=pltpu.PrefetchScalarGridSpec(
            num_scalar_prefetch=1,
            grid=(1,),
            in_specs=[whole(a) for a in args],
            out_specs=[whole(a) for a in shapes],
        ),
        out_shape=shapes,
        compiler_params=params(),
        cost_estimate=cost(20 * KR * FF * 3, 3e6),
    )(place, *args)


def local(
    tokens,
    cotangent,
    counts,
    patch_row,
    patch_col,
    w_qkv,
    w_proj,
    w_fc1,
    w_fc2,
    vectors,
    m_qkv,
    v_qkv,
    m_proj,
    v_proj,
    m_fc1,
    v_fc1,
    m_fc2,
    v_fc2,
    m_vectors,
    v_vectors,
):
    core = lax.axis_index("grp")
    chip = lax.axis_index("dp")
    first_core = core == 0
    along = jnp.where(first_core, chip // PLANE, (chip // SIDE) % SIDE)
    vr = vectors.shape[0]

    def swap(a):
        return lax.ppermute(a, "grp", [(0, 1), (1, 0)])

    def along_line(quarter):
        return [quarter] + [shift(quarter, d) for d in range(1, SIDE)]

    def line_sum(whole):
        return lax.psum_scatter(whole, BOTH, scatter_dimension=0, axis_index_groups=lines(), tiled=True)

    fc2_b = w_fc2.astype(bf16)
    share_fc2 = jnp.where(first_core, fc2_b[:FR], fc2_b[FR:])
    me = jnp.stack([core, along]).astype(jnp.int32)
    shares = share_call(me, w_qkv, vectors)
    shares, share_fc2 = lax.optimization_barrier((shares, share_fc2))
    full_fc2 = lax.all_gather(share_fc2, "dp", axis=0, tiled=True)
    quarter = plane_swap(shares).reshape(QUARTER, 3 * DC + 128)
    qkv_pieces = along_line(quarter)
    fc1_b = w_fc1.astype(bf16).reshape(KR, CHIPS, CORES, FR)
    share_fc1 = jnp.where(first_core, fc1_b[:, :, 0], fc1_b[:, :, 1]).reshape(KR, FC)
    share = jnp.concatenate([share_fc1, w_proj.astype(bf16)], axis=1)
    share = jnp.broadcast_to(share[None], (PLANE,) + share.shape)
    share, qkv_pieces[1] = lax.optimization_barrier((share, qkv_pieces[1]))
    quarter = plane_swap(share).reshape(QUARTER, FC + D)

    x_own = tokens.reshape(S, D)
    cot_own = cotangent.reshape(S, D)
    x_other, cot_other = swap(x_own), swap(cot_own)
    ints = jnp.concatenate(
        [
            patch_row.reshape(1, S),
            patch_col.reshape(1, S),
            jnp.pad(counts.reshape(1, 2), ((0, 0), (0, S - 2))),
            jnp.zeros((5, S), jnp.int32),
        ]
    )
    ints = jnp.stack([ints, swap(ints)])
    counts0 = jnp.where(first_core, ints[0, 2, :2], ints[1, 2, :2])
    counts1 = jnp.where(first_core, ints[1, 2, :1], ints[0, 2, :1])
    place = jnp.concatenate([jnp.stack([core, along]).astype(jnp.int32), counts0, counts1])

    vec, h1t, cosine, sine, q, k, v, b1, pos = qkv_call(place, x_own, x_other, ints, qkv_pieces)
    q, quarter = lax.optimization_barrier((q, quarter))
    pieces = along_line(quarter)
    mine, p0, p1 = attn_fwd_call(place, q, k, v)
    mine, pieces[1], pieces[3], cot_other = lax.optimization_barrier((mine, pieces[1], pieces[3], cot_other))
    other = swap(mine)
    gy = gy_call(place, cot_own, cot_other)
    other, gy = lax.optimization_barrier((other, gy))
    after, n2, r2, h2 = proj_call(place, mine, other, x_own, x_other, pieces, vec)
    mlp, mlp_part, gh2, act, gup, gb1 = mlp_call(place, h2, gy, pieces, full_fc2, b1)
    other_gh2 = swap(gh2)
    mlp_other = swap(mlp_part)

    gw1, gw2 = fc_grad_call(place, h2, gup, act, gy)
    gw1, gw2, other_gh2 = lax.optimization_barrier((gw1, gw2, other_gh2))
    sum_fc2 = line_sum(gw2)
    sum_fc1 = line_sum(gw1)
    ga, gab, sums_mid = mid_call(place, n2, r2, gy, gh2, other_gh2, vec)
    *gw, gh1, gh1_part = attn_bwd_call(
        place, q, k, v, gab, mine, other, p0, p1, cosine, sine, pos, h1t, qkv_pieces, pieces,
        x_own, x_other, sums_mid, gb1,
    )
    gh1_other = swap(gh1_part)

    got_fc2 = plane_swap(sum_fc2.reshape(PLANE, FR, D))
    parts = [gw[0]] + [shift(gw[d], d) for d in range(1, SIDE)]
    got_fc2, sum_fc1 = lax.optimization_barrier((got_fc2, sum_fc1))
    g_fc2 = sum_call(got_fc2)
    g2, squares = fc2_call(place, g_fc2, swap(g_fc2))
    got = plane_swap(pack_call(parts, sum_fc1))
    got, g2, squares = lax.optimization_barrier((got, g2, squares))
    grads = sum_call(got)

    grads_other = swap(grads)
    squares = norm_call(grads, grads_other, squares)
    squares, gh1 = lax.optimization_barrier((squares, gh1))
    norms = lax.all_to_all(squares, "dp", 0, 0)
    gt, mixed = last_call(x_own, ga, gh1, gh1_other, after, mlp, mlp_other, vec)
    norms, gt, mixed = lax.optimization_barrier((norms, gt, mixed))
    *updates, grad_norm, bias_proj_grad = adam_call(
        place,
        norms,
        grads,
        grads_other,
        g2,
        (w_qkv, w_proj, w_fc1, w_fc2, vectors),
        (m_qkv, m_proj, m_fc1, m_fc2, m_vectors),
        (v_qkv, v_proj, v_fc1, v_fc2, v_vectors),
    )
    return (
        mixed.reshape(1, 1, S, D),
        gt.reshape(1, 1, S, D),
        grad_norm[0, 0],
        *updates,
        bias_proj_grad.reshape(KR),
    )


def solution(mesh):
    frame = P("grp", "dp", None, None)
    ints = P("grp", "dp", None)
    rows = P("dp", None)
    cols = P(None, "dp")
    return jax.shard_map(
        local,
        mesh=mesh,
        in_specs=(frame, frame, ints, ints, ints, rows, rows, rows, rows, cols) + (rows,) * 8 + (cols,) * 2,
        out_specs=(frame, frame, P()) + (rows,) * 12 + (cols,) * 3 + (P("dp"),),
        check_vma=False,
    )
```

profile of v0, /device:TPU:0, one launch (start us, length us, event | category | flops | bytes accessed | tf_op | source)
XLA Modules:
  0.0 284.5 jit_solution(5687194526557856516)
XLA Ops:
  7.3 1.0 convert_element_type.9
  9.5 2.5 shard_map.339
  12.0 8.1 %all-to-all-start = ((bf16[16,12,1280]{2,1,0:T(8,128)(2,1)}), bf16[16,12,1280]{2,1,0:T(8,128)(2,1)S(1)}, u32[]{:S(2)}, u32[]{:S(2)}) async-start(bf16[16,12,1280]{2,1,0:T(8,128)(2,1)} %shard_map.339), calls=%async_computation | async-start | bytes 1310720 | tf_op jit(solution)/shard_map/all_to_all | solution.py:74
  21.0 10.6 %all-to-all-done = bf16[16,12,1280]{2,1,0:T(8,128)(2,1)S(1)} async-done(((bf16[16,12,1280]{2,1,0:T(8,128)(2,1)}), bf16[16,12,1280]{2,1,0:T(8,128)(2,1)S(1)}, u32[]{:S(2)}, u32[]{:S(2)}) %all-to-all-start) | async-done | bytes 491552 | tf_op jit(solution)/shard_map/all_to_all | solution.py:74
  31.8 1.0 collective-permute-start.2
  32.7 1.4 fusion
  34.5 2.4 collective-permute-start.4
  36.9 1.2 collective-permute-start.3
  38.1 4.0 %collective-permute-done.2.w1.v1 = bf16[192,1280]{1,0:T(8,128)(2,1)} collective-permute-done((bf16[192,1280]{1,0:T(8,128)(2,1)S(1)}, bf16[192,1280]{1,0:T(8,128)(2,1)}, u32[]{:S(2)}, u32[]{:S(2)}) %collective-permute-start.2) | collective-permute-done | bytes 491552 | tf_op jit(solution)/shard_map/ppermute | solution.py:70
  42.1 1.1 broadcast_in_dim.10
  43.2 5.0 %all-to-all-start.1 = ((bf16[16,12,2304]{2,1,0:T(8,128)(2,1)}), bf16[16,12,2304]{2,1,0:T(8,128)(2,1)S(1)}, u32[]{:S(2)}, u32[]{:S(2)}) async-start(bf16[16,12,2304]{2,1,0:T(8,128)(2,1)} %broadcast_in_dim.10), calls=%async_computation.1 | async-start | bytes 2359296 | tf_op jit(solution)/shard_map/all_to_all | solution.py:74
  52.6 0.9 copy-done.3
  53.5 14.0 %shard_map.340 = (f32[16,768]{1,0:T(8,128)}, bf16[2,768,576]{2,1,0:T(8,128)(2,1)}, f32[1152,384]{1,0:T(8,128)}, f32[1152,384]{1,0:T(8,128)}, bf16[1152,384]{1,0:...) custom-call(s32[5]{0:T(128)} %pad_add_fusion.2.place_ref, ...), custom_call_target="tpu_custom_call" | custom-call | flops 2064973824 | bytes 13271040 | tf_op jit(solution)/shard_map/pallas_call | solution.py:312
  67.7 1.7 collective-permute-start.6
  69.8 11.3 %shard_map.341 = (bf16[2,576,384]{2,1,0:T(8,128)(2,1)}, bf16[6,2,208,208]{3,2,1,0:T(8,128)(2,1)}, bf16[6,576,576]{2,1,0:T(8,128)(2,1)}) custom-call(s32[5]{0:T(128)} %pad_add_fusion.2.place_ref, bf16[2,576,384]{2,1,0:T(8,128)(2,1)} %bitcast.28, bf16[2,576,384]{2,1,0:T(8,128)(2,1)} %bitcast.32, bf16[2,576,384]{2,1,0:T(8,128)(2,1)} %bitcast.36, ...), custom_call_target="tpu_custom_call" | custom-call | flops 1285029888 | bytes 12000000 | tf_op jit(solution)/shard_map/pallas_call | solution.py:385
  81.1 1.0 collective-permute-done.6.w3.w13.y3
  82.1 3.7 %collective-permute-done.5.w1.w11.y1 = bf16[192,2304]{1,0:T(8,128)(2,1)S(1)} collective-permute-done((bf16[192,2304]{1,0:T(8,128)(2,1)S(1)}, bf16[192,2304]{1,0:T(8,128)(2,1)S(1)}, u32[]{:S(2)}, u32[]{:S(2)}) %collective-permute-start.5) | collective-permute-done | bytes 884768 | tf_op jit(solution)/shard_map/ppermute | solution.py:70
  86.2 2.1 collective-permute-start.9
  88.3 3.6 %shard_map.342.gy_ref = bf16[1152,768]{1,0:T(8,128)(2,1)} custom-call(s32[5]{0:T(128)} %pad_add_fusion.2.place_ref, bf16[576,768]{1,0:T(8,128)(2,1)} %bitcast.54, bf16[576,768]{1,0:T(8,128)(2,1)} %collective-permute-done.7.co_ref), custom_call_target="tpu_custom_call" | custom-call | flops 3538944 | bytes 3538944 | tf_op jit(solution)/shard_map/pallas_call | solution.py:238
  91.9 10.2 %collective-permute-done.9.w2.w12.y2 = bf16[192,2304]{1,0:T(8,128)(2,1)S(1)} collective-permute-done((bf16[192,2304]{1,0:T(8,128)(2,1)S(1)}, bf16[192,2304]{1,0:T(8,128)(2,1)S(1)}, u32[]{:S(2)}, u32[]{:S(2)}) %collective-permute-start.9) | collective-permute-done | bytes 884768 | tf_op jit(solution)/shard_map/ppermute | solution.py:70
  102.1 1.0 copy-done.7
  103.1 8.7 %shard_map.343 = (f32[576,768]{1,0:T(8,128)}, f32[1152,768]{1,0:T(8,128)}, f32[1152,8]{1,0:T(8,128)}, bf16[1152,768]{1,0:T(8,128)(2,1)}) custom-call(s32[5]{0:T(128)} %pad_add_fusion.2.place_ref, bf16[2,576,384]{2,1,0:T(8,128)(2,1)} %get-tuple-element.107.mine_ref.o0.o1, bf16[2,576,384]{2,1,0:T(8,128)(2,1)} %copy-done.6, bf16[576,768]{1,0:T(8,128)(2,1)} %bitcast.41, ...), custom_call_target="tpu_custom_call" | custom-call | flops 1358954496 | bytes 10027008 | tf_op jit(solution)/shard_map/pallas_call | solution.py:433
  111.8 18.7 %shard_map.344 = (f32[576,768]{1,0:T(8,128)}, f32[576,768]{1,0:T(8,128)}, bf16[1152,768]{1,0:T(8,128)(2,1)}, bf16[1152,1536]{1,0:T(8,128)(2,1)}, bf16[1152,1536]{1,0:T(8,128)(2,1)}, /*index=5*/f32[1,1536]{1,0:T(1,128)}) custom-call(s32[5]{0:T(128)} %pad_add_fusion.2.place_ref, bf16[1152,768]{1,0:T(8,128)(2,1)} %get-tuple-element.122.h2_ref, ...), custom_call_target="tpu_custom_call" | custom-call | flops 10871635968 | bytes 30000000 | tf_op jit(solution)/shard_map/pallas_call | solution.py:507
  130.5 2.8 collective-permute-start.10
  133.3 12.8 %shard_map.345 = (bf16[768,1536]{1,0:T(8,128)(2,1)}, bf16[1536,768]{1,0:T(8,128)(2,1)}) custom-call(s32[5]{0:T(128)} %pad_add_fusion.2.place_ref, bf16[1152,768]{1,0:T(8,128)(2,1)} %get-tuple-element.122.h2_ref, bf16[1152,1536]{1,0:T(8,128)(2,1)} %get-tuple-element.126.gup_ref, bf16[1152,1536]{1,0:T(8,128)(2,1)} %get-tuple-element.127.act_ref, ...), custom_call_target="tpu_custom_call" | custom-call | flops 5435817984 | bytes 15335424 | tf_op jit(solution)/shard_map/pallas_call | solution.py:552
  147.4 8.0 %shard_map.346 = (f32[576,768]{1,0:T(8,128)}, bf16[1152,768]{1,0:T(8,128)(2,1)}, f32[8,768]{1,0:T(8,128)}) custom-call(s32[5]{0:T(128)} %pad_add_fusion.2.place_ref, f32[1152,768]{1,0:T(8,128)} %get-tuple-element.119.n2_ref, f32[1152,8]{1,0:T(8,128)} %get-tuple-element.120.r2_ref, bf16[1152,768]{1,0:T(8,128)(2,1)} %shard_map.342.gy_ref, ...), custom_call_target="tpu_custom_call" | custom-call | flops 26542080 | bytes 12386304 | tf_op jit(solution)/shard_map/pallas_call | solution.py:602
  155.4 28.2 %shard_map.347 = (bf16[192,1664]{1,0:T(8,128)(2,1)}, bf16[192,1664]{1,0:T(8,128)(2,1)}, bf16[192,1664]{1,0:T(8,128)(2,1)}, bf16[192,1664]{1,0:T(8,128)(2,1)}, f32[576,768]{1,0:T(8,128)}, /*index=5*/f32[576,768]{1,0:T(8,128)}) custom-call(s32[5]{0:T(128)} %pad_add_fusion.2.place_ref, bf16[2,576,384]{2,1,0:T(8,128)(2,1)} %bitcast.30, ...), custom_call_target="tpu_custom_call" | custom-call | flops 7983857664 | bytes 36000000 | tf_op jit(solution)/shard_map/pallas_call | solution.py:766
  183.7 1.6 collective-permute-start.12
  185.3 1.7 collective-permute-start.13
  187.0 8.9 %all-to-all-start.2 = ((bf16[16,24,768]{2,1,0:T(8,128)(2,1)}), bf16[16,24,768]{2,1,0:T(8,128)(2,1)S(1)}, u32[]{:S(2)}, u32[]{:S(2)}) async-start(bf16[16,24,768]{2,1,0:T(8,128)(2,1)} %bitcast.55), calls=%async_computation.3 | async-start | bytes 1179648 | tf_op jit(solution)/shard_map/all_to_all | solution.py:74
  196.5 18.6 %reduce-scatter.5.cloned.1.call-done.f_ref = bf16[192,1536]{1,0:T(8,128)(2,1)} async-done(((bf16[768,1536]{1,0:T(8,128)(2,1)}), bf16[192,1536]{1,0:T(8,128)(2,1)}) %reduce-scatter.5.cloned.1.call-update) | async-done | bytes 589840 | tf_op jit(solution)/shard_map/reduce_scatter | solution.py:1006
  215.1 0.9 copy-done.15
  216.0 3.4 %shard_map.348 = bf16[16,12,3200]{2,1,0:T(8,128)(2,1)} custom-call(bf16[192,1664]{1,0:T(8,128)(2,1)} %get-tuple-element.134.q0, bf16[192,1664]{1,0:T(8,128)(2,1)} %copy-done.15, bf16[192,1664]{1,0:T(8,128)(2,1)} %collective-permute-done.12.q2, bf16[192,1664]{1,0:T(8,128)(2,1)} %collective-permute-done.13.q3, ...), custom_call_target="tpu_custom_call" | custom-call | flops 1277952 | bytes 3194880 | tf_op jit(solution)/shard_map/pallas_call | solution.py:838
  219.4 6.5 %all-to-all-start.3 = ((bf16[16,12,3200]{2,1,0:T(8,128)(2,1)}), bf16[16,12,3200]{2,1,0:T(8,128)(2,1)S(1)}, u32[]{:S(2)}, u32[]{:S(2)}) async-start(bf16[16,12,3200]{2,1,0:T(8,128)(2,1)} %shard_map.348), calls=%async_computation.5 | async-start | bytes 3276800 | tf_op jit(solution)/shard_map/all_to_all | solution.py:74
  225.9 1.8 shard_map.349.mine_ref
  227.9 1.5 collective-permute-done.14.other_ref
  230.0 2.3 shard_map.350
  232.3 14.0 %all-to-all-done.3.in_ref = bf16[16,12,3200]{2,1,0:T(8,128)(2,1)S(1)} async-done(((bf16[16,12,3200]{2,1,0:T(8,128)(2,1)}), bf16[16,12,3200]{2,1,0:T(8,128)(2,1)S(1)}, u32[]{:S(2)}, u32[]{:S(2)}) %all-to-all-start.3) | async-done | bytes 1228832 | tf_op jit(solution)/shard_map/all_to_all | solution.py:74
  246.3 1.2 copy-done.2
  247.5 2.3 shard_map.351.g_ref.mine_ref
  249.8 1.7 collective-permute-done.15.o_ref.other_ref
  252.1 2.0 shard_map.352
  254.1 6.7 %all-to-all-start.4 = ((f32[64,8,128]{2,1,0:T(8,128)}), f32[64,8,128]{2,1,0:T(8,128)S(1)}, u32[]{:S(2)}, u32[]{:S(2)}) async-start(f32[64,8,128]{2,1,0:T(8,128)} %shard_map.352), calls=%async_computation.6 | async-start | bytes 524288 | tf_op jit(solution)/shard_map/all_to_all | solution.py:1075
  260.8 1.2 copy-done.11
  262.0 6.0 %shard_map.353 = (f32[576,768]{1,0:T(8,128)}, bf16[576,768]{1,0:T(8,128)(2,1)}) custom-call(bf16[576,768]{1,0:T(8,128)(2,1)} %bitcast.43, f32[576,768]{1,0:T(8,128)} %get-tuple-element.148.ga_ref, f32[576,768]{1,0:T(8,128)} %get-tuple-element.149.gh_ref, f32[576,768]{1,0:T(8,128)} %collective-permute-done.16.other_ref, ...), custom_call_target="tpu_custom_call" | custom-call | flops 13271040 | bytes 12386304 | tf_op jit(solution)/shard_map/pallas_call | solution.py:814
  268.1 3.4 %all-to-all-done.4.norm_ref = f32[64,8,128]{2,1,0:T(8,128)S(1)} async-done(((f32[64,8,128]{2,1,0:T(8,128)}), f32[64,8,128]{2,1,0:T(8,128)S(1)}, u32[]{:S(2)}, u32[]{:S(2)}) %all-to-all-start.4) | async-done | bytes 262176 | tf_op jit(solution)/shard_map/all_to_all | solution.py:1075
  271.5 0.7 copy-done.12
  272.2 5.6 %shard_map.354 = (f32[12,2304]{1,0:T(8,128)}, f32[12,2304]{1,0:T(8,128)}, f32[12,2304]{1,0:T(8,128)}, f32[12,768]{1,0:T(8,128)}, f32[12,768]{1,0:T(8,128)}, /*in...) custom-call(s32[5]{0:T(128)} %pad_add_fusion.2.place_ref, ...), custom_call_target="tpu_custom_call" | custom-call | flops 2211840 | bytes 3000000 | tf_op jit(solution)/shard_map/pallas_call | solution.py:957
  (85 shorter events, 10.1 us)
Async XLA Ops:
  7.2 13.0 %copy-start = (bf16[1,1,576,768]{3,2,1,0:T(8,128)(2,1)S(1)}, bf16[1,1,576,768]{3,2,1,0:T(8,128)(2,1)}, u32[]{:S(2)}) copy-start(bf16[1,1,576,768]{3,2,1,0:T(8,128)(2,1)} %param.20) | copy-start | bytes 2654212
  7.2 13.2 %copy-start.16 = (f32[12,768]{1,0:T(8,128)S(1)}, f32[12,768]{1,0:T(8,128)}, u32[]{:S(2)}) copy-start(f32[12,768]{1,0:T(8,128)} %refs_1_.1) | copy-start | bytes 110596
  7.2 13.2 %copy-start.14 = (f32[12,3072]{1,0:T(8,128)S(1)}, f32[12,3072]{1,0:T(8,128)}, u32[]{:S(2)}) copy-start(f32[12,3072]{1,0:T(8,128)} %refs_2_.1) | copy-start | bytes 442372
  7.2 104.6 %all-gather.2.cloned.1.call-start = ((), (), s32[]{:S(2)}) async-start(), calls=%async_computation.7 | async-start | bytes 2396160 | tf_op jit(solution)/shard_map/all_gather | solution.py:1013
  12.0 19.6 %all-to-all-start = ((bf16[16,12,1280]{2,1,0:T(8,128)(2,1)}), bf16[16,12,1280]{2,1,0:T(8,128)(2,1)S(1)}, u32[]{:S(2)}, u32[]{:S(2)}) async-start(bf16[16,12,1280]{2,1,0:T(8,128)(2,1)} %shard_map.339), calls=%async_computation | async-start | bytes 1310720 | tf_op jit(solution)/shard_map/all_to_all | solution.py:74
  20.2 32.4 %collective-permute-start.1 = (bf16[576,768]{1,0:T(8,128)(2,1)S(1)}, bf16[576,768]{1,0:T(8,128)(2,1)S(1)}, u32[]{:S(2)}, u32[]{:S(2)}) collective-permute-start(bf16[576,768]{1,0:T(8,128)(2,1)S(1)} %bitcast.44), channel_id=1, source_target_pairs={{0,64},{64,0},{1,65},{65,1},{2,66},{66,2},{3,67},{67,3},{4,68},{68... | collective-permute-start | bytes 2654216 | tf_op jit(solution)/shard_map/ppermute | solution.py:1000
  31.8 11.4 %copy-start.9 = (bf16[192,1280]{1,0:T(8,128)(2,1)}, bf16[192,1280]{1,0:T(8,128)(2,1)S(1)}, u32[]{:S(2)}) copy-start(bf16[192,1280]{1,0:T(8,128)(2,1)S(1)} %reshape.111.w0.v0) | copy-start | bytes 1474564
  31.8 10.3 %collective-permute-start.2 = (bf16[192,1280]{1,0:T(8,128)(2,1)S(1)}, bf16[192,1280]{1,0:T(8,128)(2,1)}, u32[]{:S(2)}, u32[]{:S(2)}) collective-permute-start(bf16[192,1280]{1,0:T(8,128)(2,1)S(1)} %reshape.111.w0.v0), channel_id=1, source_target_pairs={{0,16},{16,32},{32,48},{48,0},{1,17},{17,33},{33,49},{49,1},{2,18}... | collective-permute-start | bytes 1474568 | tf_op jit(solution)/shard_map/ppermute | solution.py:70
  34.4 13.8 %copy-start.18 = (s32[1,1,576]{2,1,0:T(1,128)S(1)}, s32[1,1,576]{2,1,0:T(1,128)}, u32[]{:S(2)}) copy-start(s32[1,1,576]{2,1,0:T(1,128)} %param.24) | copy-start | bytes 6916
  34.5 13.8 %copy-start.19 = (s32[1,1,576]{2,1,0:T(1,128)S(1)}, s32[1,1,576]{2,1,0:T(1,128)}, u32[]{:S(2)}) copy-start(s32[1,1,576]{2,1,0:T(1,128)} %param.23) | copy-start | bytes 6916
  34.5 13.8 %copy-start.20 = (s32[1,1,2]{2,1,0:T(1,128)S(1)}, s32[1,1,2]{2,1,0:T(1,128)}, u32[]{:S(2)}) copy-start(s32[1,1,2]{2,1,0:T(1,128)} %param.22) | copy-start | bytes 28
  34.5 18.1 %collective-permute-start.4 = (bf16[192,1280]{1,0:T(8,128)(2,1)S(1)}, bf16[192,1280]{1,0:T(8,128)(2,1)}, u32[]{:S(2)}, u32[]{:S(2)}) collective-permute-start(bf16[192,1280]{1,0:T(8,128)(2,1)S(1)} %reshape.111.w0.v0), channel_id=1, source_target_pairs={{0,48},{16,0},{32,16},{48,32},{1,49},{17,1},{33,17},{49,33},{2,50}... | collective-permute-start | bytes 1474568 | tf_op jit(solution)/shard_map/ppermute | solution.py:70
  36.9 15.7 %collective-permute-start.3 = (bf16[192,1280]{1,0:T(8,128)(2,1)S(1)}, bf16[192,1280]{1,0:T(8,128)(2,1)}, u32[]{:S(2)}, u32[]{:S(2)}) collective-permute-start(bf16[192,1280]{1,0:T(8,128)(2,1)S(1)} %reshape.111.w0.v0), channel_id=1, source_target_pairs={{0,32},{16,48},{32,0},{48,16},{1,33},{17,49},{33,1},{49,17},{2,34}... | collective-permute-start | bytes 1474568 | tf_op jit(solution)/shard_map/ppermute | solution.py:70
  43.2 24.3 %all-to-all-start.1 = ((bf16[16,12,2304]{2,1,0:T(8,128)(2,1)}), bf16[16,12,2304]{2,1,0:T(8,128)(2,1)S(1)}, u32[]{:S(2)}, u32[]{:S(2)}) async-start(bf16[16,12,2304]{2,1,0:T(8,128)(2,1)} %broadcast_in_dim.10), calls=%async_computation.1 | async-start | bytes 2359296 | tf_op jit(solution)/shard_map/all_to_all | solution.py:74
  48.2 138.8 %reduce-scatter.3.cloned.1.call-start = ((), (), s32[]{:S(2)}) async-start(), calls=%async_computation.8 | async-start | bytes 2949120 | tf_op jit(solution)/shard_map/reduce_scatter | solution.py:1006
  48.3 1.2 collective-permute-start
  48.4 32.7 %collective-permute-start.7 = (bf16[576,768]{1,0:T(8,128)(2,1)}, bf16[576,768]{1,0:T(8,128)(2,1)}, u32[]{:S(2)}, u32[]{:S(2)}) collective-permute-start(bf16[576,768]{1,0:T(8,128)(2,1)} %bitcast.53), channel_id=1, source_target_pairs={{0,64},{64,0},{1,65},{65,1},{2,66},{66,2},{3,67},{67,3},{4,68},{68... | collective-permute-start | bytes 2654216 | tf_op jit(solution)/shard_map/ppermute | solution.py:1000
  52.6 0.9 copy-start.3
  67.7 18.5 %copy-start.1 = (bf16[192,2304]{1,0:T(8,128)(2,1)}, bf16[192,2304]{1,0:T(8,128)(2,1)S(1)}, u32[]{:S(2)}) copy-start(bf16[192,2304]{1,0:T(8,128)(2,1)S(1)} %reshape.113.w0.w10.y0) | copy-start | bytes 2654212
  67.7 14.3 %collective-permute-start.6 = (bf16[192,2304]{1,0:T(8,128)(2,1)S(1)}, bf16[192,2304]{1,0:T(8,128)(2,1)S(1)}, u32[]{:S(2)}, u32[]{:S(2)}) collective-permute-start(bf16[192,2304]{1,0:T(8,128)(2,1)S(1)} %reshape.113.w0.w10.y0), channel_id=1, source_target_pairs={{0,48},{16,0},{32,16},{48,32},{1,49},{17,1},{33,17},{49,33},{2,50}... | collective-permute-start | bytes 2654216 | tf_op jit(solution)/shard_map/ppermute | solution.py:70
  69.4 16.4 %collective-permute-start.5 = (bf16[192,2304]{1,0:T(8,128)(2,1)S(1)}, bf16[192,2304]{1,0:T(8,128)(2,1)S(1)}, u32[]{:S(2)}, u32[]{:S(2)}) collective-permute-start(bf16[192,2304]{1,0:T(8,128)(2,1)S(1)} %reshape.113.w0.w10.y0), channel_id=1, source_target_pairs={{0,16},{16,32},{32,48},{48,0},{1,17},{17,33},{33,49},{49,1},{2,18}... | collective-permute-start | bytes 2654216 | tf_op jit(solution)/shard_map/ppermute | solution.py:70
  82.1 9.8 %copy-start.4 = (bf16[192,2304]{1,0:T(8,128)(2,1)}, bf16[192,2304]{1,0:T(8,128)(2,1)S(1)}, u32[]{:S(2)}) copy-start(bf16[192,2304]{1,0:T(8,128)(2,1)S(1)} %collective-permute-done.6.w3.w13.y3) | copy-start | bytes 2654212
  85.8 6.2 %copy-start.5 = (bf16[192,2304]{1,0:T(8,128)(2,1)}, bf16[192,2304]{1,0:T(8,128)(2,1)S(1)}, u32[]{:S(2)}) copy-start(bf16[192,2304]{1,0:T(8,128)(2,1)S(1)} %collective-permute-done.5.w1.w11.y1) | copy-start | bytes 2654212
  85.8 6.2 %collective-permute-start.8 = (bf16[2,576,384]{2,1,0:T(8,128)(2,1)}, bf16[2,576,384]{2,1,0:T(8,128)(2,1)S(1)}, u32[]{:S(2)}, u32[]{:S(2)}) collective-permute-start(bf16[2,576,384]{2,1,0:T(8,128)(2,1)} %get-tuple-element.107.mine_ref.o0.o1), channel_id=1, source_target_pairs={{0,64},{64,0},{1,65},{65,1},{2,66},{66,2},{3,67},{67,3},{4,68},{68... | collective-permute-start | bytes 2654216 | tf_op jit(solution)/shard_map/ppermute | solution.py:1000
  86.2 15.9 %collective-permute-start.9 = (bf16[192,2304]{1,0:T(8,128)(2,1)S(1)}, bf16[192,2304]{1,0:T(8,128)(2,1)S(1)}, u32[]{:S(2)}, u32[]{:S(2)}) collective-permute-start(bf16[192,2304]{1,0:T(8,128)(2,1)S(1)} %reshape.113.w0.w10.y0), channel_id=1, source_target_pairs={{0,32},{16,48},{32,0},{48,16},{1,33},{17,49},{33,1},{49,17},{2,34}... | collective-permute-start | bytes 2654216 | tf_op jit(solution)/shard_map/ppermute | solution.py:70
  91.9 10.2 %copy-start.6 = (bf16[2,576,384]{2,1,0:T(8,128)(2,1)}, bf16[2,576,384]{2,1,0:T(8,128)(2,1)S(1)}, u32[]{:S(2)}) copy-start(bf16[2,576,384]{2,1,0:T(8,128)(2,1)S(1)} %collective-permute-done.8.other_ref) | copy-start | bytes 2654212
  102.1 1.0 copy-start.7
  130.5 15.6 %collective-permute-start.10 = (bf16[1152,768]{1,0:T(8,128)(2,1)}, bf16[1152,768]{1,0:T(8,128)(2,1)S(1)}, u32[]{:S(2)}, u32[]{:S(2)}) collective-permute-start(bf16[1152,768]{1,0:T(8,128)(2,1)} %get-tuple-element.125.gh2_ref), channel_id=1, source_target_pairs={{0,64},{64,0},{1,65},{65,1},{2,66},{66,2},{3,67},{67,3},{4,68},{68... | collective-permute-start | bytes 5308424 | tf_op jit(solution)/shard_map/ppermute | solution.py:1000
  146.1 1.3 copy-start.10
  146.2 68.9 %reduce-scatter.5.cloned.1.call-start = ((), (), s32[]{:S(2)}) async-start(), calls=%async_computation.9 | async-start | bytes 2949120 | tf_op jit(solution)/shard_map/reduce_scatter | solution.py:1006
  183.7 31.5 %collective-permute-start.11 = (bf16[192,1664]{1,0:T(8,128)(2,1)}, bf16[192,1664]{1,0:T(8,128)(2,1)S(1)}, u32[]{:S(2)}, u32[]{:S(2)}) collective-permute-start(bf16[192,1664]{1,0:T(8,128)(2,1)} %get-tuple-element.135), channel_id=1, source_target_pairs={{0,16},{16,32},{32,48},{48,0},{1,17},{17,33},{33,49},{49,1},{2,18}... | collective-permute-start | bytes 1916936 | tf_op jit(solution)/shard_map/ppermute | solution.py:70
  183.7 31.4 %collective-permute-start.12 = (bf16[192,1664]{1,0:T(8,128)(2,1)}, bf16[192,1664]{1,0:T(8,128)(2,1)}, u32[]{:S(2)}, u32[]{:S(2)}) collective-permute-start(bf16[192,1664]{1,0:T(8,128)(2,1)} %get-tuple-element.136), channel_id=1, source_target_pairs={{0,32},{16,48},{32,0},{48,16},{1,33},{17,49},{33,1},{49,17},{2,34}... | collective-permute-start | bytes 1916936 | tf_op jit(solution)/shard_map/ppermute | solution.py:70
  185.3 29.8 %collective-permute-start.13 = (bf16[192,1664]{1,0:T(8,128)(2,1)}, bf16[192,1664]{1,0:T(8,128)(2,1)}, u32[]{:S(2)}, u32[]{:S(2)}) collective-permute-start(bf16[192,1664]{1,0:T(8,128)(2,1)} %get-tuple-element.137), channel_id=1, source_target_pairs={{0,48},{16,0},{32,16},{48,32},{1,49},{17,1},{33,17},{49,33},{2,50}... | collective-permute-start | bytes 1916936 | tf_op jit(solution)/shard_map/ppermute | solution.py:70
  187.0 28.1 %all-to-all-start.2 = ((bf16[16,24,768]{2,1,0:T(8,128)(2,1)}), bf16[16,24,768]{2,1,0:T(8,128)(2,1)S(1)}, u32[]{:S(2)}, u32[]{:S(2)}) async-start(bf16[16,24,768]{2,1,0:T(8,128)(2,1)} %bitcast.55), calls=%async_computation.3 | async-start | bytes 1179648 | tf_op jit(solution)/shard_map/all_to_all | solution.py:74
  195.9 64.8 %collective-permute-start.17 = (f32[576,768]{1,0:T(8,128)}, f32[576,768]{1,0:T(8,128)S(1)}, u32[]{:S(2)}, u32[]{:S(2)}) collective-permute-start(f32[576,768]{1,0:T(8,128)} %get-tuple-element.153), channel_id=1, source_target_pairs={{0,64},{64,0},{1,65},{65,1},{2,66},{66,2},{3,67},{67,3},{4,68},{68... | collective-permute-start | bytes 5308424 | tf_op jit(solution)/shard_map/ppermute | solution.py:1000
  196.0 64.8 %collective-permute-start.16 = (f32[576,768]{1,0:T(8,128)}, f32[576,768]{1,0:T(8,128)}, u32[]{:S(2)}, u32[]{:S(2)}) collective-permute-start(f32[576,768]{1,0:T(8,128)} %get-tuple-element.150), channel_id=1, source_target_pairs={{0,64},{64,0},{1,65},{65,1},{2,66},{66,2},{3,67},{67,3},{4,68},{68... | collective-permute-start | bytes 5308424 | tf_op jit(solution)/shard_map/ppermute | solution.py:1000
  215.1 4.3 %copy-start.8 = (bf16[16,24,768]{2,1,0:T(8,128)(2,1)}, bf16[16,24,768]{2,1,0:T(8,128)(2,1)S(1)}, u32[]{:S(2)}) copy-start(bf16[16,24,768]{2,1,0:T(8,128)(2,1)S(1)} %all-to-all-done.2.in_ref) | copy-start | bytes 1769476
  215.1 0.9 copy-start.15
  219.4 26.9 %all-to-all-start.3 = ((bf16[16,12,3200]{2,1,0:T(8,128)(2,1)}), bf16[16,12,3200]{2,1,0:T(8,128)(2,1)S(1)}, u32[]{:S(2)}, u32[]{:S(2)}) async-start(bf16[16,12,3200]{2,1,0:T(8,128)(2,1)} %shard_map.348), calls=%async_computation.5 | async-start | bytes 3276800 | tf_op jit(solution)/shard_map/all_to_all | solution.py:74
  227.7 1.6 collective-permute-start.14
  229.4 0.6 copy-start.17
  246.3 1.2 copy-start.2
  249.8 1.7 collective-permute-start.15
  251.5 0.7 copy-start.13
  254.1 17.4 %all-to-all-start.4 = ((f32[64,8,128]{2,1,0:T(8,128)}), f32[64,8,128]{2,1,0:T(8,128)S(1)}, u32[]{:S(2)}, u32[]{:S(2)}) async-start(f32[64,8,128]{2,1,0:T(8,128)} %shard_map.352), calls=%async_computation.6 | async-start | bytes 524288 | tf_op jit(solution)/shard_map/all_to_all | solution.py:1075
  260.8 1.3 copy-start.11
  271.5 0.7 copy-start.12
Sparse Core Ops, SparseCore 0:
  12.2 83.2 all-gather.1
  146.3 25.9 reduce-scatter.2
  174.7 40.4 reduce-scatter.4
where the time goes:
time: 290 us; the launch traced here: 285 us
  Pallas kernels  131 us (45%)
  waiting for transfers between devices  68.9 us (24%)
  starting transfers between devices  52.6 us (18%)
  between operations  15.7 us (5%)
  local copies, waits for them, and re-layouts  11.1 us (4%)
  other arithmetic  4.96 us (2%)
    all_to_all x4, starting transfers between devices, plane_swap(): return lax.all_to_all(value, BOTH, 0, 0, axis_index_groups=planes())  28.6 us
    pallas_call x1, Pallas kernels, attn_bwd_call(): pl.pallas_call(attn_bwd_kernel, grid_spec=pltpu.PrefetchScalarGridSpec(nu...  28.2 us
    all_to_all x4, waiting for transfers between devices, plane_swap(): return lax.all_to_all(value, BOTH, 0, 0, axis_index_groups=planes())  24.6 us
    ppermute x9, waiting for transfers between devices, shift(): return lax.ppermute(value, BOTH, pairs)  18.9 us
    pallas_call x1, Pallas kernels, mlp_call(): pl.pallas_call(mlp_kernel, grid_spec=pltpu.PrefetchScalarGridSpec(num_sca...  18.7 us
    reduce_scatter x2, waiting for transfers between devices, line_sum(): lax.psum_scatter(whole, BOTH, scatter_dimension=0, axis_index_groups=line...  18.6 us
    pallas_call x1, Pallas kernels, qkv_call(): pl.pallas_call(qkv_kernel, grid_spec=pltpu.PrefetchScalarGridSpec(num_sca...  14 us
    pallas_call x1, Pallas kernels, fc_grad_call(): pl.pallas_call(fc_grad_kernel, grid_spec=pltpu.PrefetchScalarGridSpec(num...  12.8 us
  transfers between devices with their start and end apart: 26, of which 10 were waited for; matrix products, arithmetic and copies ran while one was open for 2% of the time, Pallas kernels for 37%

commit v1 on v0

--- a/solution.py
+++ b/solution.py
@@ -542,60 +542,64 @@
         out_ref[pl.ds(pl.multiple_of(to * block, block), block), :] = value[n * block : (n + 1) * block, :].astype(bf16)
 
 
-def fc_grad_kernel(place_ref, h2_ref, gup_ref, act_ref, gy_ref, gw1_ref, gw2_ref):
-    by_line(place_ref, t_dot(act_ref[...], gy_ref[...]), SIDE * FR, gw2_ref)
-    by_line(place_ref, t_dot(h2_ref[...], gup_ref[...]), BLOCK, gw1_ref)
-
-
-def fc_grad_call(place, h2, gup, act, gy):
-    whole = lambda a: pl.BlockSpec(a.shape, lambda i, c: (0, 0))
-    return pl.pallas_call(
-        fc_grad_kernel,
+def fc2_grad_kernel(place_ref, act_ref, gy_ref, out_ref):
+    value = t_dot(act_ref[...], gy_ref[...])
+    block = SIDE * FR
+    for n in range(FT // block):
+        m = pl.program_id(0) * (FT // block) + n
+        to = jnp.where(place_ref[0] == 0, m, (m & (SIDE - 1)) * SIDE + m // SIDE)
+        out_ref[pl.ds(pl.multiple_of(to * block, block), block), :] = value[n * block : (n + 1) * block, :].astype(bf16)
+
+
+def fc2_grad_call(place, act, gy):
+    return pl.pallas_call(
+        fc2_grad_kernel,
         grid_spec=pltpu.PrefetchScalarGridSpec(
             num_scalar_prefetch=1,
-            grid=(2,),
-            in_specs=[
-                whole(h2),
-                pl.BlockSpec((T, FC // 2), lambda i, c: (0, i)),
-                whole(act),
-                pl.BlockSpec((T, DC), lambda i, c: (0, i)),
-            ],
-            out_specs=[
-                pl.BlockSpec((D, FC // 2), lambda i, c: (0, i)),
-                pl.BlockSpec((FC, DC), lambda i, c: (0, i)),
-            ],
+            grid=(FC // FT,),
+            in_specs=[pl.BlockSpec((T, FT), lambda i, c: (0, i)), pl.BlockSpec((T, D), lambda i, c: (0, 0))],
+            out_specs=pl.BlockSpec((FC, D), lambda i, c: (0, 0)),
         ),
-        out_shape=[jax.ShapeDtypeStruct((D, FC), bf16), jax.ShapeDtypeStruct((FC, D), bf16)],
-        compiler_params=params(),
-        cost_estimate=cost(4 * T * D * FC, T * (D + FC) * 4 + D * FC * 4),
-    )(place, h2, gup, act, gy)
-
-
-def mid_kernel(place_ref, n2_ref, r2_ref, gy_ref, gh2_ref, other_ref, v_ref, ga_ref, gab_ref, sums_ref):
+        out_shape=jax.ShapeDtypeStruct((FC, D), bf16),
+        compiler_params=params(),
+        cost_estimate=cost(2 * T * D * FC, T * (D + FC) * 2 + D * FC * 2),
+    )(place, act, gy)
+
+
+def mid_kernel(
+    place_ref, h2_ref, gup_ref, n2_ref, r2_ref, gy_ref, gh2_ref, other_ref, v_ref, gw_ref, ga_ref, gab_ref, sums_ref
+):
     i = pl.program_id(0)
+    by_line(place_ref, t_dot(h2_ref[...], gup_ref[...]), BLOCK, gw_ref)
     normed, inv_std = n2_ref[...], r2_ref[:, 0:1]
     gh2 = gh2_ref[...].astype(f32) + other_ref[...].astype(f32)
     gy = gy_ref[...].astype(f32)
     ga = gy + norm_back(gh2, normed, inv_std, v_ref[2:3, :])
     gab = ga.astype(bf16)
     gab_ref[...] = gab
+    mine = (i < pl.num_programs(0) // CORES).astype(f32)
+    sums = [
+        mine * jnp.sum(a, axis=0, keepdims=True) for a in (gh2 * normed, gh2, gab.astype(f32), gy)
+    ] + [jnp.zeros((4, D), f32)]
+    sums = jnp.concatenate(sums, axis=0)
 
     @pl.when(i == 0)
     def _():
-        sums_ref[...] = jnp.zeros_like(sums_ref)
+        sums_ref[...] = sums
+
+    @pl.when(i > 0)
+    def _():
+        sums_ref[...] += sums
 
     @pl.when(i < pl.num_programs(0) // CORES)
     def _():
         ga_ref[...] = ga
-        sums_ref[0:1, :] += jnp.sum(gh2 * normed, axis=0, keepdims=True)
-        sums_ref[1:2, :] += jnp.sum(gh2, axis=0, keepdims=True)
-        sums_ref[2:3, :] += jnp.sum(gab.astype(f32), axis=0, keepdims=True)
-        sums_ref[3:4, :] += jnp.sum(gy, axis=0, keepdims=True)
-
-
-def mid_call(place, n2, r2, gy, gh2, other, vec):
+
+
+def mid_call(place, h2, gup, n2, r2, gy, gh2, other, vec):
     rows = 288
     half = S // rows
+    cols = FC * rows // T
     tile = lambda n: pl.BlockSpec((rows, n), lambda i, c: (i, 0))
     flipped = pl.BlockSpec((rows, D), lambda i, c: ((i + half) % (2 * half), 0))
     whole = lambda a: pl.BlockSpec(a.shape, lambda i, c: (0,) * a.ndim)
@@ -604,21 +608,24 @@
         grid_spec=pltpu.PrefetchScalarGridSpec(
             num_scalar_prefetch=1,
             grid=(T // rows,),
-            in_specs=[tile(D), tile(8), tile(D), tile(D), flipped, whole(vec)],
+            in_specs=[whole(h2), pl.BlockSpec((T, cols), lambda i, c: (0, i))]
+            + [tile(D), tile(8), tile(D), tile(D), flipped, whole(vec)],
             out_specs=[
+                pl.BlockSpec((D, cols), lambda i, c: (0, i)),
                 pl.BlockSpec((rows, D), lambda i, c: (jnp.minimum(i, half - 1), 0)),
                 tile(D),
                 pl.BlockSpec((8, D), lambda i, c: (0, 0)),
             ],
         ),
         out_shape=[
+            jax.ShapeDtypeStruct((D, FC), bf16),
             jax.ShapeDtypeStruct((S, D), f32),
             jax.ShapeDtypeStruct((T, D), bf16),
             jax.ShapeDtypeStruct((8, D), f32),
         ],
         compiler_params=params(),
-        cost_estimate=cost(30 * T * D, T * D * 14),
-    )(place, n2, r2, gy, gh2, other, vec)
+        cost_estimate=cost(2 * T * D * FC, T * D * 18 + T * FC * 2 + D * FC * 2),
+    )(place, h2, gup, n2, r2, gy, gh2, other, vec)
 
 
 def back_head(q_t, k, v, do, do_t, delta, p, mine, head):
@@ -1011,14 +1018,10 @@
     shares = share_call(me, w_qkv, vectors)
     shares, share_fc2 = lax.optimization_barrier((shares, share_fc2))
     full_fc2 = lax.all_gather(share_fc2, "dp", axis=0, tiled=True)
-    quarter = plane_swap(shares).reshape(QUARTER, 3 * DC + 128)
-    qkv_pieces = along_line(quarter)
     fc1_b = w_fc1.astype(bf16).reshape(KR, CHIPS, CORES, FR)
     share_fc1 = jnp.where(first_core, fc1_b[:, :, 0], fc1_b[:, :, 1]).reshape(KR, FC)
     share = jnp.concatenate([share_fc1, w_proj.astype(bf16)], axis=1)
     share = jnp.broadcast_to(share[None], (PLANE,) + share.shape)
-    share, qkv_pieces[1] = lax.optimization_barrier((share, qkv_pieces[1]))
-    quarter = plane_swap(share).reshape(QUARTER, FC + D)
 
     x_own = tokens.reshape(S, D)
     cot_own = cotangent.reshape(S, D)
@@ -1036,12 +1039,21 @@
     counts1 = jnp.where(first_core, ints[1, 2, :1], ints[0, 2, :1])
     place = jnp.concatenate([jnp.stack([core, along]).astype(jnp.int32), counts0, counts1])
 
+    quarter = plane_swap(shares).reshape(QUARTER, 3 * DC + 128)
+    quarter, share, ints, x_other, cot_other = lax.optimization_barrier(
+        (quarter, share, ints, x_other, cot_other)
+    )
+    qkv_pieces = along_line(quarter)
+    share, qkv_pieces[1] = lax.optimization_barrier((share, qkv_pieces[1]))
+    quarter = plane_swap(share).reshape(QUARTER, FC + D)
+
     vec, h1t, cosine, sine, q, k, v, b1, pos = qkv_call(place, x_own, x_other, ints, qkv_pieces)
     q, quarter = lax.optimization_barrier((q, quarter))
     pieces = along_line(quarter)
     mine, p0, p1 = attn_fwd_call(place, q, k, v)
-    mine, pieces[1], pieces[3], cot_other = lax.optimization_barrier((mine, pieces[1], pieces[3], cot_other))
+    mine, pieces[1], pieces[3] = lax.optimization_barrier((mine, pieces[1], pieces[3]))
     other = swap(mine)
+    cot_other, mine = lax.optimization_barrier((cot_other, mine))
     gy = gy_call(place, cot_own, cot_other)
     other, gy = lax.optimization_barrier((other, gy))
     after, n2, r2, h2 = proj_call(place, mine, other, x_own, x_other, pieces, vec)
@@ -1049,11 +1061,11 @@
     other_gh2 = swap(gh2)
     mlp_other = swap(mlp_part)
 
-    gw1, gw2 = fc_grad_call(place, h2, gup, act, gy)
-    gw1, gw2, other_gh2 = lax.optimization_barrier((gw1, gw2, other_gh2))
+    gw2 = fc2_grad_call(place, act, gy)
+    gw2, other_gh2 = lax.optimization_barrier((gw2, other_gh2))
     sum_fc2 = line_sum(gw2)
+    gw1, ga, gab, sums_mid = mid_call(place, h2, gup, n2, r2, gy, gh2, other_gh2, vec)
     sum_fc1 = line_sum(gw1)
-    ga, gab, sums_mid = mid_call(place, n2, r2, gy, gh2, other_gh2, vec)
     *gw, gh1, gh1_part = attn_bwd_call(
         place, q, k, v, gab, mine, other, p0, p1, cosine, sine, pos, h1t, qkv_pieces, pieces,
         x_own, x_other, sums_mid, gb1,

time: 290 us -> 297 us (1.024)
  waiting for transfers between devices: 68.9 us -> 74.2 us
    reduce_scatter x2, waiting for transfers between devices: 18.6 us -> 0.28 us  [line_sum(): lax.psum_scatter(whole, BOTH, scatter_dimension=0, axis_index_groups=line...]
    all_to_all x4, waiting for transfers between devices: 24.6 us -> 38.3 us  [plane_swap(): return lax.all_to_all(value, BOTH, 0, 0, axis_index_groups=planes())]
    ppermute x9, waiting for transfers between devices: 18.9 us -> 29.3 us  [shift(): return lax.ppermute(value, BOTH, pairs)]
    pallas_call x1, Pallas kernels: 12.8 us -> 7.58 us  [fc2_grad_call(): pl.pallas_call(fc2_grad_kernel, grid_spec=pltpu.PrefetchScalarGridSpec(nu...]
    pallas_call x1, Pallas kernels: 8.04 us -> 12.8 us  [mid_call(): pl.pallas_call(mid_kernel, grid_spec=pltpu.PrefetchScalarGridSpec(num_sca...]
    all_to_all x4, starting transfers between devices: 28.6 us -> 23.9 us  [plane_swap(): return lax.all_to_all(value, BOTH, 0, 0, axis_index_groups=planes())]
    ppermute x9, starting transfers between devices: 12 us -> 15.6 us  [shift(): return lax.ppermute(value, BOTH, pairs)]
    unnamed x42 -> x46, local copies, waits for them, and re-layouts: 7.71 us -> 8.86 us
  transfers between devices with their start and end apart: 26 -> 26, of which waited for: 10 -> 13; matrix products, arithmetic and copies ran while one was open for 2% -> 3% of each run, Pallas kernels for 37% -> 36%
where the time goes in v1:
time: 297 us; the launch traced here: 291 us
  Pallas kernels  131 us (44%)
  waiting for transfers between devices  74.2 us (25%)
  starting transfers between devices  50.1 us (17%)
  between operations  15.7 us (5%)
  local copies, waits for them, and re-layouts  13.7 us (5%)
  other arithmetic  6.33 us (2%)
    all_to_all x4, waiting for transfers between devices, plane_swap(): return lax.all_to_all(value, BOTH, 0, 0, axis_index_groups=planes())  38.3 us
    ppermute x9, waiting for transfers between devices, shift(): return lax.ppermute(value, BOTH, pairs)  29.3 us
    pallas_call x1, Pallas kernels, attn_bwd_call(): pl.pallas_call(attn_bwd_kernel, grid_spec=pltpu.PrefetchScalarGridSpec(nu...  28.4 us
    all_to_all x4, starting transfers between devices, plane_swap(): return lax.all_to_all(value, BOTH, 0, 0, axis_index_groups=planes())  23.9 us
    pallas_call x1, Pallas kernels, mlp_call(): pl.pallas_call(mlp_kernel, grid_spec=pltpu.PrefetchScalarGridSpec(num_sca...  18.7 us
    ppermute x9, starting transfers between devices, shift(): return lax.ppermute(value, BOTH, pairs)  15.6 us
    pallas_call x1, Pallas kernels, qkv_call(): pl.pallas_call(qkv_kernel, grid_spec=pltpu.PrefetchScalarGridSpec(num_sca...  14 us
    pallas_call x1, Pallas kernels, mid_call(): pl.pallas_call(mid_kernel, grid_spec=pltpu.PrefetchScalarGridSpec(num_sca...  12.8 us
  transfers between devices with their start and end apart: 26, of which 13 were waited for; matrix products, arithmetic and copies ran while one was open for 3% of the time, Pallas kernels for 36%

profile of v1, /device:TPU:0, one launch (start us, length us, event | category | flops | bytes accessed | tf_op | source)
XLA Modules:
  0.0 291.3 jit_solution(16274901387688703025)
XLA Ops:
  7.3 0.9 convert_element_type.9
  9.4 2.5 shard_map.339
  13.5 8.1 %all-to-all-start = ((bf16[16,12,1280]{2,1,0:T(8,128)(2,1)}), bf16[16,12,1280]{2,1,0:T(8,128)(2,1)S(1)}, u32[]{:S(2)}, u32[]{:S(2)}) async-start(bf16[16,12,1280]{2,1,0:T(8,128)(2,1)} %shard_map.339), calls=%async_computation | async-start | bytes 1310720 | tf_op jit(solution)/shard_map/all_to_all | solution.py:74
  22.3 1.4 fusion
  24.7 9.0 %all-to-all-done = bf16[16,12,1280]{2,1,0:T(8,128)(2,1)S(1)} async-done(((bf16[16,12,1280]{2,1,0:T(8,128)(2,1)}), bf16[16,12,1280]{2,1,0:T(8,128)(2,1)S(1)}, u32[]{:S(2)}, u32[]{:S(2)}) %all-to-all-start) | async-done | bytes 491552 | tf_op jit(solution)/shard_map/all_to_all | solution.py:74
  33.9 1.2 broadcast_in_dim.10
  35.7 9.5 %collective-permute-done.3.w1.v1 = bf16[192,1280]{1,0:T(8,128)(2,1)S(1)} collective-permute-done((bf16[192,1280]{1,0:T(8,128)(2,1)S(1)}, bf16[192,1280]{1,0:T(8,128)(2,1)S(1)}, u32[]{:S(2)}, u32[]{:S(2)}) %collective-permute-start.3) | collective-permute-done | bytes 491552 | tf_op jit(solution)/shard_map/ppermute | solution.py:70
  46.0 4.6 %all-to-all-start.1 = ((bf16[16,12,2304]{2,1,0:T(8,128)(2,1)}), bf16[16,12,2304]{2,1,0:T(8,128)(2,1)S(1)}, u32[]{:S(2)}, u32[]{:S(2)}) async-start(bf16[16,12,2304]{2,1,0:T(8,128)(2,1)} %broadcast_in_dim.10), calls=%async_computation.1 | async-start | bytes 2359296 | tf_op jit(solution)/shard_map/all_to_all | solution.py:74
  50.6 1.6 collective-permute-start.5
  52.3 1.2 collective-permute-start.4
  53.5 1.2 slice.39
  54.7 1.2 slice.38
  58.5 5.5 %collective-permute-done.5.w3.v3 = bf16[192,1280]{1,0:T(8,128)(2,1)S(1)} collective-permute-done((bf16[192,1280]{1,0:T(8,128)(2,1)S(1)}, bf16[192,1280]{1,0:T(8,128)(2,1)S(1)}, u32[]{:S(2)}, u32[]{:S(2)}) %collective-permute-start.5) | collective-permute-done | bytes 491552 | tf_op jit(solution)/shard_map/ppermute | solution.py:70
  64.0 1.6 collective-permute-done.4.w2.v2
  66.3 14.0 %shard_map.340 = (f32[16,768]{1,0:T(8,128)}, bf16[2,768,576]{2,1,0:T(8,128)(2,1)}, f32[1152,384]{1,0:T(8,128)}, f32[1152,384]{1,0:T(8,128)}, bf16[1152,384]{1,0:...) custom-call(s32[5]{0:T(128)} %pad_add_fusion.2.place_ref, ...), custom_call_target="tpu_custom_call" | custom-call | flops 2064973824 | bytes 13271040 | tf_op jit(solution)/shard_map/pallas_call | solution.py:312
  80.5 6.6 %collective-permute-start.7 = (bf16[192,2304]{1,0:T(8,128)(2,1)S(1)}, bf16[192,2304]{1,0:T(8,128)(2,1)S(1)}, u32[]{:S(2)}, u32[]{:S(2)}) collective-permute-start(bf16[192,2304]{1,0:T(8,128)(2,1)S(1)} %reshape.114.w0.w10.y0), channel_id=1, source_target_pairs={{0,48},{16,0},{32,16},{48,32},{1,49},{17,1},{33,17},{49,33},{2,50}... | collective-permute-start | bytes 2654216 | tf_op jit(solution)/shard_map/ppermute | solution.py:70
  87.2 11.3 %shard_map.341 = (bf16[2,576,384]{2,1,0:T(8,128)(2,1)}, bf16[6,2,208,208]{3,2,1,0:T(8,128)(2,1)}, bf16[6,576,576]{2,1,0:T(8,128)(2,1)}) custom-call(s32[5]{0:T(128)} %pad_add_fusion.2.place_ref, bf16[2,576,384]{2,1,0:T(8,128)(2,1)} %bitcast.28, bf16[2,576,384]{2,1,0:T(8,128)(2,1)} %bitcast.32, bf16[2,576,384]{2,1,0:T(8,128)(2,1)} %bitcast.36, ...), custom_call_target="tpu_custom_call" | custom-call | flops 1285029888 | bytes 12000000 | tf_op jit(solution)/shard_map/pallas_call | solution.py:385
  99.2 2.5 collective-permute-done.6.w1.w11.y1
  102.0 1.4 collective-permute-start.9
  103.4 3.6 %shard_map.342.gy_ref = bf16[1152,768]{1,0:T(8,128)(2,1)} custom-call(s32[5]{0:T(128)} %pad_add_fusion.2.place_ref, bf16[576,768]{1,0:T(8,128)(2,1)} %bitcast.54, bf16[576,768]{1,0:T(8,128)(2,1)} %copy-done.12), custom_call_target="tpu_custom_call" | custom-call | flops 3538944 | bytes 3538944 | tf_op jit(solution)/shard_map/pallas_call | solution.py:238
  106.9 9.6 %collective-permute-done.9.w2.w12.y2 = bf16[192,2304]{1,0:T(8,128)(2,1)S(1)} collective-permute-done((bf16[192,2304]{1,0:T(8,128)(2,1)S(1)}, bf16[192,2304]{1,0:T(8,128)(2,1)S(1)}, u32[]{:S(2)}, u32[]{:S(2)}) %collective-permute-start.9) | collective-permute-done | bytes 884768 | tf_op jit(solution)/shard_map/ppermute | solution.py:70
  116.5 0.9 copy-done.6
  117.4 8.8 %shard_map.343 = (f32[576,768]{1,0:T(8,128)}, f32[1152,768]{1,0:T(8,128)}, f32[1152,8]{1,0:T(8,128)}, bf16[1152,768]{1,0:T(8,128)(2,1)}) custom-call(s32[5]{0:T(128)} %pad_add_fusion.2.place_ref, bf16[2,576,384]{2,1,0:T(8,128)(2,1)} %get-tuple-element.117.mine_ref.o0.o1, bf16[2,576,384]{2,1,0:T(8,128)(2,1)} %copy-done.5, bf16[576,768]{1,0:T(8,128)(2,1)} %bitcast.42, ...), custom_call_target="tpu_custom_call" | custom-call | flops 1358954496 | bytes 10027008 | tf_op jit(solution)/shard_map/pallas_call | solution.py:433
  126.3 18.7 %shard_map.344 = (f32[576,768]{1,0:T(8,128)}, f32[576,768]{1,0:T(8,128)}, bf16[1152,768]{1,0:T(8,128)(2,1)}, bf16[1152,1536]{1,0:T(8,128)(2,1)}, bf16[1152,1536]{1,0:T(8,128)(2,1)}, /*index=5*/f32[1,1536]{1,0:T(1,128)}) custom-call(s32[5]{0:T(128)} %pad_add_fusion.2.place_ref, bf16[1152,768]{1,0:T(8,128)(2,1)} %get-tuple-element.129.h2_ref, ...), custom_call_target="tpu_custom_call" | custom-call | flops 10871635968 | bytes 30000000 | tf_op jit(solution)/shard_map/pallas_call | solution.py:507
  145.1 7.6 %shard_map.345 = bf16[1536,768]{1,0:T(8,128)(2,1)} custom-call(s32[5]{0:T(128)} %pad_add_fusion.2.place_ref, bf16[1152,1536]{1,0:T(8,128)(2,1)} %get-tuple-element.137.act_ref, bf16[1152,768]{1,0:T(8,128)(2,1)} %shard_map.342.gy_ref), custom_call_target="tpu_custom_call" | custom-call | flops 2717908992 | bytes 7667712 | tf_op jit(solution)/shard_map/pallas_call | solution.py:555
  152.9 1.0 copy-done.9
  153.9 12.8 %shard_map.346 = (bf16[768,1536]{1,0:T(8,128)(2,1)}, f32[576,768]{1,0:T(8,128)}, bf16[1152,768]{1,0:T(8,128)(2,1)}, f32[8,768]{1,0:T(8,128)}) custom-call(s32[5]{0:T(128)} %pad_add_fusion.2.place_ref, bf16[1152,768]{1,0:T(8,128)(2,1)} %get-tuple-element.129.h2_ref, bf16[1152,1536]{1,0:T(8,128)(2,1)} %get-tuple-element.133.gup_ref, ...), custom_call_target="tpu_custom_call" | custom-call | flops 2717908992 | bytes 21823488 | tf_op jit(solution)/shard_map/pallas_call | solution.py:606
  166.7 28.4 %shard_map.347 = (bf16[192,1664]{1,0:T(8,128)(2,1)}, bf16[192,1664]{1,0:T(8,128)(2,1)}, bf16[192,1664]{1,0:T(8,128)(2,1)}, bf16[192,1664]{1,0:T(8,128)(2,1)}, f32[576,768]{1,0:T(8,128)}, /*index=5*/f32[576,768]{1,0:T(8,128)}) custom-call(s32[5]{0:T(128)} %pad_add_fusion.2.place_ref, bf16[2,576,384]{2,1,0:T(8,128)(2,1)} %bitcast.30, ...), custom_call_target="tpu_custom_call" | custom-call | flops 7983857664 | bytes 36000000 | tf_op jit(solution)/shard_map/pallas_call | solution.py:773
  195.3 2.3 collective-permute-start.12
  197.6 1.6 collective-permute-start.13
  199.2 6.1 %all-to-all-start.2 = ((bf16[16,24,768]{2,1,0:T(8,128)(2,1)}), bf16[16,24,768]{2,1,0:T(8,128)(2,1)S(1)}, u32[]{:S(2)}, u32[]{:S(2)}) async-start(bf16[16,24,768]{2,1,0:T(8,128)(2,1)} %bitcast.55), calls=%async_computation.3 | async-start | bytes 1179648 | tf_op jit(solution)/shard_map/all_to_all | solution.py:74
  206.4 14.2 %all-to-all-done.2.in_ref = bf16[16,24,768]{2,1,0:T(8,128)(2,1)S(1)} async-done(((bf16[16,24,768]{2,1,0:T(8,128)(2,1)}), bf16[16,24,768]{2,1,0:T(8,128)(2,1)S(1)}, u32[]{:S(2)}, u32[]{:S(2)}) %all-to-all-start.2) | async-done | bytes 589856 | tf_op jit(solution)/shard_map/all_to_all | solution.py:74
  220.7 0.8 copy-done.15
  221.5 3.4 %shard_map.348 = bf16[16,12,3200]{2,1,0:T(8,128)(2,1)} custom-call(bf16[192,1664]{1,0:T(8,128)(2,1)} %get-tuple-element.142.q0, bf16[192,1664]{1,0:T(8,128)(2,1)} %copy-done.15, bf16[192,1664]{1,0:T(8,128)(2,1)} %collective-permute-done.12.q2, bf16[192,1664]{1,0:T(8,128)(2,1)} %collective-permute-done.13.q3, ...), custom_call_target="tpu_custom_call" | custom-call | flops 1277952 | bytes 3194880 | tf_op jit(solution)/shard_map/pallas_call | solution.py:845
  224.9 5.1 %all-to-all-start.3 = ((bf16[16,12,3200]{2,1,0:T(8,128)(2,1)}), bf16[16,12,3200]{2,1,0:T(8,128)(2,1)S(1)}, u32[]{:S(2)}, u32[]{:S(2)}) async-start(bf16[16,12,3200]{2,1,0:T(8,128)(2,1)} %shard_map.348), calls=%async_computation.5 | async-start | bytes 3276800 | tf_op jit(solution)/shard_map/all_to_all | solution.py:74
  230.0 1.8 shard_map.349.mine_ref
  231.8 1.5 collective-permute-done.14.other_ref
  233.9 2.3 shard_map.350
  236.2 15.0 %all-to-all-done.3.in_ref = bf16[16,12,3200]{2,1,0:T(8,128)(2,1)S(1)} async-done(((bf16[16,12,3200]{2,1,0:T(8,128)(2,1)}), bf16[16,12,3200]{2,1,0:T(8,128)(2,1)S(1)}, u32[]{:S(2)}, u32[]{:S(2)}) %all-to-all-start.3) | async-done | bytes 1228832 | tf_op jit(solution)/shard_map/all_to_all | solution.py:74
  251.3 1.2 copy-done.1
  252.4 2.3 shard_map.351.g_ref.mine_ref
  254.8 1.7 collective-permute-done.15.o_ref.other_ref
  257.1 2.0 shard_map.352
  259.1 8.4 %all-to-all-start.4 = ((f32[64,8,128]{2,1,0:T(8,128)}), f32[64,8,128]{2,1,0:T(8,128)S(1)}, u32[]{:S(2)}, u32[]{:S(2)}) async-start(f32[64,8,128]{2,1,0:T(8,128)} %shard_map.352), calls=%async_computation.6 | async-start | bytes 524288 | tf_op jit(solution)/shard_map/all_to_all | solution.py:1087
  267.5 1.3 copy-done.10
  268.8 6.2 %shard_map.353 = (f32[576,768]{1,0:T(8,128)}, bf16[576,768]{1,0:T(8,128)(2,1)}) custom-call(bf16[576,768]{1,0:T(8,128)(2,1)} %bitcast.44, f32[576,768]{1,0:T(8,128)} %get-tuple-element.156.ga_ref, f32[576,768]{1,0:T(8,128)} %get-tuple-element.157.gh_ref, f32[576,768]{1,0:T(8,128)} %collective-permute-done.16.other_ref, ...), custom_call_target="tpu_custom_call" | custom-call | flops 13271040 | bytes 12386304 | tf_op jit(solution)/shard_map/pallas_call | solution.py:821
  275.0 3.2 %all-to-all-done.4.norm_ref = f32[64,8,128]{2,1,0:T(8,128)S(1)} async-done(((f32[64,8,128]{2,1,0:T(8,128)}), f32[64,8,128]{2,1,0:T(8,128)S(1)}, u32[]{:S(2)}, u32[]{:S(2)}) %all-to-all-start.4) | async-done | bytes 262176 | tf_op jit(solution)/shard_map/all_to_all | solution.py:1087
  278.9 5.6 %shard_map.354 = (f32[12,2304]{1,0:T(8,128)}, f32[12,2304]{1,0:T(8,128)}, f32[12,2304]{1,0:T(8,128)}, f32[12,768]{1,0:T(8,128)}, f32[12,768]{1,0:T(8,128)}, /*in...) custom-call(s32[5]{0:T(128)} %pad_add_fusion.2.place_ref, ...), custom_call_target="tpu_custom_call" | custom-call | flops 2211840 | bytes 3000000 | tf_op jit(solution)/shard_map/pallas_call | solution.py:964
  (89 shorter events, 12.9 us)
Async XLA Ops:
  7.2 14.5 %copy-start.14 = (f32[12,3072]{1,0:T(8,128)S(1)}, f32[12,3072]{1,0:T(8,128)}, u32[]{:S(2)}) copy-start(f32[12,3072]{1,0:T(8,128)} %refs_2_.1) | copy-start | bytes 442372
  7.2 119.1 %all-gather.2.cloned.1.call-start = ((), (), s32[]{:S(2)}) async-start(), calls=%async_computation.7 | async-start | bytes 2396160 | tf_op jit(solution)/shard_map/all_gather | solution.py:1020
  11.9 11.8 %copy-start.19 = (f32[12,768]{1,0:T(8,128)S(1)}, f32[12,768]{1,0:T(8,128)}, u32[]{:S(2)}) copy-start(f32[12,768]{1,0:T(8,128)} %refs_1_.1) | copy-start | bytes 110596
  12.0 21.9 %collective-permute-start.1 = (bf16[576,768]{1,0:T(8,128)(2,1)}, bf16[576,768]{1,0:T(8,128)(2,1)S(1)}, u32[]{:S(2)}, u32[]{:S(2)}) collective-permute-start(bf16[576,768]{1,0:T(8,128)(2,1)} %bitcast.40), channel_id=1, source_target_pairs={{0,64},{64,0},{1,65},{65,1},{2,66},{66,2},{3,67},{67,3},{4,68},{68... | collective-permute-start | bytes 2654216 | tf_op jit(solution)/shard_map/ppermute | solution.py:1007
  12.0 21.8 %collective-permute-start.2 = (bf16[576,768]{1,0:T(8,128)(2,1)}, bf16[576,768]{1,0:T(8,128)(2,1)S(1)}, u32[]{:S(2)}, u32[]{:S(2)}) collective-permute-start(bf16[576,768]{1,0:T(8,128)(2,1)} %bitcast.53), channel_id=1, source_target_pairs={{0,64},{64,0},{1,65},{65,1},{2,66},{66,2},{3,67},{67,3},{4,68},{68... | collective-permute-start | bytes 2654216 | tf_op jit(solution)/shard_map/ppermute | solution.py:1007
  13.4 10.7 %copy-start.20 = (s32[1,8,576]{2,1,0:T(8,128)}, s32[1,8,576]{2,1,0:T(8,128)S(1)}, u32[]{:S(2)}) copy-start(s32[1,8,576]{2,1,0:T(8,128)S(1)} %get-tuple-element.185) | copy-start | bytes 55300
  13.4 10.7 %collective-permute-start = (s32[8,576]{1,0:T(8,128)S(1)}, s32[8,576]{1,0:T(8,128)S(1)}, u32[]{:S(2)}, u32[]{:S(2)}) collective-permute-start(s32[8,576]{1,0:T(8,128)S(1)} %get-tuple-element.186), channel_id=1, source_target_pairs={{0,64},{64,0},{1,65},{65,1},{2,66},{66,2},{3,67},{67,3},{4,68},{68... | collective-permute-start | bytes 55304 | tf_op jit(solution)/shard_map/ppermute | solution.py:1007
  13.5 20.2 %all-to-all-start = ((bf16[16,12,1280]{2,1,0:T(8,128)(2,1)}), bf16[16,12,1280]{2,1,0:T(8,128)(2,1)S(1)}, u32[]{:S(2)}, u32[]{:S(2)}) async-start(bf16[16,12,1280]{2,1,0:T(8,128)(2,1)} %shard_map.339), calls=%async_computation | async-start | bytes 1310720 | tf_op jit(solution)/shard_map/all_to_all | solution.py:74
  24.1 21.1 %copy-start.22 = (s32[8,576]{1,0:T(8,128)}, s32[8,576]{1,0:T(8,128)S(1)}, u32[]{:S(2)}) copy-start(s32[8,576]{1,0:T(8,128)S(1)} %collective-permute-done) | copy-start | bytes 55300
  33.8 18.4 %copy-start.8 = (bf16[192,1280]{1,0:T(8,128)(2,1)}, bf16[192,1280]{1,0:T(8,128)(2,1)S(1)}, u32[]{:S(2)}) copy-start(bf16[192,1280]{1,0:T(8,128)(2,1)S(1)} %reshape.111.w0.v0) | copy-start | bytes 1474564
  33.8 12.2 %copy-start.2 = (bf16[576,768]{1,0:T(8,128)(2,1)}, bf16[576,768]{1,0:T(8,128)(2,1)S(1)}, u32[]{:S(2)}) copy-start(bf16[576,768]{1,0:T(8,128)(2,1)S(1)} %collective-permute-done.1.xo_ref) | copy-start | bytes 2654212
  33.9 12.2 %copy-start.12 = (bf16[576,768]{1,0:T(8,128)(2,1)}, bf16[576,768]{1,0:T(8,128)(2,1)S(1)}, u32[]{:S(2)}) copy-start(bf16[576,768]{1,0:T(8,128)(2,1)S(1)} %collective-permute-done.2.co_ref) | copy-start | bytes 2654212
  35.1 10.1 %collective-permute-start.3 = (bf16[192,1280]{1,0:T(8,128)(2,1)S(1)}, bf16[192,1280]{1,0:T(8,128)(2,1)S(1)}, u32[]{:S(2)}, u32[]{:S(2)}) collective-permute-start(bf16[192,1280]{1,0:T(8,128)(2,1)S(1)} %reshape.111.w0.v0), channel_id=1, source_target_pairs={{0,16},{16,32},{32,48},{48,0},{1,17},{17,33},{33,49},{49,1},{2,18}... | collective-permute-start | bytes 1474568 | tf_op jit(solution)/shard_map/ppermute | solution.py:70
  45.2 0.8 copy-start.16
  46.0 34.3 %all-to-all-start.1 = ((bf16[16,12,2304]{2,1,0:T(8,128)(2,1)}), bf16[16,12,2304]{2,1,0:T(8,128)(2,1)S(1)}, u32[]{:S(2)}, u32[]{:S(2)}) async-start(bf16[16,12,2304]{2,1,0:T(8,128)(2,1)} %broadcast_in_dim.10), calls=%async_computation.1 | async-start | bytes 2359296 | tf_op jit(solution)/shard_map/all_to_all | solution.py:74
  50.6 148.6 %reduce-scatter.3.cloned.1.call-start = ((), (), s32[]{:S(2)}) async-start(), calls=%async_computation.8 | async-start | bytes 2949120 | tf_op jit(solution)/shard_map/reduce_scatter | solution.py:1013
  50.6 13.3 %collective-permute-start.5 = (bf16[192,1280]{1,0:T(8,128)(2,1)S(1)}, bf16[192,1280]{1,0:T(8,128)(2,1)S(1)}, u32[]{:S(2)}, u32[]{:S(2)}) collective-permute-start(bf16[192,1280]{1,0:T(8,128)(2,1)S(1)} %reshape.111.w0.v0), channel_id=1, source_target_pairs={{0,48},{16,0},{32,16},{48,32},{1,49},{17,1},{33,17},{49,33},{2,50}... | collective-permute-start | bytes 1474568 | tf_op jit(solution)/shard_map/ppermute | solution.py:70
  52.3 13.3 %collective-permute-start.4 = (bf16[192,1280]{1,0:T(8,128)(2,1)S(1)}, bf16[192,1280]{1,0:T(8,128)(2,1)S(1)}, u32[]{:S(2)}, u32[]{:S(2)}) collective-permute-start(bf16[192,1280]{1,0:T(8,128)(2,1)S(1)} %reshape.111.w0.v0), channel_id=1, source_target_pairs={{0,32},{16,48},{32,0},{48,16},{1,33},{17,49},{33,1},{49,17},{2,34}... | collective-permute-start | bytes 1474568 | tf_op jit(solution)/shard_map/ppermute | solution.py:70
  63.9 1.6 copy-start.17
  65.5 0.8 copy-start.18
  80.5 21.4 %copy-start = (bf16[192,2304]{1,0:T(8,128)(2,1)}, bf16[192,2304]{1,0:T(8,128)(2,1)S(1)}, u32[]{:S(2)}) copy-start(bf16[192,2304]{1,0:T(8,128)(2,1)S(1)} %reshape.114.w0.w10.y0) | copy-start | bytes 2654212
  80.5 18.6 %collective-permute-start.7 = (bf16[192,2304]{1,0:T(8,128)(2,1)S(1)}, bf16[192,2304]{1,0:T(8,128)(2,1)S(1)}, u32[]{:S(2)}, u32[]{:S(2)}) collective-permute-start(bf16[192,2304]{1,0:T(8,128)(2,1)S(1)} %reshape.114.w0.w10.y0), channel_id=1, source_target_pairs={{0,48},{16,0},{32,16},{48,32},{1,49},{17,1},{33,17},{49,33},{2,50}... | collective-permute-start | bytes 2654216 | tf_op jit(solution)/shard_map/ppermute | solution.py:70
  87.2 14.5 %collective-permute-start.6 = (bf16[192,2304]{1,0:T(8,128)(2,1)S(1)}, bf16[192,2304]{1,0:T(8,128)(2,1)S(1)}, u32[]{:S(2)}, u32[]{:S(2)}) collective-permute-start(bf16[192,2304]{1,0:T(8,128)(2,1)S(1)} %reshape.114.w0.w10.y0), channel_id=1, source_target_pairs={{0,16},{16,32},{32,48},{48,0},{1,17},{17,33},{33,49},{49,1},{2,18}... | collective-permute-start | bytes 2654216 | tf_op jit(solution)/shard_map/ppermute | solution.py:70
  99.2 7.8 %copy-start.3 = (bf16[192,2304]{1,0:T(8,128)(2,1)}, bf16[192,2304]{1,0:T(8,128)(2,1)S(1)}, u32[]{:S(2)}) copy-start(bf16[192,2304]{1,0:T(8,128)(2,1)S(1)} %collective-permute-done.7.w3.w13.y3) | copy-start | bytes 2654212
  101.7 5.2 %copy-start.4 = (bf16[192,2304]{1,0:T(8,128)(2,1)}, bf16[192,2304]{1,0:T(8,128)(2,1)S(1)}, u32[]{:S(2)}) copy-start(bf16[192,2304]{1,0:T(8,128)(2,1)S(1)} %collective-permute-done.6.w1.w11.y1) | copy-start | bytes 2654212
  101.7 5.2 %collective-permute-start.8 = (bf16[2,576,384]{2,1,0:T(8,128)(2,1)}, bf16[2,576,384]{2,1,0:T(8,128)(2,1)S(1)}, u32[]{:S(2)}, u32[]{:S(2)}) collective-permute-start(bf16[2,576,384]{2,1,0:T(8,128)(2,1)} %get-tuple-element.117.mine_ref.o0.o1), channel_id=1, source_target_pairs={{0,64},{64,0},{1,65},{65,1},{2,66},{66,2},{3,67},{67,3},{4,68},{68... | collective-permute-start | bytes 2654216 | tf_op jit(solution)/shard_map/ppermute | solution.py:1007
  102.0 14.5 %collective-permute-start.9 = (bf16[192,2304]{1,0:T(8,128)(2,1)S(1)}, bf16[192,2304]{1,0:T(8,128)(2,1)S(1)}, u32[]{:S(2)}, u32[]{:S(2)}) collective-permute-start(bf16[192,2304]{1,0:T(8,128)(2,1)S(1)} %reshape.114.w0.w10.y0), channel_id=1, source_target_pairs={{0,32},{16,48},{32,0},{48,16},{1,33},{17,49},{33,1},{49,17},{2,34}... | collective-permute-start | bytes 2654216 | tf_op jit(solution)/shard_map/ppermute | solution.py:70
  106.9 9.6 %copy-start.5 = (bf16[2,576,384]{2,1,0:T(8,128)(2,1)}, bf16[2,576,384]{2,1,0:T(8,128)(2,1)S(1)}, u32[]{:S(2)}) copy-start(bf16[2,576,384]{2,1,0:T(8,128)(2,1)S(1)} %collective-permute-done.8.other_ref) | copy-start | bytes 2654212
  116.5 0.9 copy-start.6
  145.0 7.6 %collective-permute-start.10 = (bf16[1152,768]{1,0:T(8,128)(2,1)}, bf16[1152,768]{1,0:T(8,128)(2,1)S(1)}, u32[]{:S(2)}, u32[]{:S(2)}) collective-permute-start(bf16[1152,768]{1,0:T(8,128)(2,1)} %get-tuple-element.136.gh2_ref), channel_id=1, source_target_pairs={{0,64},{64,0},{1,65},{65,1},{2,66},{66,2},{3,67},{67,3},{4,68},{68... | collective-permute-start | bytes 5308424 | tf_op jit(solution)/shard_map/ppermute | solution.py:1007
  152.6 1.3 copy-start.9
  152.7 53.8 %reduce-scatter.5.cloned.1.call-start = ((), (), s32[]{:S(2)}) async-start(), calls=%async_computation.9 | async-start | bytes 2949120 | tf_op jit(solution)/shard_map/reduce_scatter | solution.py:1013
  195.1 25.6 %collective-permute-start.11 = (bf16[192,1664]{1,0:T(8,128)(2,1)}, bf16[192,1664]{1,0:T(8,128)(2,1)S(1)}, u32[]{:S(2)}, u32[]{:S(2)}) collective-permute-start(bf16[192,1664]{1,0:T(8,128)(2,1)} %get-tuple-element.143), channel_id=1, source_target_pairs={{0,16},{16,32},{32,48},{48,0},{1,17},{17,33},{33,49},{49,1},{2,18}... | collective-permute-start | bytes 1916936 | tf_op jit(solution)/shard_map/ppermute | solution.py:70
  195.3 25.4 %collective-permute-start.12 = (bf16[192,1664]{1,0:T(8,128)(2,1)}, bf16[192,1664]{1,0:T(8,128)(2,1)}, u32[]{:S(2)}, u32[]{:S(2)}) collective-permute-start(bf16[192,1664]{1,0:T(8,128)(2,1)} %get-tuple-element.144), channel_id=1, source_target_pairs={{0,32},{16,48},{32,0},{48,16},{1,33},{17,49},{33,1},{49,17},{2,34}... | collective-permute-start | bytes 1916936 | tf_op jit(solution)/shard_map/ppermute | solution.py:70
  197.6 23.1 %collective-permute-start.13 = (bf16[192,1664]{1,0:T(8,128)(2,1)}, bf16[192,1664]{1,0:T(8,128)(2,1)}, u32[]{:S(2)}, u32[]{:S(2)}) collective-permute-start(bf16[192,1664]{1,0:T(8,128)(2,1)} %get-tuple-element.145), channel_id=1, source_target_pairs={{0,48},{16,0},{32,16},{48,32},{1,49},{17,1},{33,17},{49,33},{2,50}... | collective-permute-start | bytes 1916936 | tf_op jit(solution)/shard_map/ppermute | solution.py:70
  199.2 21.5 %all-to-all-start.2 = ((bf16[16,24,768]{2,1,0:T(8,128)(2,1)}), bf16[16,24,768]{2,1,0:T(8,128)(2,1)S(1)}, u32[]{:S(2)}, u32[]{:S(2)}) async-start(bf16[16,24,768]{2,1,0:T(8,128)(2,1)} %bitcast.55), calls=%async_computation.3 | async-start | bytes 1179648 | tf_op jit(solution)/shard_map/all_to_all | solution.py:74
  205.3 62.1 %collective-permute-start.17 = (f32[576,768]{1,0:T(8,128)}, f32[576,768]{1,0:T(8,128)S(1)}, u32[]{:S(2)}, u32[]{:S(2)}) collective-permute-start(f32[576,768]{1,0:T(8,128)} %get-tuple-element.161), channel_id=1, source_target_pairs={{0,64},{64,0},{1,65},{65,1},{2,66},{66,2},{3,67},{67,3},{4,68},{68... | collective-permute-start | bytes 5308424 | tf_op jit(solution)/shard_map/ppermute | solution.py:1007
  205.4 62.1 %collective-permute-start.16 = (f32[576,768]{1,0:T(8,128)}, f32[576,768]{1,0:T(8,128)}, u32[]{:S(2)}, u32[]{:S(2)}) collective-permute-start(f32[576,768]{1,0:T(8,128)} %get-tuple-element.158), channel_id=1, source_target_pairs={{0,64},{64,0},{1,65},{65,1},{2,66},{66,2},{3,67},{67,3},{4,68},{68... | collective-permute-start | bytes 5308424 | tf_op jit(solution)/shard_map/ppermute | solution.py:1007
  220.7 4.3 %copy-start.7 = (bf16[16,24,768]{2,1,0:T(8,128)(2,1)}, bf16[16,24,768]{2,1,0:T(8,128)(2,1)S(1)}, u32[]{:S(2)}) copy-start(bf16[16,24,768]{2,1,0:T(8,128)(2,1)S(1)} %all-to-all-done.2.in_ref) | copy-start | bytes 1769476
  220.7 0.9 copy-start.15
  224.9 26.3 %all-to-all-start.3 = ((bf16[16,12,3200]{2,1,0:T(8,128)(2,1)}), bf16[16,12,3200]{2,1,0:T(8,128)(2,1)S(1)}, u32[]{:S(2)}, u32[]{:S(2)}) async-start(bf16[16,12,3200]{2,1,0:T(8,128)(2,1)} %shard_map.348), calls=%async_computation.5 | async-start | bytes 3276800 | tf_op jit(solution)/shard_map/all_to_all | solution.py:74
  231.8 1.5 collective-permute-start.14
  251.3 1.2 copy-start.1
  254.8 1.7 collective-permute-start.15
  256.4 0.7 copy-start.13
  259.1 19.1 %all-to-all-start.4 = ((f32[64,8,128]{2,1,0:T(8,128)}), f32[64,8,128]{2,1,0:T(8,128)S(1)}, u32[]{:S(2)}, u32[]{:S(2)}) async-start(f32[64,8,128]{2,1,0:T(8,128)} %shard_map.352), calls=%async_computation.6 | async-start | bytes 524288 | tf_op jit(solution)/shard_map/all_to_all | solution.py:1087
  267.5 1.3 copy-start.10
  278.2 0.7 copy-start.11
  (1 other events, 0.6 us)
Sparse Core Ops, SparseCore 0:
  12.1 81.3 all-gather.1
  152.8 23.9 reduce-scatter.2
  179.2 27.1 reduce-scatter.4

commit v2 on v1

--- a/solution.py
+++ b/solution.py
@@ -195,7 +195,7 @@
     return sine, cosine
 
 
-def share_kernel(place_ref, w_ref, v_ref, out_ref):
+def share_kernel(place_ref, w_ref, v_ref, f_ref, out_ref, fc2_ref):
     core = place_ref[0]
     w = w_ref[...].astype(bf16)
     cols = []
@@ -209,22 +209,29 @@
     share = jnp.concatenate(cols, axis=1)
     for n in range(PLANE):
         out_ref[n] = share
-
-
-def share_call(place, w, vectors):
+    fc2_ref[...] = jnp.where(core == 0, f_ref[:FR, :], f_ref[FR:, :]).astype(bf16)
+
+
+def share_call(place, w, vectors, w_fc2):
     whole = lambda a: pl.BlockSpec(a.shape, lambda i, c: (0, 0))
     return pl.pallas_call(
         share_kernel,
         grid_spec=pltpu.PrefetchScalarGridSpec(
             num_scalar_prefetch=1,
             grid=(1,),
-            in_specs=[whole(w), whole(vectors)],
-            out_specs=pl.BlockSpec((PLANE, KR, 3 * DC + 128), lambda i, c: (0, 0, 0)),
+            in_specs=[whole(w), whole(vectors), whole(w_fc2)],
+            out_specs=[
+                pl.BlockSpec((PLANE, KR, 3 * DC + 128), lambda i, c: (0, 0, 0)),
+                pl.BlockSpec((FR, D), lambda i, c: (0, 0)),
+            ],
         ),
-        out_shape=jax.ShapeDtypeStruct((PLANE, KR, 3 * DC + 128), bf16),
+        out_shape=[
+            jax.ShapeDtypeStruct((PLANE, KR, 3 * DC + 128), bf16),
+            jax.ShapeDtypeStruct((FR, D), bf16),
+        ],
         compiler_params=params(),
         cost_estimate=cost(KR * D * 3, 1e6),
-    )(place, w, vectors)
+    )(place, w, vectors, w_fc2)
 
 
 def gy_kernel(place_ref, c_ref, co_ref, gy_ref):
@@ -829,25 +836,29 @@
     )(x, ga, gh, other, after, mlp, mlp_other, vec)
 
 
-WIDE = PACK + FC
-
-
-def pack_kernel(q0, q1, q2, q3, f_ref, out_ref):
+WIDE = PACK + 2 * FC
+
+
+def pack_kernel(q0, q1, q2, q3, f1_ref, f2_ref, out_ref):
     total = q0[...].astype(f32) + q1[...].astype(f32) + q2[...].astype(f32) + q3[...].astype(f32)
-    fc1 = f_ref[...].astype(f32)
+    f1 = f1_ref[...].astype(f32)
+    f2 = f2_ref[...].astype(f32)
     for n in range(PLANE):
         at = slice(n * KR, (n + 1) * KR)
         out_ref[n, :, :PACK] = total[at, :].astype(bf16)
-        out_ref[n, :, PACK:] = fc1[at, :].astype(bf16)
-
-
-def pack_call(parts, fc1):
+        out_ref[n, :, PACK : PACK + FC] = f1[at, :].astype(bf16)
+        for h in range(2):
+            to = PACK + FC + h * D
+            out_ref[n, :, to : to + D] = f2[(2 * n + h) * KR : (2 * n + h + 1) * KR, :].astype(bf16)
+
+
+def pack_call(parts, fc1, fc2):
     return pl.pallas_call(
         pack_kernel,
         out_shape=jax.ShapeDtypeStruct((PLANE, KR, WIDE), bf16),
         compiler_params=params(),
-        cost_estimate=cost(QUARTER * PACK * 4, QUARTER * PACK * 10),
-    )(*parts, fc1)
+        cost_estimate=cost(QUARTER * PACK * 4, QUARTER * PACK * 14),
+    )(*parts, fc1, fc2)
 
 
 def sum_kernel(in_ref, out_ref):
@@ -866,53 +877,27 @@
     )(packed)
 
 
-def fc2_kernel(place_ref, mine_ref, other_ref, out_ref, sq_ref):
-    first = place_ref[0] == 0
-    a, b = mine_ref[...], other_ref[...]
-    out_ref[:FR, :] = jnp.where(first, a, b)
-    out_ref[FR:, :] = jnp.where(first, b, a)
-    total = jnp.sum(a * a + b * b, axis=(0, 1), keepdims=True)
-    sq_ref[...] = jnp.broadcast_to(total, sq_ref.shape)
-
-
-def fc2_call(place, mine, other):
-    whole = lambda a: pl.BlockSpec(a.shape, lambda i, c: (0,) * len(a.shape))
-    shapes = [jax.ShapeDtypeStruct(s, f32) for s in ((2 * FR, D), (8, 128))]
-    return pl.pallas_call(
-        fc2_kernel,
-        grid_spec=pltpu.PrefetchScalarGridSpec(
-            num_scalar_prefetch=1,
-            grid=(1,),
-            in_specs=[whole(mine), whole(other)],
-            out_specs=[whole(a) for a in shapes],
-        ),
-        out_shape=shapes,
-        compiler_params=params(),
-        cost_estimate=cost(6 * FR * D, FR * D * 16),
-    )(place, mine, other)
-
-
-def norm_kernel(g_ref, o_ref, sq_ref, out_ref):
+def norm_kernel(g_ref, o_ref, out_ref):
     g, o = g_ref[...], o_ref[...]
     part = jnp.sum(g * g + o * o, axis=(0, 1), keepdims=True)
     cross = g[:, 4 * DC : PACK] * o[:, 4 * DC : PACK]
     part += 2.0 * jnp.sum(cross, axis=(0, 1), keepdims=True)
-    out_ref[...] = jnp.broadcast_to((part + sq_ref[0:1, 0:1])[None], out_ref.shape)
-
-
-def norm_call(g, o, squares):
+    out_ref[...] = jnp.broadcast_to(part[None], out_ref.shape)
+
+
+def norm_call(g, o):
     return pl.pallas_call(
         norm_kernel,
         out_shape=jax.ShapeDtypeStruct((CHIPS, 8, 128), f32),
         compiler_params=params(),
-        cost_estimate=cost(4 * KR * PACK, 1e6),
-    )(g, o, squares)
+        cost_estimate=cost(4 * KR * WIDE, 1e6),
+    )(g, o)
 
 
 RATES = (D ** (-0.5), max(1, 2 * D // S) ** (-0.5), D ** (-0.5), FF ** (-0.5), RATE_VECTOR)
 
 
-def adam_kernel(place_ref, norm_ref, mine_ref, other_ref, g2_ref, *refs):
+def adam_kernel(place_ref, norm_ref, mine_ref, other_ref, *refs):
     masters, firsts, seconds = refs[0:5], refs[5:10], refs[10:15]
     outs = refs[15:30]
     norm_out, bias_out = refs[30:32]
@@ -949,16 +934,20 @@
         at = slice(PACK + r * DC, PACK + (r + 1) * DC)
         part = exact_dot(g0[:, at], spots_t(0)) + exact_dot(g1[:, at], spots_t(1))
         update(2, (rows, slice(r * D, (r + 1) * D)), part)
-    update(3, (rows, rows), g2_ref[...])
+    for c, g in ((0, g0), (1, g1)):
+        for h in range(2):
+            row = c * FR + h * KR
+            to = PACK + FC + h * D
+            update(3, (slice(row, row + KR), rows), g[:, to : to + D])
     vec = (g0 + g1)[:, 4 * DC : 4 * DC + 128]
     vec = jnp.concatenate([vec, jnp.zeros((16 - KR, 128), f32)], axis=0).T[:16, :KR]
     update(4, (rows, rows), vec[: masters[4].shape[0], :])
     bias_out[...] = vec[7:8, :] * clip
 
 
-def adam_call(place, norm, mine, other, g2, masters, firsts, seconds):
+def adam_call(place, norm, mine, other, masters, firsts, seconds):
     whole = lambda a: pl.BlockSpec(a.shape, lambda i, c: (0,) * len(a.shape))
-    args = [norm, mine, other, g2, *masters, *firsts, *seconds]
+    args = [norm, mine, other, *masters, *firsts, *seconds]
     shapes = [jax.ShapeDtypeStruct(m.shape, f32) for m in masters for _ in range(3)]
     shapes += [jax.ShapeDtypeStruct((1, 128), f32), jax.ShapeDtypeStruct((1, KR), f32)]
     return pl.pallas_call(
@@ -1012,11 +1001,8 @@
     def line_sum(whole):
         return lax.psum_scatter(whole, BOTH, scatter_dimension=0, axis_index_groups=lines(), tiled=True)
 
-    fc2_b = w_fc2.astype(bf16)
-    share_fc2 = jnp.where(first_core, fc2_b[:FR], fc2_b[FR:])
     me = jnp.stack([core, along]).astype(jnp.int32)
-    shares = share_call(me, w_qkv, vectors)
-    shares, share_fc2 = lax.optimization_barrier((shares, share_fc2))
+    shares, share_fc2 = share_call(me, w_qkv, vectors, w_fc2)
     full_fc2 = lax.all_gather(share_fc2, "dp", axis=0, tiled=True)
     fc1_b = w_fc1.astype(bf16).reshape(KR, CHIPS, CORES, FR)
     share_fc1 = jnp.where(first_core, fc1_b[:, :, 0], fc1_b[:, :, 1]).reshape(KR, FC)
@@ -1040,11 +1026,9 @@
     place = jnp.concatenate([jnp.stack([core, along]).astype(jnp.int32), counts0, counts1])
 
     quarter = plane_swap(shares).reshape(QUARTER, 3 * DC + 128)
-    quarter, share, ints, x_other, cot_other = lax.optimization_barrier(
-        (quarter, share, ints, x_other, cot_other)
-    )
+    quarter, share, x_other, cot_other = lax.optimization_barrier((quarter, share, x_other, cot_other))
     qkv_pieces = along_line(quarter)
-    share, qkv_pieces[1] = lax.optimization_barrier((share, qkv_pieces[1]))
+    share, qkv_pieces = lax.optimization_barrier((share, qkv_pieces))
     quarter = plane_swap(share).reshape(QUARTER, FC + D)
 
     vec, h1t, cosine, sine, q, k, v, b1, pos = qkv_call(place, x_own, x_other, ints, qkv_pieces)
@@ -1072,27 +1056,19 @@
     )
     gh1_other = swap(gh1_part)
 
-    got_fc2 = plane_swap(sum_fc2.reshape(PLANE, FR, D))
     parts = [gw[0]] + [shift(gw[d], d) for d in range(1, SIDE)]
-    got_fc2, sum_fc1 = lax.optimization_barrier((got_fc2, sum_fc1))
-    g_fc2 = sum_call(got_fc2)
-    g2, squares = fc2_call(place, g_fc2, swap(g_fc2))
-    got = plane_swap(pack_call(parts, sum_fc1))
-    got, g2, squares = lax.optimization_barrier((got, g2, squares))
+    got = plane_swap(pack_call(parts, sum_fc1, sum_fc2))
+    gt, mixed = last_call(x_own, ga, gh1, gh1_other, after, mlp, mlp_other, vec)
+    got, gt, mixed = lax.optimization_barrier((got, gt, mixed))
     grads = sum_call(got)
 
     grads_other = swap(grads)
-    squares = norm_call(grads, grads_other, squares)
-    squares, gh1 = lax.optimization_barrier((squares, gh1))
-    norms = lax.all_to_all(squares, "dp", 0, 0)
-    gt, mixed = last_call(x_own, ga, gh1, gh1_other, after, mlp, mlp_other, vec)
-    norms, gt, mixed = lax.optimization_barrier((norms, gt, mixed))
+    norms = lax.all_to_all(norm_call(grads, grads_other), "dp", 0, 0)
     *updates, grad_norm, bias_proj_grad = adam_call(
         place,
         norms,
         grads,
         grads_other,
-        g2,
         (w_qkv, w_proj, w_fc1, w_fc2, vectors),
         (m_qkv, m_proj, m_fc1, m_fc2, m_vectors),
         (v_qkv, v_proj, v_fc1, v_fc2, v_vectors),

time: 297 us -> 304 us (1.024)
  blocking collectives: 0 us -> 18.5 us
  waiting for transfers between devices: 74.2 us -> 92.6 us
  starting transfers between devices: 50.1 us -> 33.6 us
  local copies, waits for them, and re-layouts: 13.7 us -> 7.77 us
    ppermute x9, waiting for transfers between devices: 29.3 us -> 56.3 us  [shift(): return lax.ppermute(value, BOTH, pairs)]
    all_to_all x0 -> x1, blocking collectives: none -> 18.5 us  [local(): norms = lax.all_to_all(norm_call(grads, grads_other), 'dp', 0, 0)]
    all_to_all x1 -> x0, starting transfers between devices: 8.42 us -> none  [local(): norms = lax.all_to_all(squares, 'dp', 0, 0)]
    all_to_all x4 -> x3, waiting for transfers between devices: 38.3 us -> 30.5 us  [plane_swap(): return lax.all_to_all(value, BOTH, 0, 0, axis_index_groups=planes())]
    ppermute x9, starting transfers between devices: 15.6 us -> 10 us  [shift(): return lax.ppermute(value, BOTH, pairs)]
    unnamed x46 -> x42, local copies, waits for them, and re-layouts: 8.86 us -> 4.38 us
    all_to_all x4 -> x3, starting transfers between devices: 23.9 us -> 19.5 us  [plane_swap(): return lax.all_to_all(value, BOTH, 0, 0, axis_index_groups=planes())]
    all_to_all x1 -> x0, waiting for transfers between devices: 3.18 us -> none  [local(): norms = lax.all_to_all(squares, 'dp', 0, 0)]
  transfers between devices with their start and end apart: 26 -> 23, of which waited for: 13 -> 13; matrix products, arithmetic and copies ran while one was open for 3% -> 2% of each run, Pallas kernels for 36% -> 28%
where the time goes in v2:
time: 304 us; the launch traced here: 299 us
  Pallas kernels  128 us (42%)
  waiting for transfers between devices  92.6 us (30%)
  starting transfers between devices  33.6 us (11%)
  blocking collectives  18.5 us (6%)
  between operations  16 us (5%)
  local copies, waits for them, and re-layouts  7.77 us (3%)
  other arithmetic  3.41 us (1%)
    ppermute x9, waiting for transfers between devices, shift(): return lax.ppermute(value, BOTH, pairs)  56.3 us
    all_to_all x3, waiting for transfers between devices, plane_swap(): return lax.all_to_all(value, BOTH, 0, 0, axis_index_groups=planes())  30.5 us
    pallas_call x1, Pallas kernels, attn_bwd_call(): pl.pallas_call(attn_bwd_kernel, grid_spec=pltpu.PrefetchScalarGridSpec(nu...  28.1 us
    all_to_all x3, starting transfers between devices, plane_swap(): return lax.all_to_all(value, BOTH, 0, 0, axis_index_groups=planes())  19.5 us
    pallas_call x1, Pallas kernels, mlp_call(): pl.pallas_call(mlp_kernel, grid_spec=pltpu.PrefetchScalarGridSpec(num_sca...  18.7 us
    all_to_all x1, blocking collectives, local(): norms = lax.all_to_all(norm_call(grads, grads_other), 'dp', 0, 0)  18.5 us
    pallas_call x1, Pallas kernels, qkv_call(): pl.pallas_call(qkv_kernel, grid_spec=pltpu.PrefetchScalarGridSpec(num_sca...  14 us
    pallas_call x1, Pallas kernels, mid_call(): pl.pallas_call(mid_kernel, grid_spec=pltpu.PrefetchScalarGridSpec(num_sca...  12.6 us
  transfers between devices with their start and end apart: 23, of which 13 were waited for; matrix products, arithmetic and copies ran while one was open for 2% of the time, Pallas kernels for 28%

profile of v2, /device:TPU:0, one launch (start us, length us, event | category | flops | bytes accessed | tf_op | source)
XLA Modules:
  0.0 299.3 jit_solution(6496307209985244475)
XLA Ops:
  7.9 2.6 shard_map.339
  11.1 8.1 %all-to-all-start = ((bf16[16,12,1280]{2,1,0:T(8,128)(2,1)}), bf16[16,12,1280]{2,1,0:T(8,128)(2,1)S(1)}, u32[]{:S(2)}, u32[]{:S(2)}) async-start(bf16[16,12,1280]{2,1,0:T(8,128)(2,1)} %get-tuple-element.95), calls=%async_computation | async-start | bytes 1310720 | tf_op jit(solution)/shard_map/all_to_all | solution.py:74
  19.9 1.4 fusion
  21.6 9.4 %all-to-all-done = bf16[16,12,1280]{2,1,0:T(8,128)(2,1)S(1)} async-done(((bf16[16,12,1280]{2,1,0:T(8,128)(2,1)}), bf16[16,12,1280]{2,1,0:T(8,128)(2,1)S(1)}, u32[]{:S(2)}, u32[]{:S(2)}) %all-to-all-start) | async-done | bytes 491552 | tf_op jit(solution)/shard_map/all_to_all | solution.py:74
  31.2 1.1 broadcast_in_dim.10
  32.3 1.8 collective-permute-start.5
  34.2 0.9 collective-permute-start.4
  35.1 0.7 collective-permute-start.3
  35.9 9.9 %collective-permute-done.5.w3.v3 = bf16[192,1280]{1,0:T(8,128)(2,1)S(1)} collective-permute-done((bf16[192,1280]{1,0:T(8,128)(2,1)S(1)}, bf16[192,1280]{1,0:T(8,128)(2,1)S(1)}, u32[]{:S(2)}, u32[]{:S(2)}) %collective-permute-start.5) | collective-permute-done | bytes 491552 | tf_op jit(solution)/shard_map/ppermute | solution.py:70
  45.9 4.0 %collective-permute-done.3.w1.v1 = bf16[192,1280]{1,0:T(8,128)(2,1)} collective-permute-done((bf16[192,1280]{1,0:T(8,128)(2,1)S(1)}, bf16[192,1280]{1,0:T(8,128)(2,1)}, u32[]{:S(2)}, u32[]{:S(2)}) %collective-permute-start.3) | collective-permute-done | bytes 491552 | tf_op jit(solution)/shard_map/ppermute | solution.py:70
  49.9 5.3 %all-to-all-start.1 = ((bf16[16,12,2304]{2,1,0:T(8,128)(2,1)}), bf16[16,12,2304]{2,1,0:T(8,128)(2,1)S(1)}, u32[]{:S(2)}, u32[]{:S(2)}) async-start(bf16[16,12,2304]{2,1,0:T(8,128)(2,1)} %broadcast_in_dim.10), calls=%async_computation.1 | async-start | bytes 2359296 | tf_op jit(solution)/shard_map/all_to_all | solution.py:74
  56.0 0.7 collective-permute-done
  58.5 0.7 pad_add_fusion.2.place_ref
  59.8 14.0 %shard_map.340 = (f32[16,768]{1,0:T(8,128)}, bf16[2,768,576]{2,1,0:T(8,128)(2,1)}, f32[1152,384]{1,0:T(8,128)}, f32[1152,384]{1,0:T(8,128)}, bf16[1152,384]{1,0:...) custom-call(s32[5]{0:T(128)} %pad_add_fusion.2.place_ref, ...), custom_call_target="tpu_custom_call" | custom-call | flops 2064973824 | bytes 13271040 | tf_op jit(solution)/shard_map/pallas_call | solution.py:319
  74.0 0.7 collective-permute-start.7
  74.7 1.4 collective-permute-start.6
  76.1 11.3 %shard_map.341 = (bf16[2,576,384]{2,1,0:T(8,128)(2,1)}, bf16[6,2,208,208]{3,2,1,0:T(8,128)(2,1)}, bf16[6,576,576]{2,1,0:T(8,128)(2,1)}) custom-call(s32[5]{0:T(128)} %pad_add_fusion.2.place_ref, bf16[2,576,384]{2,1,0:T(8,128)(2,1)} %bitcast.27, bf16[2,576,384]{2,1,0:T(8,128)(2,1)} %bitcast.31, bf16[2,576,384]{2,1,0:T(8,128)(2,1)} %bitcast.35, ...), custom_call_target="tpu_custom_call" | custom-call | flops 1285029888 | bytes 12000000 | tf_op jit(solution)/shard_map/pallas_call | solution.py:392
  87.5 6.0 %collective-permute-done.7.w3.w13.y3 = bf16[192,2304]{1,0:T(8,128)(2,1)S(1)} collective-permute-done((bf16[192,2304]{1,0:T(8,128)(2,1)S(1)}, bf16[192,2304]{1,0:T(8,128)(2,1)S(1)}, u32[]{:S(2)}, u32[]{:S(2)}) %collective-permute-start.7) | collective-permute-done | bytes 884768 | tf_op jit(solution)/shard_map/ppermute | solution.py:70
  93.5 1.8 collective-permute-done.6.w1.w11.y1
  95.3 1.5 collective-permute-start.8
  96.8 0.9 collective-permute-start.9
  97.6 3.6 %shard_map.342.gy_ref = bf16[1152,768]{1,0:T(8,128)(2,1)} custom-call(s32[5]{0:T(128)} %pad_add_fusion.2.place_ref, bf16[576,768]{1,0:T(8,128)(2,1)} %bitcast.53, bf16[576,768]{1,0:T(8,128)(2,1)} %copy-done.10), custom_call_target="tpu_custom_call" | custom-call | flops 3538944 | bytes 3538944 | tf_op jit(solution)/shard_map/pallas_call | solution.py:245
  101.2 10.1 %collective-permute-done.9.w2.w12.y2 = bf16[192,2304]{1,0:T(8,128)(2,1)S(1)} collective-permute-done((bf16[192,2304]{1,0:T(8,128)(2,1)S(1)}, bf16[192,2304]{1,0:T(8,128)(2,1)S(1)}, u32[]{:S(2)}, u32[]{:S(2)}) %collective-permute-start.9) | collective-permute-done | bytes 884768 | tf_op jit(solution)/shard_map/ppermute | solution.py:70
  111.3 0.9 copy-done.6
  112.2 8.8 %shard_map.343 = (f32[576,768]{1,0:T(8,128)}, f32[1152,768]{1,0:T(8,128)}, f32[1152,8]{1,0:T(8,128)}, bf16[1152,768]{1,0:T(8,128)(2,1)}) custom-call(s32[5]{0:T(128)} %pad_add_fusion.2.place_ref, bf16[2,576,384]{2,1,0:T(8,128)(2,1)} %get-tuple-element.112.mine_ref.o0.o1, bf16[2,576,384]{2,1,0:T(8,128)(2,1)} %copy-done.5, bf16[576,768]{1,0:T(8,128)(2,1)} %bitcast.41, ...), custom_call_target="tpu_custom_call" | custom-call | flops 1358954496 | bytes 10027008 | tf_op jit(solution)/shard_map/pallas_call | solution.py:440
  121.1 18.7 %shard_map.344 = (f32[576,768]{1,0:T(8,128)}, f32[576,768]{1,0:T(8,128)}, bf16[1152,768]{1,0:T(8,128)(2,1)}, bf16[1152,1536]{1,0:T(8,128)(2,1)}, bf16[1152,1536]{1,0:T(8,128)(2,1)}, /*index=5*/f32[1,1536]{1,0:T(1,128)}) custom-call(s32[5]{0:T(128)} %pad_add_fusion.2.place_ref, bf16[1152,768]{1,0:T(8,128)(2,1)} %get-tuple-element.124.h2_ref, ...), custom_call_target="tpu_custom_call" | custom-call | flops 10871635968 | bytes 30000000 | tf_op jit(solution)/shard_map/pallas_call | solution.py:514
  139.8 7.6 %shard_map.345 = bf16[1536,768]{1,0:T(8,128)(2,1)} custom-call(s32[5]{0:T(128)} %pad_add_fusion.2.place_ref, bf16[1152,1536]{1,0:T(8,128)(2,1)} %get-tuple-element.132.act_ref, bf16[1152,768]{1,0:T(8,128)(2,1)} %shard_map.342.gy_ref), custom_call_target="tpu_custom_call" | custom-call | flops 2717908992 | bytes 7667712 | tf_op jit(solution)/shard_map/pallas_call | solution.py:562
  147.4 1.3 copy-done.8
  148.6 12.6 %shard_map.346 = (bf16[768,1536]{1,0:T(8,128)(2,1)}, f32[576,768]{1,0:T(8,128)}, bf16[1152,768]{1,0:T(8,128)(2,1)}, f32[8,768]{1,0:T(8,128)}) custom-call(s32[5]{0:T(128)} %pad_add_fusion.2.place_ref, bf16[1152,768]{1,0:T(8,128)(2,1)} %get-tuple-element.124.h2_ref, bf16[1152,1536]{1,0:T(8,128)(2,1)} %get-tuple-element.128.gup_ref, ...), custom_call_target="tpu_custom_call" | custom-call | flops 2717908992 | bytes 21823488 | tf_op jit(solution)/shard_map/pallas_call | solution.py:613
  162.0 28.1 %shard_map.347 = (bf16[192,1664]{1,0:T(8,128)(2,1)}, bf16[192,1664]{1,0:T(8,128)(2,1)}, bf16[192,1664]{1,0:T(8,128)(2,1)}, bf16[192,1664]{1,0:T(8,128)(2,1)}, f32[576,768]{1,0:T(8,128)}, /*index=5*/f32[576,768]{1,0:T(8,128)}) custom-call(s32[5]{0:T(128)} %pad_add_fusion.2.place_ref, bf16[2,576,384]{2,1,0:T(8,128)(2,1)} %bitcast.29, ...), custom_call_target="tpu_custom_call" | custom-call | flops 7983857664 | bytes 36000000 | tf_op jit(solution)/shard_map/pallas_call | solution.py:780
  190.2 2.0 collective-permute-start.12
  192.3 1.4 collective-permute-start.13
  193.7 1.1 collective-permute-start.15
  194.8 12.9 %collective-permute-done.11.q1 = bf16[192,1664]{1,0:T(8,128)(2,1)S(1)} collective-permute-done((bf16[192,1664]{1,0:T(8,128)(2,1)}, bf16[192,1664]{1,0:T(8,128)(2,1)S(1)}, u32[]{:S(2)}, u32[]{:S(2)}) %collective-permute-start.11) | collective-permute-done | bytes 639008 | tf_op jit(solution)/shard_map/ppermute | solution.py:70
  207.7 7.7 %collective-permute-done.12.q2 = bf16[192,1664]{1,0:T(8,128)(2,1)S(1)} collective-permute-done((bf16[192,1664]{1,0:T(8,128)(2,1)}, bf16[192,1664]{1,0:T(8,128)(2,1)S(1)}, u32[]{:S(2)}, u32[]{:S(2)}) %collective-permute-start.12) | collective-permute-done | bytes 639008 | tf_op jit(solution)/shard_map/ppermute | solution.py:70
  215.4 3.8 %collective-permute-done.13.q3 = bf16[192,1664]{1,0:T(8,128)(2,1)S(1)} collective-permute-done((bf16[192,1664]{1,0:T(8,128)(2,1)}, bf16[192,1664]{1,0:T(8,128)(2,1)S(1)}, u32[]{:S(2)}, u32[]{:S(2)}) %collective-permute-start.13) | collective-permute-done | bytes 639008 | tf_op jit(solution)/shard_map/ppermute | solution.py:70
  219.2 2.9 reduce-scatter.5.cloned.1.call-done.f2_ref
  222.0 3.9 %shard_map.348 = bf16[16,12,4736]{2,1,0:T(8,128)(2,1)} custom-call(bf16[192,1664]{1,0:T(8,128)(2,1)} %get-tuple-element.137.q0, bf16[192,1664]{1,0:T(8,128)(2,1)} %copy-done.12, bf16[192,1664]{1,0:T(8,128)(2,1)} %copy-done.13, bf16[192,1664]{1,0:T(8,128)(2,1)} %copy-done.14, bf16[192,1536]{1,0:T(8,128)(2,1)} %reduce-scatter.3.cloned.1.call-done.f1_ref, ...), custom_call_target="tpu_custom_call" | custom-call | flops 1277952 | bytes 4472832 | tf_op jit(solution)/shard_map/pallas_call | solution.py:856
  225.9 6.1 %all-to-all-start.2 = ((bf16[16,12,4736]{2,1,0:T(8,128)(2,1)}), bf16[16,12,4736]{2,1,0:T(8,128)(2,1)S(1)}, u32[]{:S(2)}, u32[]{:S(2)}) async-start(bf16[16,12,4736]{2,1,0:T(8,128)(2,1)} %shard_map.348), calls=%async_computation.4 | async-start | bytes 4849664 | tf_op jit(solution)/shard_map/all_to_all | solution.py:74
  232.1 6.1 %shard_map.349 = (f32[576,768]{1,0:T(8,128)}, bf16[576,768]{1,0:T(8,128)(2,1)}) custom-call(bf16[576,768]{1,0:T(8,128)(2,1)} %bitcast.43, f32[576,768]{1,0:T(8,128)} %get-tuple-element.143.ga_ref, f32[576,768]{1,0:T(8,128)} %get-tuple-element.144.gh_ref, f32[576,768]{1,0:T(8,128)} %collective-permute-done.14.other_ref, ...), custom_call_target="tpu_custom_call" | custom-call | flops 13271040 | bytes 12386304 | tf_op jit(solution)/shard_map/pallas_call | solution.py:828
  238.1 21.1 %all-to-all-done.2.in_ref = bf16[16,12,4736]{2,1,0:T(8,128)(2,1)S(1)} async-done(((bf16[16,12,4736]{2,1,0:T(8,128)(2,1)}), bf16[16,12,4736]{2,1,0:T(8,128)(2,1)S(1)}, u32[]{:S(2)}, u32[]{:S(2)}) %all-to-all-start.2) | async-done | bytes 1818656 | tf_op jit(solution)/shard_map/all_to_all | solution.py:74
  259.3 1.4 copy-done
  260.7 2.7 shard_map.350.g_ref.mine_ref
  263.7 1.8 collective-permute-done.16.o_ref.other_ref
  265.5 0.7 copy-done.9
  266.2 2.0 shard_map.351
  268.1 18.5 %all_to_all.20.norm_ref = f32[64,8,128]{2,1,0:T(8,128)} all-to-all(f32[64,8,128]{2,1,0:T(8,128)} %shard_map.351), channel_id=1, replica_groups=mesh['grp'=2,'dp'=64] {'dp'}, dimensions={0} | all-to-all | bytes 524288 | tf_op jit(solution)/shard_map/all_to_all | solution.py:1066
  286.6 5.7 %shard_map.352 = (f32[12,2304]{1,0:T(8,128)}, f32[12,2304]{1,0:T(8,128)}, f32[12,2304]{1,0:T(8,128)}, f32[12,768]{1,0:T(8,128)}, f32[12,768]{1,0:T(8,128)}, /*in...) custom-call(s32[5]{0:T(128)} %pad_add_fusion.2.place_ref, ...), custom_call_target="tpu_custom_call" | custom-call | flops 2211840 | bytes 3000000 | tf_op jit(solution)/shard_map/pallas_call | solution.py:953
  (76 shorter events, 5.8 us)
Async XLA Ops:
  7.2 12.0 %copy-start.11 = (f32[12,3072]{1,0:T(8,128)S(1)}, f32[12,3072]{1,0:T(8,128)}, u32[]{:S(2)}) copy-start(f32[12,3072]{1,0:T(8,128)} %refs_2_.1) | copy-start | bytes 442372
  7.2 14.1 %copy-start.17 = (f32[12,768]{1,0:T(8,128)S(1)}, f32[12,768]{1,0:T(8,128)}, u32[]{:S(2)}) copy-start(f32[12,768]{1,0:T(8,128)} %refs_1_.1) | copy-start | bytes 110596
  7.2 113.8 %all-gather.2.cloned.1.call-start = ((), (), s32[]{:S(2)}) async-start(), calls=%async_computation.6 | async-start | bytes 2396160 | tf_op jit(solution)/shard_map/all_gather | solution.py:1006
  10.5 20.7 %collective-permute-start.1 = (bf16[576,768]{1,0:T(8,128)(2,1)}, bf16[576,768]{1,0:T(8,128)(2,1)S(1)}, u32[]{:S(2)}, u32[]{:S(2)}) collective-permute-start(bf16[576,768]{1,0:T(8,128)(2,1)} %bitcast.39), channel_id=1, source_target_pairs={{0,64},{64,0},{1,65},{65,1},{2,66},{66,2},{3,67},{67,3},{4,68},{68... | collective-permute-start | bytes 2654216 | tf_op jit(solution)/shard_map/ppermute | solution.py:996
  10.6 20.6 %collective-permute-start.2 = (bf16[576,768]{1,0:T(8,128)(2,1)}, bf16[576,768]{1,0:T(8,128)(2,1)S(1)}, u32[]{:S(2)}, u32[]{:S(2)}) collective-permute-start(bf16[576,768]{1,0:T(8,128)(2,1)} %bitcast.52), channel_id=1, source_target_pairs={{0,64},{64,0},{1,65},{65,1},{2,66},{66,2},{3,67},{67,3},{4,68},{68... | collective-permute-start | bytes 2654216 | tf_op jit(solution)/shard_map/ppermute | solution.py:996
  11.1 19.9 %all-to-all-start = ((bf16[16,12,1280]{2,1,0:T(8,128)(2,1)}), bf16[16,12,1280]{2,1,0:T(8,128)(2,1)S(1)}, u32[]{:S(2)}, u32[]{:S(2)}) async-start(bf16[16,12,1280]{2,1,0:T(8,128)(2,1)} %get-tuple-element.95), calls=%async_computation | async-start | bytes 1310720 | tf_op jit(solution)/shard_map/all_to_all | solution.py:74
  31.1 18.8 %copy-start.7 = (bf16[192,1280]{1,0:T(8,128)(2,1)}, bf16[192,1280]{1,0:T(8,128)(2,1)S(1)}, u32[]{:S(2)}) copy-start(bf16[192,1280]{1,0:T(8,128)(2,1)S(1)} %reshape.108.w0.v0) | copy-start | bytes 1474564
  31.1 24.1 %copy-start.18 = (s32[1,1,576]{2,1,0:T(1,128)S(1)}, s32[1,1,576]{2,1,0:T(1,128)}, u32[]{:S(2)}) copy-start(s32[1,1,576]{2,1,0:T(1,128)} %param.24) | copy-start | bytes 6916
  31.1 24.1 %copy-start.19 = (s32[1,1,576]{2,1,0:T(1,128)S(1)}, s32[1,1,576]{2,1,0:T(1,128)}, u32[]{:S(2)}) copy-start(s32[1,1,576]{2,1,0:T(1,128)} %param.23) | copy-start | bytes 6916
  31.1 24.1 %copy-start.20 = (s32[1,1,2]{2,1,0:T(1,128)S(1)}, s32[1,1,2]{2,1,0:T(1,128)}, u32[]{:S(2)}) copy-start(s32[1,1,2]{2,1,0:T(1,128)} %param.22) | copy-start | bytes 28
  31.2 18.7 %copy-start.2 = (bf16[576,768]{1,0:T(8,128)(2,1)}, bf16[576,768]{1,0:T(8,128)(2,1)S(1)}, u32[]{:S(2)}) copy-start(bf16[576,768]{1,0:T(8,128)(2,1)S(1)} %collective-permute-done.1.xo_ref) | copy-start | bytes 2654212
  31.2 18.7 %copy-start.10 = (bf16[576,768]{1,0:T(8,128)(2,1)}, bf16[576,768]{1,0:T(8,128)(2,1)S(1)}, u32[]{:S(2)}) copy-start(bf16[576,768]{1,0:T(8,128)(2,1)S(1)} %collective-permute-done.2.co_ref) | copy-start | bytes 2654212
  32.3 13.5 %collective-permute-start.5 = (bf16[192,1280]{1,0:T(8,128)(2,1)S(1)}, bf16[192,1280]{1,0:T(8,128)(2,1)S(1)}, u32[]{:S(2)}, u32[]{:S(2)}) collective-permute-start(bf16[192,1280]{1,0:T(8,128)(2,1)S(1)} %reshape.108.w0.v0), channel_id=1, source_target_pairs={{0,48},{16,0},{32,16},{48,32},{1,49},{17,1},{33,17},{49,33},{2,50}... | collective-permute-start | bytes 1474568 | tf_op jit(solution)/shard_map/ppermute | solution.py:70
  34.2 11.7 %collective-permute-start.4 = (bf16[192,1280]{1,0:T(8,128)(2,1)S(1)}, bf16[192,1280]{1,0:T(8,128)(2,1)S(1)}, u32[]{:S(2)}, u32[]{:S(2)}) collective-permute-start(bf16[192,1280]{1,0:T(8,128)(2,1)S(1)} %reshape.108.w0.v0), channel_id=1, source_target_pairs={{0,32},{16,48},{32,0},{48,16},{1,33},{17,49},{33,1},{49,17},{2,34}... | collective-permute-start | bytes 1474568 | tf_op jit(solution)/shard_map/ppermute | solution.py:70
  35.1 14.8 %collective-permute-start.3 = (bf16[192,1280]{1,0:T(8,128)(2,1)S(1)}, bf16[192,1280]{1,0:T(8,128)(2,1)}, u32[]{:S(2)}, u32[]{:S(2)}) collective-permute-start(bf16[192,1280]{1,0:T(8,128)(2,1)S(1)} %reshape.108.w0.v0), channel_id=1, source_target_pairs={{0,16},{16,32},{32,48},{48,0},{1,17},{17,33},{33,49},{49,1},{2,18}... | collective-permute-start | bytes 1474568 | tf_op jit(solution)/shard_map/ppermute | solution.py:70
  45.8 4.0 %copy-start.15 = (bf16[192,1280]{1,0:T(8,128)(2,1)}, bf16[192,1280]{1,0:T(8,128)(2,1)S(1)}, u32[]{:S(2)}) copy-start(bf16[192,1280]{1,0:T(8,128)(2,1)S(1)} %collective-permute-done.5.w3.v3) | copy-start | bytes 1474564
  45.9 4.0 %copy-start.16 = (bf16[192,1280]{1,0:T(8,128)(2,1)}, bf16[192,1280]{1,0:T(8,128)(2,1)S(1)}, u32[]{:S(2)}) copy-start(bf16[192,1280]{1,0:T(8,128)(2,1)S(1)} %collective-permute-done.4.w2.v2) | copy-start | bytes 1474564
  49.9 23.9 %all-to-all-start.1 = ((bf16[16,12,2304]{2,1,0:T(8,128)(2,1)}), bf16[16,12,2304]{2,1,0:T(8,128)(2,1)S(1)}, u32[]{:S(2)}, u32[]{:S(2)}) async-start(bf16[16,12,2304]{2,1,0:T(8,128)(2,1)} %broadcast_in_dim.10), calls=%async_computation.1 | async-start | bytes 2359296 | tf_op jit(solution)/shard_map/all_to_all | solution.py:74
  55.2 164.0 %reduce-scatter.3.cloned.1.call-start = ((), (), s32[]{:S(2)}) async-start(), calls=%async_computation.7 | async-start | bytes 2949120 | tf_op jit(solution)/shard_map/reduce_scatter | solution.py:1002
  55.3 1.4 collective-permute-start
  74.0 22.7 %copy-start.1 = (bf16[192,2304]{1,0:T(8,128)(2,1)}, bf16[192,2304]{1,0:T(8,128)(2,1)S(1)}, u32[]{:S(2)}) copy-start(bf16[192,2304]{1,0:T(8,128)(2,1)S(1)} %reshape.111.w0.w10.y0) | copy-start | bytes 2654212
  74.0 19.4 %collective-permute-start.7 = (bf16[192,2304]{1,0:T(8,128)(2,1)S(1)}, bf16[192,2304]{1,0:T(8,128)(2,1)S(1)}, u32[]{:S(2)}, u32[]{:S(2)}) collective-permute-start(bf16[192,2304]{1,0:T(8,128)(2,1)S(1)} %reshape.111.w0.w10.y0), channel_id=1, source_target_pairs={{0,48},{16,0},{32,16},{48,32},{1,49},{17,1},{33,17},{49,33},{2,50}... | collective-permute-start | bytes 2654216 | tf_op jit(solution)/shard_map/ppermute | solution.py:70
  74.7 20.6 %collective-permute-start.6 = (bf16[192,2304]{1,0:T(8,128)(2,1)S(1)}, bf16[192,2304]{1,0:T(8,128)(2,1)S(1)}, u32[]{:S(2)}, u32[]{:S(2)}) collective-permute-start(bf16[192,2304]{1,0:T(8,128)(2,1)S(1)} %reshape.111.w0.w10.y0), channel_id=1, source_target_pairs={{0,16},{16,32},{32,48},{48,0},{1,17},{17,33},{33,49},{49,1},{2,18}... | collective-permute-start | bytes 2654216 | tf_op jit(solution)/shard_map/ppermute | solution.py:70
  93.5 7.7 %copy-start.3 = (bf16[192,2304]{1,0:T(8,128)(2,1)}, bf16[192,2304]{1,0:T(8,128)(2,1)S(1)}, u32[]{:S(2)}) copy-start(bf16[192,2304]{1,0:T(8,128)(2,1)S(1)} %collective-permute-done.7.w3.w13.y3) | copy-start | bytes 2654212
  95.3 5.9 %copy-start.4 = (bf16[192,2304]{1,0:T(8,128)(2,1)}, bf16[192,2304]{1,0:T(8,128)(2,1)S(1)}, u32[]{:S(2)}) copy-start(bf16[192,2304]{1,0:T(8,128)(2,1)S(1)} %collective-permute-done.6.w1.w11.y1) | copy-start | bytes 2654212
  95.3 5.9 %collective-permute-start.8 = (bf16[2,576,384]{2,1,0:T(8,128)(2,1)}, bf16[2,576,384]{2,1,0:T(8,128)(2,1)S(1)}, u32[]{:S(2)}, u32[]{:S(2)}) collective-permute-start(bf16[2,576,384]{2,1,0:T(8,128)(2,1)} %get-tuple-element.112.mine_ref.o0.o1), channel_id=1, source_target_pairs={{0,64},{64,0},{1,65},{65,1},{2,66},{66,2},{3,67},{67,3},{4,68},{68... | collective-permute-start | bytes 2654216 | tf_op jit(solution)/shard_map/ppermute | solution.py:996
  96.8 14.5 %collective-permute-start.9 = (bf16[192,2304]{1,0:T(8,128)(2,1)S(1)}, bf16[192,2304]{1,0:T(8,128)(2,1)S(1)}, u32[]{:S(2)}, u32[]{:S(2)}) collective-permute-start(bf16[192,2304]{1,0:T(8,128)(2,1)S(1)} %reshape.111.w0.w10.y0), channel_id=1, source_target_pairs={{0,32},{16,48},{32,0},{48,16},{1,33},{17,49},{33,1},{49,17},{2,34}... | collective-permute-start | bytes 2654216 | tf_op jit(solution)/shard_map/ppermute | solution.py:70
  101.2 10.1 %copy-start.5 = (bf16[2,576,384]{2,1,0:T(8,128)(2,1)}, bf16[2,576,384]{2,1,0:T(8,128)(2,1)S(1)}, u32[]{:S(2)}) copy-start(bf16[2,576,384]{2,1,0:T(8,128)(2,1)S(1)} %collective-permute-done.8.other_ref) | copy-start | bytes 2654212
  111.3 0.9 copy-start.6
  139.7 7.7 %collective-permute-start.10 = (bf16[1152,768]{1,0:T(8,128)(2,1)}, bf16[1152,768]{1,0:T(8,128)(2,1)S(1)}, u32[]{:S(2)}, u32[]{:S(2)}) collective-permute-start(bf16[1152,768]{1,0:T(8,128)(2,1)} %get-tuple-element.131.gh2_ref), channel_id=1, source_target_pairs={{0,64},{64,0},{1,65},{65,1},{2,66},{66,2},{3,67},{67,3},{4,68},{68... | collective-permute-start | bytes 5308424 | tf_op jit(solution)/shard_map/ppermute | solution.py:996
  147.4 1.3 copy-start.8
  161.3 60.7 %reduce-scatter.5.cloned.1.call-start = ((), (), s32[]{:S(2)}) async-start(), calls=%async_computation.8 | async-start | bytes 2949120 | tf_op jit(solution)/shard_map/reduce_scatter | solution.py:1002
  190.2 17.6 %collective-permute-start.11 = (bf16[192,1664]{1,0:T(8,128)(2,1)}, bf16[192,1664]{1,0:T(8,128)(2,1)S(1)}, u32[]{:S(2)}, u32[]{:S(2)}) collective-permute-start(bf16[192,1664]{1,0:T(8,128)(2,1)} %get-tuple-element.138), channel_id=1, source_target_pairs={{0,16},{16,32},{32,48},{48,0},{1,17},{17,33},{33,49},{49,1},{2,18}... | collective-permute-start | bytes 1916936 | tf_op jit(solution)/shard_map/ppermute | solution.py:70
  190.2 25.1 %collective-permute-start.12 = (bf16[192,1664]{1,0:T(8,128)(2,1)}, bf16[192,1664]{1,0:T(8,128)(2,1)S(1)}, u32[]{:S(2)}, u32[]{:S(2)}) collective-permute-start(bf16[192,1664]{1,0:T(8,128)(2,1)} %get-tuple-element.139), channel_id=1, source_target_pairs={{0,32},{16,48},{32,0},{48,16},{1,33},{17,49},{33,1},{49,17},{2,34}... | collective-permute-start | bytes 1916936 | tf_op jit(solution)/shard_map/ppermute | solution.py:70
  192.3 26.9 %collective-permute-start.13 = (bf16[192,1664]{1,0:T(8,128)(2,1)}, bf16[192,1664]{1,0:T(8,128)(2,1)S(1)}, u32[]{:S(2)}, u32[]{:S(2)}) collective-permute-start(bf16[192,1664]{1,0:T(8,128)(2,1)} %get-tuple-element.140), channel_id=1, source_target_pairs={{0,48},{16,0},{32,16},{48,32},{1,49},{17,1},{33,17},{49,33},{2,50}... | collective-permute-start | bytes 1916936 | tf_op jit(solution)/shard_map/ppermute | solution.py:70
  193.7 38.3 %collective-permute-start.15 = (f32[576,768]{1,0:T(8,128)}, f32[576,768]{1,0:T(8,128)}, u32[]{:S(2)}, u32[]{:S(2)}) collective-permute-start(f32[576,768]{1,0:T(8,128)} %get-tuple-element.148), channel_id=1, source_target_pairs={{0,64},{64,0},{1,65},{65,1},{2,66},{66,2},{3,67},{67,3},{4,68},{68... | collective-permute-start | bytes 5308424 | tf_op jit(solution)/shard_map/ppermute | solution.py:996
  194.8 37.3 %collective-permute-start.14 = (f32[576,768]{1,0:T(8,128)}, f32[576,768]{1,0:T(8,128)}, u32[]{:S(2)}, u32[]{:S(2)}) collective-permute-start(f32[576,768]{1,0:T(8,128)} %get-tuple-element.145), channel_id=1, source_target_pairs={{0,64},{64,0},{1,65},{65,1},{2,66},{66,2},{3,67},{67,3},{4,68},{68... | collective-permute-start | bytes 5308424 | tf_op jit(solution)/shard_map/ppermute | solution.py:996
  207.7 14.3 %copy-start.12 = (bf16[192,1664]{1,0:T(8,128)(2,1)}, bf16[192,1664]{1,0:T(8,128)(2,1)S(1)}, u32[]{:S(2)}) copy-start(bf16[192,1664]{1,0:T(8,128)(2,1)S(1)} %collective-permute-done.11.q1) | copy-start | bytes 1916932
  215.4 6.7 %copy-start.13 = (bf16[192,1664]{1,0:T(8,128)(2,1)}, bf16[192,1664]{1,0:T(8,128)(2,1)S(1)}, u32[]{:S(2)}) copy-start(bf16[192,1664]{1,0:T(8,128)(2,1)S(1)} %collective-permute-done.12.q2) | copy-start | bytes 1916932
  219.2 2.9 copy-start.14
  225.9 33.3 %all-to-all-start.2 = ((bf16[16,12,4736]{2,1,0:T(8,128)(2,1)}), bf16[16,12,4736]{2,1,0:T(8,128)(2,1)S(1)}, u32[]{:S(2)}, u32[]{:S(2)}) async-start(bf16[16,12,4736]{2,1,0:T(8,128)(2,1)} %shard_map.348), calls=%async_computation.4 | async-start | bytes 4849664 | tf_op jit(solution)/shard_map/all_to_all | solution.py:74
  259.3 1.4 copy-start
  263.4 2.1 collective-permute-start.16
  265.5 0.7 copy-start.9
Sparse Core Ops, SparseCore 0:
  11.5 83.8 all-gather.1
  161.4 23.2 reduce-scatter.2
  187.1 34.8 reduce-scatter.4

commit v3 on v1

--- a/solution.py
+++ b/solution.py
@@ -195,7 +195,7 @@
     return sine, cosine
 
 
-def share_kernel(place_ref, w_ref, v_ref, out_ref):
+def share_kernel(place_ref, w_ref, v_ref, f_ref, out_ref, fc2_ref):
     core = place_ref[0]
     w = w_ref[...].astype(bf16)
     cols = []
@@ -209,22 +209,29 @@
     share = jnp.concatenate(cols, axis=1)
     for n in range(PLANE):
         out_ref[n] = share
-
-
-def share_call(place, w, vectors):
+    fc2_ref[...] = jnp.where(core == 0, f_ref[:FR, :], f_ref[FR:, :]).astype(bf16)
+
+
+def share_call(place, w, vectors, w_fc2):
     whole = lambda a: pl.BlockSpec(a.shape, lambda i, c: (0, 0))
     return pl.pallas_call(
         share_kernel,
         grid_spec=pltpu.PrefetchScalarGridSpec(
             num_scalar_prefetch=1,
             grid=(1,),
-            in_specs=[whole(w), whole(vectors)],
-            out_specs=pl.BlockSpec((PLANE, KR, 3 * DC + 128), lambda i, c: (0, 0, 0)),
+            in_specs=[whole(w), whole(vectors), whole(w_fc2)],
+            out_specs=[
+                pl.BlockSpec((PLANE, KR, 3 * DC + 128), lambda i, c: (0, 0, 0)),
+                pl.BlockSpec((FR, D), lambda i, c: (0, 0)),
+            ],
         ),
-        out_shape=jax.ShapeDtypeStruct((PLANE, KR, 3 * DC + 128), bf16),
+        out_shape=[
+            jax.ShapeDtypeStruct((PLANE, KR, 3 * DC + 128), bf16),
+            jax.ShapeDtypeStruct((FR, D), bf16),
+        ],
         compiler_params=params(),
         cost_estimate=cost(KR * D * 3, 1e6),
-    )(place, w, vectors)
+    )(place, w, vectors, w_fc2)
 
 
 def gy_kernel(place_ref, c_ref, co_ref, gy_ref):
@@ -1012,16 +1019,17 @@
     def line_sum(whole):
         return lax.psum_scatter(whole, BOTH, scatter_dimension=0, axis_index_groups=lines(), tiled=True)
 
-    fc2_b = w_fc2.astype(bf16)
-    share_fc2 = jnp.where(first_core, fc2_b[:FR], fc2_b[FR:])
     me = jnp.stack([core, along]).astype(jnp.int32)
-    shares = share_call(me, w_qkv, vectors)
-    shares, share_fc2 = lax.optimization_barrier((shares, share_fc2))
+    shares, share_fc2 = share_call(me, w_qkv, vectors, w_fc2)
     full_fc2 = lax.all_gather(share_fc2, "dp", axis=0, tiled=True)
+    quarter = plane_swap(shares).reshape(QUARTER, 3 * DC + 128)
+    qkv_pieces = along_line(quarter)
     fc1_b = w_fc1.astype(bf16).reshape(KR, CHIPS, CORES, FR)
     share_fc1 = jnp.where(first_core, fc1_b[:, :, 0], fc1_b[:, :, 1]).reshape(KR, FC)
     share = jnp.concatenate([share_fc1, w_proj.astype(bf16)], axis=1)
     share = jnp.broadcast_to(share[None], (PLANE,) + share.shape)
+    share, qkv_pieces[1] = lax.optimization_barrier((share, qkv_pieces[1]))
+    quarter = plane_swap(share).reshape(QUARTER, FC + D)
 
     x_own = tokens.reshape(S, D)
     cot_own = cotangent.reshape(S, D)
@@ -1039,21 +1047,12 @@
     counts1 = jnp.where(first_core, ints[1, 2, :1], ints[0, 2, :1])
     place = jnp.concatenate([jnp.stack([core, along]).astype(jnp.int32), counts0, counts1])
 
-    quarter = plane_swap(shares).reshape(QUARTER, 3 * DC + 128)
-    quarter, share, ints, x_other, cot_other = lax.optimization_barrier(
-        (quarter, share, ints, x_other, cot_other)
-    )
-    qkv_pieces = along_line(quarter)
-    share, qkv_pieces[1] = lax.optimization_barrier((share, qkv_pieces[1]))
-    quarter = plane_swap(share).reshape(QUARTER, FC + D)
-
     vec, h1t, cosine, sine, q, k, v, b1, pos = qkv_call(place, x_own, x_other, ints, qkv_pieces)
     q, quarter = lax.optimization_barrier((q, quarter))
     pieces = along_line(quarter)
     mine, p0, p1 = attn_fwd_call(place, q, k, v)
-    mine, pieces[1], pieces[3] = lax.optimization_barrier((mine, pieces[1], pieces[3]))
+    mine, pieces[1], pieces[3], cot_other = lax.optimization_barrier((mine, pieces[1], pieces[3], cot_other))
     other = swap(mine)
-    cot_other, mine = lax.optimization_barrier((cot_other, mine))
     gy = gy_call(place, cot_own, cot_other)
     other, gy = lax.optimization_barrier((other, gy))
     after, n2, r2, h2 = proj_call(place, mine, other, x_own, x_other, pieces, vec)
@@ -1077,16 +1076,14 @@
     got_fc2, sum_fc1 = lax.optimization_barrier((got_fc2, sum_fc1))
     g_fc2 = sum_call(got_fc2)
     g2, squares = fc2_call(place, g_fc2, swap(g_fc2))
-    got = plane_swap(pack_call(parts, sum_fc1))
-    got, g2, squares = lax.optimization_barrier((got, g2, squares))
+    packed, gh1 = lax.optimization_barrier((pack_call(parts, sum_fc1), gh1))
+    got = plane_swap(packed)
+    gt, mixed = last_call(x_own, ga, gh1, gh1_other, after, mlp, mlp_other, vec)
+    got, g2, squares, gt, mixed = lax.optimization_barrier((got, g2, squares, gt, mixed))
     grads = sum_call(got)
 
     grads_other = swap(grads)
-    squares = norm_call(grads, grads_other, squares)
-    squares, gh1 = lax.optimization_barrier((squares, gh1))
-    norms = lax.all_to_all(squares, "dp", 0, 0)
-    gt, mixed = last_call(x_own, ga, gh1, gh1_other, after, mlp, mlp_other, vec)
-    norms, gt, mixed = lax.optimization_barrier((norms, gt, mixed))
+    norms = lax.all_to_all(norm_call(grads, grads_other, squares), "dp", 0, 0)
     *updates, grad_norm, bias_proj_grad = adam_call(
         place,
         norms,

time: 297 us -> 285 us (0.960)
  waiting for transfers between devices: 74.2 us -> 53.6 us
  blocking collectives: 0 us -> 19.9 us
  starting transfers between devices: 50.1 us -> 45.3 us
    all_to_all x0 -> x1, blocking collectives: none -> 19.9 us  [local(): norms = lax.all_to_all(norm_call(grads, grads_other, squares), 'dp', 0, 0)]
    ppermute x9, waiting for transfers between devices: 29.3 us -> 18.5 us  [shift(): return lax.ppermute(value, BOTH, pairs)]
    all_to_all x4, waiting for transfers between devices: 38.3 us -> 28.1 us  [plane_swap(): return lax.all_to_all(value, BOTH, 0, 0, axis_index_groups=planes())]
    all_to_all x1 -> x0, starting transfers between devices: 8.42 us -> none  [local(): norms = lax.all_to_all(squares, 'dp', 0, 0)]
    ppermute x9, starting transfers between devices: 1.85 us -> 8.41 us  [swap(): return lax.ppermute(a, 'grp', [(0, 1), (1, 0)])]
    reduce_scatter x2, waiting for transfers between devices: 0.28 us -> 5.32 us  [line_sum(): lax.psum_scatter(whole, BOTH, scatter_dimension=0, axis_index_groups=line...]
    ppermute x9, starting transfers between devices: 15.6 us -> 12 us  [shift(): return lax.ppermute(value, BOTH, pairs)]
    all_to_all x1 -> x0, waiting for transfers between devices: 3.18 us -> none  [local(): norms = lax.all_to_all(squares, 'dp', 0, 0)]
  transfers between devices with their start and end apart: 26 -> 25, of which waited for: 13 -> 9; matrix products, arithmetic and copies ran while one was open for 3% -> 2% of each run, Pallas kernels for 36% -> 36%
where the time goes in v3:
time: 285 us; the launch traced here: 280 us
  Pallas kernels  131 us (46%)
  waiting for transfers between devices  53.6 us (19%)
  starting transfers between devices  45.3 us (16%)
  blocking collectives  19.9 us (7%)
  between operations  15.7 us (6%)
  local copies, waits for them, and re-layouts  10.8 us (4%)
  other arithmetic  3.42 us (1%)
    pallas_call x1, Pallas kernels, attn_bwd_call(): pl.pallas_call(attn_bwd_kernel, grid_spec=pltpu.PrefetchScalarGridSpec(nu...  28.4 us
    all_to_all x4, waiting for transfers between devices, plane_swap(): return lax.all_to_all(value, BOTH, 0, 0, axis_index_groups=planes())  28.1 us
    all_to_all x4, starting transfers between devices, plane_swap(): return lax.all_to_all(value, BOTH, 0, 0, axis_index_groups=planes())  24.6 us
    all_to_all x1, blocking collectives, local(): norms = lax.all_to_all(norm_call(grads, grads_other, squares), 'dp', 0, 0)  19.9 us
    pallas_call x1, Pallas kernels, mlp_call(): pl.pallas_call(mlp_kernel, grid_spec=pltpu.PrefetchScalarGridSpec(num_sca...  18.7 us
    ppermute x9, waiting for transfers between devices, shift(): return lax.ppermute(value, BOTH, pairs)  18.5 us
    pallas_call x1, Pallas kernels, qkv_call(): pl.pallas_call(qkv_kernel, grid_spec=pltpu.PrefetchScalarGridSpec(num_sca...  14 us
    pallas_call x1, Pallas kernels, mid_call(): pl.pallas_call(mid_kernel, grid_spec=pltpu.PrefetchScalarGridSpec(num_sca...  12.8 us
  transfers between devices with their start and end apart: 25, of which 9 were waited for; matrix products, arithmetic and copies ran while one was open for 2% of the time, Pallas kernels for 36%

profile of v3, /device:TPU:0, one launch (start us, length us, event | category | flops | bytes accessed | tf_op | source)
XLA Modules:
  0.0 280.0 jit_solution(11321287076658717432)
XLA Ops:
  7.9 2.6 shard_map.339
  10.5 8.1 %all-to-all-start = ((bf16[16,12,1280]{2,1,0:T(8,128)(2,1)}), bf16[16,12,1280]{2,1,0:T(8,128)(2,1)S(1)}, u32[]{:S(2)}, u32[]{:S(2)}) async-start(bf16[16,12,1280]{2,1,0:T(8,128)(2,1)} %get-tuple-element.95), calls=%async_computation | async-start | bytes 1310720 | tf_op jit(solution)/shard_map/all_to_all | solution.py:74
  19.5 10.6 %all-to-all-done = bf16[16,12,1280]{2,1,0:T(8,128)(2,1)S(1)} async-done(((bf16[16,12,1280]{2,1,0:T(8,128)(2,1)}), bf16[16,12,1280]{2,1,0:T(8,128)(2,1)S(1)}, u32[]{:S(2)}, u32[]{:S(2)}) %all-to-all-start) | async-done | bytes 491552 | tf_op jit(solution)/shard_map/all_to_all | solution.py:74
  30.2 1.0 collective-permute-start.2
  31.2 1.4 fusion
  32.9 2.4 collective-permute-start.4
  35.4 1.2 collective-permute-start.3
  36.6 4.0 %collective-permute-done.2.w1.v1 = bf16[192,1280]{1,0:T(8,128)(2,1)} collective-permute-done((bf16[192,1280]{1,0:T(8,128)(2,1)S(1)}, bf16[192,1280]{1,0:T(8,128)(2,1)}, u32[]{:S(2)}, u32[]{:S(2)}) %collective-permute-start.2) | collective-permute-done | bytes 491552 | tf_op jit(solution)/shard_map/ppermute | solution.py:70
  40.5 1.1 broadcast_in_dim.10
  41.6 5.0 %all-to-all-start.1 = ((bf16[16,12,2304]{2,1,0:T(8,128)(2,1)}), bf16[16,12,2304]{2,1,0:T(8,128)(2,1)S(1)}, u32[]{:S(2)}, u32[]{:S(2)}) async-start(bf16[16,12,2304]{2,1,0:T(8,128)(2,1)} %broadcast_in_dim.10), calls=%async_computation.1 | async-start | bytes 2359296 | tf_op jit(solution)/shard_map/all_to_all | solution.py:74
  46.8 1.0 collective-permute-start.7
  51.5 0.9 copy-done.2
  52.4 14.0 %shard_map.340 = (f32[16,768]{1,0:T(8,128)}, bf16[2,768,576]{2,1,0:T(8,128)(2,1)}, f32[1152,384]{1,0:T(8,128)}, f32[1152,384]{1,0:T(8,128)}, bf16[1152,384]{1,0:...) custom-call(s32[5]{0:T(128)} %pad_add_fusion.2.place_ref, ...), custom_call_target="tpu_custom_call" | custom-call | flops 2064973824 | bytes 13271040 | tf_op jit(solution)/shard_map/pallas_call | solution.py:319
  66.6 1.3 collective-permute-start.6
  67.8 0.8 collective-permute-start.5
  68.7 11.3 %shard_map.341 = (bf16[2,576,384]{2,1,0:T(8,128)(2,1)}, bf16[6,2,208,208]{3,2,1,0:T(8,128)(2,1)}, bf16[6,576,576]{2,1,0:T(8,128)(2,1)}) custom-call(s32[5]{0:T(128)} %pad_add_fusion.2.place_ref, bf16[2,576,384]{2,1,0:T(8,128)(2,1)} %bitcast.28, bf16[2,576,384]{2,1,0:T(8,128)(2,1)} %bitcast.32, bf16[2,576,384]{2,1,0:T(8,128)(2,1)} %bitcast.36, ...), custom_call_target="tpu_custom_call" | custom-call | flops 1285029888 | bytes 12000000 | tf_op jit(solution)/shard_map/pallas_call | solution.py:392
  80.0 0.9 collective-permute-done.6.w3.w13.y3
  80.9 3.3 %collective-permute-done.5.w1.w11.y1 = bf16[192,2304]{1,0:T(8,128)(2,1)S(1)} collective-permute-done((bf16[192,2304]{1,0:T(8,128)(2,1)S(1)}, bf16[192,2304]{1,0:T(8,128)(2,1)S(1)}, u32[]{:S(2)}, u32[]{:S(2)}) %collective-permute-start.5) | collective-permute-done | bytes 884768 | tf_op jit(solution)/shard_map/ppermute | solution.py:70
  85.0 2.0 collective-permute-start.9
  87.0 3.6 %shard_map.342.gy_ref = bf16[1152,768]{1,0:T(8,128)(2,1)} custom-call(s32[5]{0:T(128)} %pad_add_fusion.2.place_ref, bf16[576,768]{1,0:T(8,128)(2,1)} %bitcast.53, bf16[576,768]{1,0:T(8,128)(2,1)} %collective-permute-done.7.co_ref), custom_call_target="tpu_custom_call" | custom-call | flops 3538944 | bytes 3538944 | tf_op jit(solution)/shard_map/pallas_call | solution.py:245
  90.6 10.3 %collective-permute-done.9.w2.w12.y2 = bf16[192,2304]{1,0:T(8,128)(2,1)S(1)} collective-permute-done((bf16[192,2304]{1,0:T(8,128)(2,1)S(1)}, bf16[192,2304]{1,0:T(8,128)(2,1)S(1)}, u32[]{:S(2)}, u32[]{:S(2)}) %collective-permute-start.9) | collective-permute-done | bytes 884768 | tf_op jit(solution)/shard_map/ppermute | solution.py:70
  100.9 0.9 copy-done.6
  101.8 8.8 %shard_map.343 = (f32[576,768]{1,0:T(8,128)}, f32[1152,768]{1,0:T(8,128)}, f32[1152,8]{1,0:T(8,128)}, bf16[1152,768]{1,0:T(8,128)(2,1)}) custom-call(s32[5]{0:T(128)} %pad_add_fusion.2.place_ref, bf16[2,576,384]{2,1,0:T(8,128)(2,1)} %get-tuple-element.104.mine_ref.o0.o1, bf16[2,576,384]{2,1,0:T(8,128)(2,1)} %copy-done.5, bf16[576,768]{1,0:T(8,128)(2,1)} %bitcast.42, ...), custom_call_target="tpu_custom_call" | custom-call | flops 1358954496 | bytes 10027008 | tf_op jit(solution)/shard_map/pallas_call | solution.py:440
  110.7 18.7 %shard_map.344 = (f32[576,768]{1,0:T(8,128)}, f32[576,768]{1,0:T(8,128)}, bf16[1152,768]{1,0:T(8,128)(2,1)}, bf16[1152,1536]{1,0:T(8,128)(2,1)}, bf16[1152,1536]{1,0:T(8,128)(2,1)}, /*index=5*/f32[1,1536]{1,0:T(1,128)}) custom-call(s32[5]{0:T(128)} %pad_add_fusion.2.place_ref, bf16[1152,768]{1,0:T(8,128)(2,1)} %get-tuple-element.116.h2_ref, ...), custom_call_target="tpu_custom_call" | custom-call | flops 10871635968 | bytes 30000000 | tf_op jit(solution)/shard_map/pallas_call | solution.py:514
  129.4 2.9 %collective-permute-start.10 = (bf16[1152,768]{1,0:T(8,128)(2,1)}, bf16[1152,768]{1,0:T(8,128)(2,1)S(1)}, u32[]{:S(2)}, u32[]{:S(2)}) collective-permute-start(bf16[1152,768]{1,0:T(8,128)(2,1)} %get-tuple-element.123.gh2_ref), channel_id=1, source_target_pairs={{0,64},{64,0},{1,65},{65,1},{2,66},{66,2},{3,67},{67,3},{4,68},{68... | collective-permute-start | bytes 5308424 | tf_op jit(solution)/shard_map/ppermute | solution.py:1014
  132.3 7.6 %shard_map.345 = bf16[1536,768]{1,0:T(8,128)(2,1)} custom-call(s32[5]{0:T(128)} %pad_add_fusion.2.place_ref, bf16[1152,1536]{1,0:T(8,128)(2,1)} %get-tuple-element.124.act_ref, bf16[1152,768]{1,0:T(8,128)(2,1)} %shard_map.342.gy_ref), custom_call_target="tpu_custom_call" | custom-call | flops 2717908992 | bytes 7667712 | tf_op jit(solution)/shard_map/pallas_call | solution.py:562
  140.1 1.0 copy-done.9
  141.1 12.8 %shard_map.346 = (bf16[768,1536]{1,0:T(8,128)(2,1)}, f32[576,768]{1,0:T(8,128)}, bf16[1152,768]{1,0:T(8,128)(2,1)}, f32[8,768]{1,0:T(8,128)}) custom-call(s32[5]{0:T(128)} %pad_add_fusion.2.place_ref, bf16[1152,768]{1,0:T(8,128)(2,1)} %get-tuple-element.116.h2_ref, bf16[1152,1536]{1,0:T(8,128)(2,1)} %get-tuple-element.120.gup_ref, ...), custom_call_target="tpu_custom_call" | custom-call | flops 2717908992 | bytes 21823488 | tf_op jit(solution)/shard_map/pallas_call | solution.py:613
  154.0 28.4 %shard_map.347 = (bf16[192,1664]{1,0:T(8,128)(2,1)}, bf16[192,1664]{1,0:T(8,128)(2,1)}, bf16[192,1664]{1,0:T(8,128)(2,1)}, bf16[192,1664]{1,0:T(8,128)(2,1)}, f32[576,768]{1,0:T(8,128)}, /*index=5*/f32[576,768]{1,0:T(8,128)}) custom-call(s32[5]{0:T(128)} %pad_add_fusion.2.place_ref, bf16[2,576,384]{2,1,0:T(8,128)(2,1)} %bitcast.30, ...), custom_call_target="tpu_custom_call" | custom-call | flops 7983857664 | bytes 36000000 | tf_op jit(solution)/shard_map/pallas_call | solution.py:780
  182.4 1.0 collective-permute-start.12
  183.5 2.2 collective-permute-start.13
  185.7 3.6 %collective-permute-start.16 = (f32[576,768]{1,0:T(8,128)}, f32[576,768]{1,0:T(8,128)S(1)}, u32[]{:S(2)}, u32[]{:S(2)}) collective-permute-start(f32[576,768]{1,0:T(8,128)} %get-tuple-element.146), channel_id=1, source_target_pairs={{0,64},{64,0},{1,65},{65,1},{2,66},{66,2},{3,67},{67,3},{4,68},{68... | collective-permute-start | bytes 5308424 | tf_op jit(solution)/shard_map/ppermute | solution.py:1014
  189.2 6.2 %all-to-all-start.2 = ((bf16[16,24,768]{2,1,0:T(8,128)(2,1)}), bf16[16,24,768]{2,1,0:T(8,128)(2,1)S(1)}, u32[]{:S(2)}, u32[]{:S(2)}) async-start(bf16[16,24,768]{2,1,0:T(8,128)(2,1)} %bitcast.55), calls=%async_computation.3 | async-start | bytes 1179648 | tf_op jit(solution)/shard_map/all_to_all | solution.py:74
  195.4 5.3 %reduce-scatter.5.cloned.1.call-done.f_ref = bf16[192,1536]{1,0:T(8,128)(2,1)} async-done(((bf16[768,1536]{1,0:T(8,128)(2,1)}), bf16[192,1536]{1,0:T(8,128)(2,1)}) %reduce-scatter.5.cloned.1.call-update) | async-done | bytes 589840 | tf_op jit(solution)/shard_map/reduce_scatter | solution.py:1020
  200.7 8.9 %all-to-all-done.2.in_ref = bf16[16,24,768]{2,1,0:T(8,128)(2,1)S(1)} async-done(((bf16[16,24,768]{2,1,0:T(8,128)(2,1)}), bf16[16,24,768]{2,1,0:T(8,128)(2,1)S(1)}, u32[]{:S(2)}, u32[]{:S(2)}) %all-to-all-start.2) | async-done | bytes 589856 | tf_op jit(solution)/shard_map/all_to_all | solution.py:74
  210.5 3.4 %shard_map.348 = bf16[16,12,3200]{2,1,0:T(8,128)(2,1)} custom-call(bf16[192,1664]{1,0:T(8,128)(2,1)} %get-tuple-element.129.q0, bf16[192,1664]{1,0:T(8,128)(2,1)} %copy-done.14, bf16[192,1664]{1,0:T(8,128)(2,1)} %collective-permute-done.12.q2, bf16[192,1664]{1,0:T(8,128)(2,1)} %collective-permute-done.13.q3, ...), custom_call_target="tpu_custom_call" | custom-call | flops 1277952 | bytes 3194880 | tf_op jit(solution)/shard_map/pallas_call | solution.py:852
  213.9 5.3 %all-to-all-start.3 = ((bf16[16,12,3200]{2,1,0:T(8,128)(2,1)}), bf16[16,12,3200]{2,1,0:T(8,128)(2,1)S(1)}, u32[]{:S(2)}, u32[]{:S(2)}) async-start(bf16[16,12,3200]{2,1,0:T(8,128)(2,1)} %shard_map.348), calls=%async_computation.5 | async-start | bytes 3276800 | tf_op jit(solution)/shard_map/all_to_all | solution.py:74
  219.3 1.8 shard_map.349.mine_ref
  221.1 1.3 copy-done.10
  222.4 6.1 %shard_map.351 = (f32[576,768]{1,0:T(8,128)}, bf16[576,768]{1,0:T(8,128)(2,1)}) custom-call(bf16[576,768]{1,0:T(8,128)(2,1)} %bitcast.44, f32[576,768]{1,0:T(8,128)} %get-tuple-element.141.ga_ref, f32[576,768]{1,0:T(8,128)} %get-tuple-element.142.gh_ref, f32[576,768]{1,0:T(8,128)} %collective-permute-done.15.other_ref, ...), custom_call_target="tpu_custom_call" | custom-call | flops 13271040 | bytes 12386304 | tf_op jit(solution)/shard_map/pallas_call | solution.py:828
  229.1 2.3 shard_map.350
  231.4 8.5 %all-to-all-done.3.in_ref = bf16[16,12,3200]{2,1,0:T(8,128)(2,1)S(1)} async-done(((bf16[16,12,3200]{2,1,0:T(8,128)(2,1)}), bf16[16,12,3200]{2,1,0:T(8,128)(2,1)S(1)}, u32[]{:S(2)}, u32[]{:S(2)}) %all-to-all-start.3) | async-done | bytes 1228832 | tf_op jit(solution)/shard_map/all_to_all | solution.py:74
  239.9 1.2 copy-done.1
  241.1 2.3 shard_map.352.g_ref.mine_ref
  243.4 1.7 collective-permute-done.17.o_ref.other_ref
  245.7 2.0 shard_map.353
  247.7 19.9 %all_to_all.25.norm_ref = f32[64,8,128]{2,1,0:T(8,128)} all-to-all(f32[64,8,128]{2,1,0:T(8,128)} %shard_map.353), channel_id=1, replica_groups=mesh['grp'=2,'dp'=64] {'dp'}, dimensions={0} | all-to-all | bytes 524288 | tf_op jit(solution)/shard_map/all_to_all | solution.py:1086
  267.6 5.6 %shard_map.354 = (f32[12,2304]{1,0:T(8,128)}, f32[12,2304]{1,0:T(8,128)}, f32[12,2304]{1,0:T(8,128)}, f32[12,768]{1,0:T(8,128)}, f32[12,768]{1,0:T(8,128)}, /*in...) custom-call(s32[5]{0:T(128)} %pad_add_fusion.2.place_ref, ...), custom_call_target="tpu_custom_call" | custom-call | flops 2211840 | bytes 3000000 | tf_op jit(solution)/shard_map/pallas_call | solution.py:971
  (80 shorter events, 7.9 us)
Async XLA Ops:
  7.2 11.6 %copy-start.15 = (f32[12,768]{1,0:T(8,128)S(1)}, f32[12,768]{1,0:T(8,128)}, u32[]{:S(2)}) copy-start(f32[12,768]{1,0:T(8,128)} %refs_1_.1) | copy-start | bytes 110596
  7.2 11.6 %copy-start.13 = (f32[12,3072]{1,0:T(8,128)S(1)}, f32[12,3072]{1,0:T(8,128)}, u32[]{:S(2)}) copy-start(f32[12,3072]{1,0:T(8,128)} %refs_2_.1) | copy-start | bytes 442372
  7.2 103.5 %all-gather.2.cloned.1.call-start = ((), (), s32[]{:S(2)}) async-start(), calls=%async_computation.7 | async-start | bytes 2396160 | tf_op jit(solution)/shard_map/all_gather | solution.py:1024
  10.5 19.6 %all-to-all-start = ((bf16[16,12,1280]{2,1,0:T(8,128)(2,1)}), bf16[16,12,1280]{2,1,0:T(8,128)(2,1)S(1)}, u32[]{:S(2)}, u32[]{:S(2)}) async-start(bf16[16,12,1280]{2,1,0:T(8,128)(2,1)} %get-tuple-element.95), calls=%async_computation | async-start | bytes 1310720 | tf_op jit(solution)/shard_map/all_to_all | solution.py:74
  18.6 32.8 %collective-permute-start.1 = (bf16[576,768]{1,0:T(8,128)(2,1)}, bf16[576,768]{1,0:T(8,128)(2,1)S(1)}, u32[]{:S(2)}, u32[]{:S(2)}) collective-permute-start(bf16[576,768]{1,0:T(8,128)(2,1)} %bitcast.40), channel_id=1, source_target_pairs={{0,64},{64,0},{1,65},{65,1},{2,66},{66,2},{3,67},{67,3},{4,68},{68... | collective-permute-start | bytes 2654216 | tf_op jit(solution)/shard_map/ppermute | solution.py:1014
  30.2 11.4 %copy-start.8 = (bf16[192,1280]{1,0:T(8,128)(2,1)}, bf16[192,1280]{1,0:T(8,128)(2,1)S(1)}, u32[]{:S(2)}) copy-start(bf16[192,1280]{1,0:T(8,128)(2,1)S(1)} %reshape.111.w0.v0) | copy-start | bytes 1474564
  30.2 10.3 %collective-permute-start.2 = (bf16[192,1280]{1,0:T(8,128)(2,1)S(1)}, bf16[192,1280]{1,0:T(8,128)(2,1)}, u32[]{:S(2)}, u32[]{:S(2)}) collective-permute-start(bf16[192,1280]{1,0:T(8,128)(2,1)S(1)} %reshape.111.w0.v0), channel_id=1, source_target_pairs={{0,16},{16,32},{32,48},{48,0},{1,17},{17,33},{33,49},{49,1},{2,18}... | collective-permute-start | bytes 1474568 | tf_op jit(solution)/shard_map/ppermute | solution.py:70
  32.9 13.8 %copy-start.17 = (s32[1,1,576]{2,1,0:T(1,128)S(1)}, s32[1,1,576]{2,1,0:T(1,128)}, u32[]{:S(2)}) copy-start(s32[1,1,576]{2,1,0:T(1,128)} %param.24) | copy-start | bytes 6916
  32.9 13.8 %copy-start.18 = (s32[1,1,576]{2,1,0:T(1,128)S(1)}, s32[1,1,576]{2,1,0:T(1,128)}, u32[]{:S(2)}) copy-start(s32[1,1,576]{2,1,0:T(1,128)} %param.23) | copy-start | bytes 6916
  32.9 13.8 %copy-start.19 = (s32[1,1,2]{2,1,0:T(1,128)S(1)}, s32[1,1,2]{2,1,0:T(1,128)}, u32[]{:S(2)}) copy-start(s32[1,1,2]{2,1,0:T(1,128)} %param.22) | copy-start | bytes 28
  32.9 13.9 %copy-start.11 = (bf16[1,1,576,768]{3,2,1,0:T(8,128)(2,1)S(1)}, bf16[1,1,576,768]{3,2,1,0:T(8,128)(2,1)}, u32[]{:S(2)}) copy-start(bf16[1,1,576,768]{3,2,1,0:T(8,128)(2,1)} %param.21) | copy-start | bytes 2654212
  32.9 18.5 %collective-permute-start.4 = (bf16[192,1280]{1,0:T(8,128)(2,1)S(1)}, bf16[192,1280]{1,0:T(8,128)(2,1)}, u32[]{:S(2)}, u32[]{:S(2)}) collective-permute-start(bf16[192,1280]{1,0:T(8,128)(2,1)S(1)} %reshape.111.w0.v0), channel_id=1, source_target_pairs={{0,48},{16,0},{32,16},{48,32},{1,49},{17,1},{33,17},{49,33},{2,50}... | collective-permute-start | bytes 1474568 | tf_op jit(solution)/shard_map/ppermute | solution.py:70
  35.4 16.1 %collective-permute-start.3 = (bf16[192,1280]{1,0:T(8,128)(2,1)S(1)}, bf16[192,1280]{1,0:T(8,128)(2,1)}, u32[]{:S(2)}, u32[]{:S(2)}) collective-permute-start(bf16[192,1280]{1,0:T(8,128)(2,1)S(1)} %reshape.111.w0.v0), channel_id=1, source_target_pairs={{0,32},{16,48},{32,0},{48,16},{1,33},{17,49},{33,1},{49,17},{2,34}... | collective-permute-start | bytes 1474568 | tf_op jit(solution)/shard_map/ppermute | solution.py:70
  41.6 24.8 %all-to-all-start.1 = ((bf16[16,12,2304]{2,1,0:T(8,128)(2,1)}), bf16[16,12,2304]{2,1,0:T(8,128)(2,1)S(1)}, u32[]{:S(2)}, u32[]{:S(2)}) async-start(bf16[16,12,2304]{2,1,0:T(8,128)(2,1)} %broadcast_in_dim.10), calls=%async_computation.1 | async-start | bytes 2359296 | tf_op jit(solution)/shard_map/all_to_all | solution.py:74
  46.6 142.6 %reduce-scatter.3.cloned.1.call-start = ((), (), s32[]{:S(2)}) async-start(), calls=%async_computation.8 | async-start | bytes 2949120 | tf_op jit(solution)/shard_map/reduce_scatter | solution.py:1020
  46.8 1.6 collective-permute-start
  46.8 33.2 %collective-permute-start.7 = (bf16[576,768]{1,0:T(8,128)(2,1)S(1)}, bf16[576,768]{1,0:T(8,128)(2,1)}, u32[]{:S(2)}, u32[]{:S(2)}) collective-permute-start(bf16[576,768]{1,0:T(8,128)(2,1)S(1)} %bitcast.54), channel_id=1, source_target_pairs={{0,64},{64,0},{1,65},{65,1},{2,66},{66,2},{3,67},{67,3},{4,68},{68... | collective-permute-start | bytes 2654216 | tf_op jit(solution)/shard_map/ppermute | solution.py:1014
  51.5 0.9 copy-start.2
  66.6 18.4 %copy-start = (bf16[192,2304]{1,0:T(8,128)(2,1)}, bf16[192,2304]{1,0:T(8,128)(2,1)S(1)}, u32[]{:S(2)}) copy-start(bf16[192,2304]{1,0:T(8,128)(2,1)S(1)} %reshape.113.w0.w10.y0) | copy-start | bytes 2654212
  66.6 14.3 %collective-permute-start.6 = (bf16[192,2304]{1,0:T(8,128)(2,1)S(1)}, bf16[192,2304]{1,0:T(8,128)(2,1)S(1)}, u32[]{:S(2)}, u32[]{:S(2)}) collective-permute-start(bf16[192,2304]{1,0:T(8,128)(2,1)S(1)} %reshape.113.w0.w10.y0), channel_id=1, source_target_pairs={{0,48},{16,0},{32,16},{48,32},{1,49},{17,1},{33,17},{49,33},{2,50}... | collective-permute-start | bytes 2654216 | tf_op jit(solution)/shard_map/ppermute | solution.py:70
  67.8 16.4 %collective-permute-start.5 = (bf16[192,2304]{1,0:T(8,128)(2,1)S(1)}, bf16[192,2304]{1,0:T(8,128)(2,1)S(1)}, u32[]{:S(2)}, u32[]{:S(2)}) collective-permute-start(bf16[192,2304]{1,0:T(8,128)(2,1)S(1)} %reshape.113.w0.w10.y0), channel_id=1, source_target_pairs={{0,16},{16,32},{32,48},{48,0},{1,17},{17,33},{33,49},{49,1},{2,18}... | collective-permute-start | bytes 2654216 | tf_op jit(solution)/shard_map/ppermute | solution.py:70
  80.9 9.7 %copy-start.3 = (bf16[192,2304]{1,0:T(8,128)(2,1)}, bf16[192,2304]{1,0:T(8,128)(2,1)S(1)}, u32[]{:S(2)}) copy-start(bf16[192,2304]{1,0:T(8,128)(2,1)S(1)} %collective-permute-done.6.w3.w13.y3) | copy-start | bytes 2654212
  84.2 6.4 %copy-start.4 = (bf16[192,2304]{1,0:T(8,128)(2,1)}, bf16[192,2304]{1,0:T(8,128)(2,1)S(1)}, u32[]{:S(2)}) copy-start(bf16[192,2304]{1,0:T(8,128)(2,1)S(1)} %collective-permute-done.5.w1.w11.y1) | copy-start | bytes 2654212
  84.2 6.4 %collective-permute-start.8 = (bf16[2,576,384]{2,1,0:T(8,128)(2,1)}, bf16[2,576,384]{2,1,0:T(8,128)(2,1)S(1)}, u32[]{:S(2)}, u32[]{:S(2)}) collective-permute-start(bf16[2,576,384]{2,1,0:T(8,128)(2,1)} %get-tuple-element.104.mine_ref.o0.o1), channel_id=1, source_target_pairs={{0,64},{64,0},{1,65},{65,1},{2,66},{66,2},{3,67},{67,3},{4,68},{68... | collective-permute-start | bytes 2654216 | tf_op jit(solution)/shard_map/ppermute | solution.py:1014
  85.0 15.9 %collective-permute-start.9 = (bf16[192,2304]{1,0:T(8,128)(2,1)S(1)}, bf16[192,2304]{1,0:T(8,128)(2,1)S(1)}, u32[]{:S(2)}, u32[]{:S(2)}) collective-permute-start(bf16[192,2304]{1,0:T(8,128)(2,1)S(1)} %reshape.113.w0.w10.y0), channel_id=1, source_target_pairs={{0,32},{16,48},{32,0},{48,16},{1,33},{17,49},{33,1},{49,17},{2,34}... | collective-permute-start | bytes 2654216 | tf_op jit(solution)/shard_map/ppermute | solution.py:70
  90.6 10.3 %copy-start.5 = (bf16[2,576,384]{2,1,0:T(8,128)(2,1)}, bf16[2,576,384]{2,1,0:T(8,128)(2,1)S(1)}, u32[]{:S(2)}) copy-start(bf16[2,576,384]{2,1,0:T(8,128)(2,1)S(1)} %collective-permute-done.8.other_ref) | copy-start | bytes 2654212
  100.9 0.9 copy-start.6
  129.4 10.5 %collective-permute-start.10 = (bf16[1152,768]{1,0:T(8,128)(2,1)}, bf16[1152,768]{1,0:T(8,128)(2,1)S(1)}, u32[]{:S(2)}, u32[]{:S(2)}) collective-permute-start(bf16[1152,768]{1,0:T(8,128)(2,1)} %get-tuple-element.123.gh2_ref), channel_id=1, source_target_pairs={{0,64},{64,0},{1,65},{65,1},{2,66},{66,2},{3,67},{67,3},{4,68},{68... | collective-permute-start | bytes 5308424 | tf_op jit(solution)/shard_map/ppermute | solution.py:1014
  139.8 1.2 copy-start.9
  139.9 60.9 %reduce-scatter.5.cloned.1.call-start = ((), (), s32[]{:S(2)}) async-start(), calls=%async_computation.9 | async-start | bytes 2949120 | tf_op jit(solution)/shard_map/reduce_scatter | solution.py:1020
  182.4 27.3 %collective-permute-start.11 = (bf16[192,1664]{1,0:T(8,128)(2,1)}, bf16[192,1664]{1,0:T(8,128)(2,1)S(1)}, u32[]{:S(2)}, u32[]{:S(2)}) collective-permute-start(bf16[192,1664]{1,0:T(8,128)(2,1)} %get-tuple-element.130), channel_id=1, source_target_pairs={{0,16},{16,32},{32,48},{48,0},{1,17},{17,33},{33,49},{49,1},{2,18}... | collective-permute-start | bytes 1916936 | tf_op jit(solution)/shard_map/ppermute | solution.py:70
  182.4 27.2 %collective-permute-start.12 = (bf16[192,1664]{1,0:T(8,128)(2,1)}, bf16[192,1664]{1,0:T(8,128)(2,1)}, u32[]{:S(2)}, u32[]{:S(2)}) collective-permute-start(bf16[192,1664]{1,0:T(8,128)(2,1)} %get-tuple-element.131), channel_id=1, source_target_pairs={{0,32},{16,48},{32,0},{48,16},{1,33},{17,49},{33,1},{49,17},{2,34}... | collective-permute-start | bytes 1916936 | tf_op jit(solution)/shard_map/ppermute | solution.py:70
  183.5 26.2 %collective-permute-start.13 = (bf16[192,1664]{1,0:T(8,128)(2,1)}, bf16[192,1664]{1,0:T(8,128)(2,1)}, u32[]{:S(2)}, u32[]{:S(2)}) collective-permute-start(bf16[192,1664]{1,0:T(8,128)(2,1)} %get-tuple-element.132), channel_id=1, source_target_pairs={{0,48},{16,0},{32,16},{48,32},{1,49},{17,1},{33,17},{49,33},{2,50}... | collective-permute-start | bytes 1916936 | tf_op jit(solution)/shard_map/ppermute | solution.py:70
  185.7 35.4 %collective-permute-start.16 = (f32[576,768]{1,0:T(8,128)}, f32[576,768]{1,0:T(8,128)S(1)}, u32[]{:S(2)}, u32[]{:S(2)}) collective-permute-start(f32[576,768]{1,0:T(8,128)} %get-tuple-element.146), channel_id=1, source_target_pairs={{0,64},{64,0},{1,65},{65,1},{2,66},{66,2},{3,67},{67,3},{4,68},{68... | collective-permute-start | bytes 5308424 | tf_op jit(solution)/shard_map/ppermute | solution.py:1014
  189.2 31.8 %collective-permute-start.15 = (f32[576,768]{1,0:T(8,128)}, f32[576,768]{1,0:T(8,128)}, u32[]{:S(2)}, u32[]{:S(2)}) collective-permute-start(f32[576,768]{1,0:T(8,128)} %get-tuple-element.143), channel_id=1, source_target_pairs={{0,64},{64,0},{1,65},{65,1},{2,66},{66,2},{3,67},{67,3},{4,68},{68... | collective-permute-start | bytes 5308424 | tf_op jit(solution)/shard_map/ppermute | solution.py:1014
  189.2 20.4 %all-to-all-start.2 = ((bf16[16,24,768]{2,1,0:T(8,128)(2,1)}), bf16[16,24,768]{2,1,0:T(8,128)(2,1)S(1)}, u32[]{:S(2)}, u32[]{:S(2)}) async-start(bf16[16,24,768]{2,1,0:T(8,128)(2,1)} %bitcast.55), calls=%async_computation.3 | async-start | bytes 1179648 | tf_op jit(solution)/shard_map/all_to_all | solution.py:74
  209.6 4.3 %copy-start.7 = (bf16[16,24,768]{2,1,0:T(8,128)(2,1)}, bf16[16,24,768]{2,1,0:T(8,128)(2,1)S(1)}, u32[]{:S(2)}) copy-start(bf16[16,24,768]{2,1,0:T(8,128)(2,1)S(1)} %all-to-all-done.2.in_ref) | copy-start | bytes 1769476
  209.7 0.9 copy-start.14
  213.9 26.0 %all-to-all-start.3 = ((bf16[16,12,3200]{2,1,0:T(8,128)(2,1)}), bf16[16,12,3200]{2,1,0:T(8,128)(2,1)S(1)}, u32[]{:S(2)}, u32[]{:S(2)}) async-start(bf16[16,12,3200]{2,1,0:T(8,128)(2,1)} %shard_map.348), calls=%async_computation.5 | async-start | bytes 3276800 | tf_op jit(solution)/shard_map/all_to_all | solution.py:74
  221.1 7.4 %collective-permute-start.14 = (f32[24,768]{1,0:T(8,128)}, f32[24,768]{1,0:T(8,128)S(1)}, u32[]{:S(2)}, u32[]{:S(2)}) collective-permute-start(f32[24,768]{1,0:T(8,128)} %shard_map.349.mine_ref), channel_id=1, source_target_pairs={{0,64},{64,0},{1,65},{65,1},{2,66},{66,2},{3,67},{67,3},{4,68},{68... | collective-permute-start | bytes 221192 | tf_op jit(solution)/shard_map/ppermute | solution.py:1014
  221.1 1.3 copy-start.10
  228.4 0.6 copy-start.16
  239.9 1.2 copy-start.1
  243.4 1.7 collective-permute-start.17
  245.1 0.7 copy-start.12
Sparse Core Ops, SparseCore 0:
  11.5 82.7 all-gather.1
  140.0 25.8 reduce-scatter.2
  168.3 32.3 reduce-scatter.4

commit v4 on v3

--- a/solution.py
+++ b/solution.py
@@ -130,8 +130,11 @@
     return spots(core, (DC, D), 1, 0)
 
 
-def params(**kw):
-    return pltpu.CompilerParams(vmem_limit_bytes=VMEM_LIMIT, **kw)
+SMALL_LIMIT = 16 * 1024 * 1024
+
+
+def params(limit=VMEM_LIMIT):
+    return pltpu.CompilerParams(vmem_limit_bytes=limit)
 
 
 def cost(flops, bytes_accessed, transcendentals=0):
@@ -816,24 +819,27 @@
     )
 
 
-def last_kernel(x_ref, ga_ref, gh_ref, other_ref, after_ref, mlp_ref, mlpo_ref, v_ref, gt_ref, out_ref):
+def last_kernel(x_ref, ga_ref, gh_ref, other_ref, v_ref, gt_ref):
     normed, inv_std = stats(x_ref[...].astype(f32))
     gt_ref[...] = ga_ref[...] + norm_back(gh_ref[...] + other_ref[...], normed, inv_std, v_ref[0:1, :])
+
+
+def mixed_kernel(after_ref, mlp_ref, mlpo_ref, v_ref, out_ref):
     out_ref[...] = (after_ref[...] + (mlp_ref[...] + mlpo_ref[...] + v_ref[8:9, :])).astype(bf16)
 
 
-def last_call(x, ga, gh, other, after, mlp, mlp_other, vec):
+def by_rows(kernel, out_type, flops, *args):
     rows = 288
-    tile = lambda n: pl.BlockSpec((rows, n), lambda i: (i, 0))
-    return pl.pallas_call(
-        last_kernel,
+    tile = pl.BlockSpec((rows, D), lambda i: (i, 0))
+    return pl.pallas_call(
+        kernel,
         grid=(S // rows,),
-        in_specs=[tile(D)] * 7 + [pl.BlockSpec(vec.shape, lambda i: (0, 0))],
-        out_specs=[tile(D), tile(D)],
-        out_shape=[jax.ShapeDtypeStruct((S, D), f32), jax.ShapeDtypeStruct((S, D), bf16)],
+        in_specs=[tile] * (len(args) - 1) + [pl.BlockSpec(args[-1].shape, lambda i: (0, 0))],
+        out_specs=tile,
+        out_shape=jax.ShapeDtypeStruct((S, D), out_type),
         compiler_params=params(),
-        cost_estimate=cost(30 * S * D, S * D * 28),
-    )(x, ga, gh, other, after, mlp, mlp_other, vec)
+        cost_estimate=cost(flops * S * D, S * D * 16),
+    )(*args)
 
 
 WIDE = PACK + FC
@@ -868,7 +874,7 @@
     return pl.pallas_call(
         sum_kernel,
         out_shape=jax.ShapeDtypeStruct(packed.shape[1:], f32),
-        compiler_params=params(),
+        compiler_params=params(SMALL_LIMIT),
         cost_estimate=cost(packed.size, packed.size * 2),
     )(packed)
 
@@ -894,7 +900,7 @@
             out_specs=[whole(a) for a in shapes],
         ),
         out_shape=shapes,
-        compiler_params=params(),
+        compiler_params=params(SMALL_LIMIT),
         cost_estimate=cost(6 * FR * D, FR * D * 16),
     )(place, mine, other)
 
@@ -911,7 +917,7 @@
     return pl.pallas_call(
         norm_kernel,
         out_shape=jax.ShapeDtypeStruct((CHIPS, 8, 128), f32),
-        compiler_params=params(),
+        compiler_params=params(SMALL_LIMIT),
         cost_estimate=cost(4 * KR * PACK, 1e6),
     )(g, o, squares)
 
@@ -977,7 +983,7 @@
             out_specs=[whole(a) for a in shapes],
         ),
         out_shape=shapes,
-        compiler_params=params(),
+        compiler_params=params(SMALL_LIMIT),
         cost_estimate=cost(20 * KR * FF * 3, 3e6),
     )(place, *args)
 
@@ -1078,12 +1084,15 @@
     g2, squares = fc2_call(place, g_fc2, swap(g_fc2))
     packed, gh1 = lax.optimization_barrier((pack_call(parts, sum_fc1), gh1))
     got = plane_swap(packed)
-    gt, mixed = last_call(x_own, ga, gh1, gh1_other, after, mlp, mlp_other, vec)
-    got, g2, squares, gt, mixed = lax.optimization_barrier((got, g2, squares, gt, mixed))
+    gt = by_rows(last_kernel, f32, 25, x_own, ga, gh1, gh1_other, vec)
+    got, g2, squares, gt = lax.optimization_barrier((got, g2, squares, gt))
     grads = sum_call(got)
 
     grads_other = swap(grads)
-    norms = lax.all_to_all(norm_call(grads, grads_other, squares), "dp", 0, 0)
+    squares, mlp = lax.optimization_barrier((norm_call(grads, grads_other, squares), mlp))
+    norms = lax.all_to_all(squares, "dp", 0, 0)
+    mixed = by_rows(mixed_kernel, bf16, 4, after, mlp, mlp_other, vec)
+    norms, mixed = lax.optimization_barrier((norms, mixed))
     *updates, grad_norm, bias_proj_grad = adam_call(
         place,
         norms,

time: 285 us -> 280 us (0.982)
  blocking collectives: 19.9 us -> 0 us
  waiting for transfers between devices: 53.6 us -> 73.5 us
  Pallas kernels: 131 us -> 125 us
  starting transfers between devices: 45.3 us -> 49.2 us
    all_to_all x1 -> x0, blocking collectives: 19.9 us -> none  [local(): norms = lax.all_to_all(norm_call(grads, grads_other, squares), 'dp', 0, 0)]
    all_to_all x4, waiting for transfers between devices: 28.1 us -> 40.2 us  [plane_swap(): return lax.all_to_all(value, BOTH, 0, 0, axis_index_groups=planes())]
    all_to_all x0 -> x1, starting transfers between devices: none -> 9.52 us  [local(): norms = lax.all_to_all(squares, 'dp', 0, 0)]
    all_to_all x0 -> x1, waiting for transfers between devices: none -> 6.94 us  [local(): norms = lax.all_to_all(squares, 'dp', 0, 0)]
    ppermute x9, waiting for transfers between devices: 18.5 us -> 24.3 us  [shift(): return lax.ppermute(value, BOTH, pairs)]
    reduce_scatter x2, waiting for transfers between devices: 5.32 us -> 0.52 us  [line_sum(): lax.psum_scatter(whole, BOTH, scatter_dimension=0, axis_index_groups=line...]
    ppermute x9, starting transfers between devices: 8.41 us -> 3.8 us  [swap(): return lax.ppermute(a, 'grp', [(0, 1), (1, 0)])]
    pallas_call x2, Pallas kernels: 4.09 us -> 0.3 us  [sum_call(): pl.pallas_call(sum_kernel, out_shape=jax.ShapeDtypeStruct(packed.shape[1:...]
  transfers between devices with their start and end apart: 25 -> 26, of which waited for: 9 -> 10; matrix products, arithmetic and copies ran while one was open for 2% -> 3% of each run, Pallas kernels for 36% -> 36%
where the time goes in v4:
time: 280 us; the launch traced here: 275 us
  Pallas kernels  125 us (45%)
  waiting for transfers between devices  73.5 us (26%)
  starting transfers between devices  49.2 us (18%)
  between operations  16 us (6%)
  local copies, waits for them, and re-layouts  8.59 us (3%)
  other arithmetic  3.34 us (1%)
    all_to_all x4, waiting for transfers between devices, plane_swap(): return lax.all_to_all(value, BOTH, 0, 0, axis_index_groups=planes())  40.2 us
    pallas_call x1, Pallas kernels, attn_bwd_call(): pl.pallas_call(attn_bwd_kernel, grid_spec=pltpu.PrefetchScalarGridSpec(nu...  28.4 us
    ppermute x9, waiting for transfers between devices, shift(): return lax.ppermute(value, BOTH, pairs)  24.3 us
    all_to_all x4, starting transfers between devices, plane_swap(): return lax.all_to_all(value, BOTH, 0, 0, axis_index_groups=planes())  23.6 us
    pallas_call x1, Pallas kernels, mlp_call(): pl.pallas_call(mlp_kernel, grid_spec=pltpu.PrefetchScalarGridSpec(num_sca...  18.7 us
    pallas_call x1, Pallas kernels, qkv_call(): pl.pallas_call(qkv_kernel, grid_spec=pltpu.PrefetchScalarGridSpec(num_sca...  14 us
    pallas_call x1, Pallas kernels, mid_call(): pl.pallas_call(mid_kernel, grid_spec=pltpu.PrefetchScalarGridSpec(num_sca...  12.8 us
    ppermute x9, starting transfers between devices, shift(): return lax.ppermute(value, BOTH, pairs)  11.9 us
  transfers between devices with their start and end apart: 26, of which 10 were waited for; matrix products, arithmetic and copies ran while one was open for 3% of the time, Pallas kernels for 36%

profile of v4, /device:TPU:0, one launch (start us, length us, event | category | flops | bytes accessed | tf_op | source)
XLA Modules:
  0.0 275.3 jit_solution(18128338130346877948)
XLA Ops:
  7.3 0.6 pad_add_fusion.3.place_ref
  7.9 2.6 shard_map.339
  10.5 8.1 %all-to-all-start = ((bf16[16,12,1280]{2,1,0:T(8,128)(2,1)}), bf16[16,12,1280]{2,1,0:T(8,128)(2,1)S(1)}, u32[]{:S(2)}, u32[]{:S(2)}) async-start(bf16[16,12,1280]{2,1,0:T(8,128)(2,1)} %get-tuple-element.96), calls=%async_computation | async-start | bytes 1310720 | tf_op jit(solution)/shard_map/all_to_all | solution.py:74
  18.9 0.6 reshape.112
  19.5 10.6 %all-to-all-done = bf16[16,12,1280]{2,1,0:T(8,128)(2,1)S(1)} async-done(((bf16[16,12,1280]{2,1,0:T(8,128)(2,1)}), bf16[16,12,1280]{2,1,0:T(8,128)(2,1)S(1)}, u32[]{:S(2)}, u32[]{:S(2)}) %all-to-all-start) | async-done | bytes 491552 | tf_op jit(solution)/shard_map/all_to_all | solution.py:74
  30.1 0.9 reshape.111.w0.v0
  31.0 0.9 collective-permute-start.2
  31.9 1.4 fusion
  33.6 2.4 collective-permute-start.4
  36.0 1.2 collective-permute-start.3
  37.3 4.1 %collective-permute-done.2.w1.v1 = bf16[192,1280]{1,0:T(8,128)(2,1)S(1)} collective-permute-done((bf16[192,1280]{1,0:T(8,128)(2,1)}, bf16[192,1280]{1,0:T(8,128)(2,1)S(1)}, u32[]{:S(2)}, u32[]{:S(2)}) %collective-permute-start.2) | collective-permute-done | bytes 491552 | tf_op jit(solution)/shard_map/ppermute | solution.py:70
  41.4 1.2 broadcast_in_dim.10
  42.6 4.9 %all-to-all-start.1 = ((bf16[16,12,2304]{2,1,0:T(8,128)(2,1)}), bf16[16,12,2304]{2,1,0:T(8,128)(2,1)S(1)}, u32[]{:S(2)}, u32[]{:S(2)}) async-start(bf16[16,12,2304]{2,1,0:T(8,128)(2,1)} %broadcast_in_dim.10), calls=%async_computation.1 | async-start | bytes 2359296 | tf_op jit(solution)/shard_map/all_to_all | solution.py:74
  47.7 1.0 collective-permute-start.7
  51.1 0.6 pad_add_fusion.2.place_ref
  51.7 0.6 pad_add_fusion.ints_ref
  52.3 0.9 copy-done.17
  53.3 14.0 %shard_map.340 = (f32[16,768]{1,0:T(8,128)}, bf16[2,768,576]{2,1,0:T(8,128)(2,1)}, f32[1152,384]{1,0:T(8,128)}, f32[1152,384]{1,0:T(8,128)}, bf16[1152,384]{1,0:...) custom-call(s32[5]{0:T(128)} %pad_add_fusion.2.place_ref, ...), custom_call_target="tpu_custom_call" | custom-call | flops 2064973824 | bytes 13271040 | tf_op jit(solution)/shard_map/pallas_call | solution.py:322
  67.6 4.0 %collective-permute-start.6 = (bf16[192,2304]{1,0:T(8,128)(2,1)S(1)}, bf16[192,2304]{1,0:T(8,128)(2,1)S(1)}, u32[]{:S(2)}, u32[]{:S(2)}) collective-permute-start(bf16[192,2304]{1,0:T(8,128)(2,1)S(1)} %reshape.113.w0.w10.y0), channel_id=1, source_target_pairs={{0,48},{16,0},{32,16},{48,32},{1,49},{17,1},{33,17},{49,33},{2,50}... | collective-permute-start | bytes 2654216 | tf_op jit(solution)/shard_map/ppermute | solution.py:70
  71.6 11.3 %shard_map.341 = (bf16[2,576,384]{2,1,0:T(8,128)(2,1)}, bf16[6,2,208,208]{3,2,1,0:T(8,128)(2,1)}, bf16[6,576,576]{2,1,0:T(8,128)(2,1)}) custom-call(s32[5]{0:T(128)} %pad_add_fusion.2.place_ref, bf16[2,576,384]{2,1,0:T(8,128)(2,1)} %bitcast.28, bf16[2,576,384]{2,1,0:T(8,128)(2,1)} %bitcast.32, bf16[2,576,384]{2,1,0:T(8,128)(2,1)} %bitcast.36, ...), custom_call_target="tpu_custom_call" | custom-call | flops 1285029888 | bytes 12000000 | tf_op jit(solution)/shard_map/pallas_call | solution.py:395
  82.9 5.6 %collective-permute-done.6.w3.w13.y3 = bf16[192,2304]{1,0:T(8,128)(2,1)S(1)} collective-permute-done((bf16[192,2304]{1,0:T(8,128)(2,1)S(1)}, bf16[192,2304]{1,0:T(8,128)(2,1)S(1)}, u32[]{:S(2)}, u32[]{:S(2)}) %collective-permute-start.6) | collective-permute-done | bytes 884768 | tf_op jit(solution)/shard_map/ppermute | solution.py:70
  88.4 3.7 %collective-permute-done.5.w1.w11.y1 = bf16[192,2304]{1,0:T(8,128)(2,1)S(1)} collective-permute-done((bf16[192,2304]{1,0:T(8,128)(2,1)S(1)}, bf16[192,2304]{1,0:T(8,128)(2,1)S(1)}, u32[]{:S(2)}, u32[]{:S(2)}) %collective-permute-start.5) | collective-permute-done | bytes 884768 | tf_op jit(solution)/shard_map/ppermute | solution.py:70
  92.4 3.6 %shard_map.342.gy_ref = bf16[1152,768]{1,0:T(8,128)(2,1)} custom-call(s32[5]{0:T(128)} %pad_add_fusion.2.place_ref, bf16[576,768]{1,0:T(8,128)(2,1)} %bitcast.15.c_ref, bf16[576,768]{1,0:T(8,128)(2,1)} %collective-permute-done.7.co_ref), custom_call_target="tpu_custom_call" | custom-call | flops 3538944 | bytes 3538944 | tf_op jit(solution)/shard_map/pallas_call | solution.py:248
  96.0 10.9 %collective-permute-done.9.w2.w12.y2 = bf16[192,2304]{1,0:T(8,128)(2,1)S(1)} collective-permute-done((bf16[192,2304]{1,0:T(8,128)(2,1)S(1)}, bf16[192,2304]{1,0:T(8,128)(2,1)S(1)}, u32[]{:S(2)}, u32[]{:S(2)}) %collective-permute-start.9) | collective-permute-done | bytes 884768 | tf_op jit(solution)/shard_map/ppermute | solution.py:70
  107.0 0.9 copy-done.21
  107.9 8.8 %shard_map.343 = (f32[576,768]{1,0:T(8,128)}, f32[1152,768]{1,0:T(8,128)}, f32[1152,8]{1,0:T(8,128)}, bf16[1152,768]{1,0:T(8,128)(2,1)}) custom-call(s32[5]{0:T(128)} %pad_add_fusion.2.place_ref, bf16[2,576,384]{2,1,0:T(8,128)(2,1)} %get-tuple-element.105.mine_ref.o0.o1, bf16[2,576,384]{2,1,0:T(8,128)(2,1)} %copy-done.20, bf16[576,768]{1,0:T(8,128)(2,1)} %bitcast.42, ...), custom_call_target="tpu_custom_call" | custom-call | flops 1358954496 | bytes 10027008 | tf_op jit(solution)/shard_map/pallas_call | solution.py:443
  116.7 18.7 %shard_map.344 = (f32[576,768]{1,0:T(8,128)}, f32[576,768]{1,0:T(8,128)}, bf16[1152,768]{1,0:T(8,128)(2,1)}, bf16[1152,1536]{1,0:T(8,128)(2,1)}, bf16[1152,1536]{1,0:T(8,128)(2,1)}, /*index=5*/f32[1,1536]{1,0:T(1,128)}) custom-call(s32[5]{0:T(128)} %pad_add_fusion.2.place_ref, bf16[1152,768]{1,0:T(8,128)(2,1)} %get-tuple-element.117.h2_ref, ...), custom_call_target="tpu_custom_call" | custom-call | flops 10871635968 | bytes 30000000 | tf_op jit(solution)/shard_map/pallas_call | solution.py:517
  135.4 7.6 %shard_map.345 = bf16[1536,768]{1,0:T(8,128)(2,1)} custom-call(s32[5]{0:T(128)} %pad_add_fusion.2.place_ref, bf16[1152,1536]{1,0:T(8,128)(2,1)} %get-tuple-element.125.act_ref, bf16[1152,768]{1,0:T(8,128)(2,1)} %shard_map.342.gy_ref), custom_call_target="tpu_custom_call" | custom-call | flops 2717908992 | bytes 7667712 | tf_op jit(solution)/shard_map/pallas_call | solution.py:565
  143.3 1.0 copy-done.22
  144.3 12.8 %shard_map.346 = (bf16[768,1536]{1,0:T(8,128)(2,1)}, f32[576,768]{1,0:T(8,128)}, bf16[1152,768]{1,0:T(8,128)(2,1)}, f32[8,768]{1,0:T(8,128)}) custom-call(s32[5]{0:T(128)} %pad_add_fusion.2.place_ref, bf16[1152,768]{1,0:T(8,128)(2,1)} %get-tuple-element.117.h2_ref, bf16[1152,1536]{1,0:T(8,128)(2,1)} %get-tuple-element.121.gup_ref, ...), custom_call_target="tpu_custom_call" | custom-call | flops 2717908992 | bytes 21823488 | tf_op jit(solution)/shard_map/pallas_call | solution.py:616
  157.1 28.4 %shard_map.347 = (bf16[192,1664]{1,0:T(8,128)(2,1)}, bf16[192,1664]{1,0:T(8,128)(2,1)}, bf16[192,1664]{1,0:T(8,128)(2,1)}, bf16[192,1664]{1,0:T(8,128)(2,1)}, f32[576,768]{1,0:T(8,128)}, /*index=5*/f32[576,768]{1,0:T(8,128)}) custom-call(s32[5]{0:T(128)} %pad_add_fusion.2.place_ref, bf16[2,576,384]{2,1,0:T(8,128)(2,1)} %bitcast.30, ...), custom_call_target="tpu_custom_call" | custom-call | flops 7983857664 | bytes 36000000 | tf_op jit(solution)/shard_map/pallas_call | solution.py:783
  185.6 1.4 collective-permute-start.12
  187.0 1.9 collective-permute-start.13
  188.8 1.9 collective-permute-start.15
  190.8 5.2 %all-to-all-start.2 = ((bf16[16,24,768]{2,1,0:T(8,128)(2,1)}), bf16[16,24,768]{2,1,0:T(8,128)(2,1)S(1)}, u32[]{:S(2)}, u32[]{:S(2)}) async-start(bf16[16,24,768]{2,1,0:T(8,128)(2,1)} %bitcast.55), calls=%async_computation.3 | async-start | bytes 1179648 | tf_op jit(solution)/shard_map/all_to_all | solution.py:74
  196.8 14.1 %all-to-all-done.2.in_ref = bf16[16,24,768]{2,1,0:T(8,128)(2,1)S(1)} async-done(((bf16[16,24,768]{2,1,0:T(8,128)(2,1)}), bf16[16,24,768]{2,1,0:T(8,128)(2,1)S(1)}, u32[]{:S(2)}, u32[]{:S(2)}) %all-to-all-start.2) | async-done | bytes 589856 | tf_op jit(solution)/shard_map/all_to_all | solution.py:74
  211.0 0.8 copy-done.23
  212.2 3.4 %shard_map.348 = bf16[16,12,3200]{2,1,0:T(8,128)(2,1)} custom-call(bf16[192,1664]{1,0:T(8,128)(2,1)} %get-tuple-element.130.q0, bf16[192,1664]{1,0:T(8,128)(2,1)} %copy-done.23, bf16[192,1664]{1,0:T(8,128)(2,1)} %copy-done.24, bf16[192,1664]{1,0:T(8,128)(2,1)} %copy-done.25, bf16[192,1536]{1,0:T(8,128)(2,1)} %reduce-scatter.5.cloned.1.call-done.f_ref), custom_call_target="tpu_custom_call" | custom-call | flops 1277952 | bytes 3194880 | tf_op jit(solution)/shard_map/pallas_call | solution.py:858
  215.6 5.4 %all-to-all-start.3 = ((bf16[16,12,3200]{2,1,0:T(8,128)(2,1)}), bf16[16,12,3200]{2,1,0:T(8,128)(2,1)S(1)}, u32[]{:S(2)}, u32[]{:S(2)}) async-start(bf16[16,12,3200]{2,1,0:T(8,128)(2,1)} %shard_map.348), calls=%async_computation.5 | async-start | bytes 3276800 | tf_op jit(solution)/shard_map/all_to_all | solution.py:74
  221.2 4.3 %shard_map.351 = f32[576,768]{1,0:T(8,128)} custom-call(bf16[576,768]{1,0:T(8,128)(2,1)} %bitcast.44, f32[576,768]{1,0:T(8,128)} %get-tuple-element.142.ga_ref, f32[576,768]{1,0:T(8,128)} %get-tuple-element.143.gh_ref, f32[576,768]{1,0:T(8,128)} %collective-permute-done.15.other_ref, f32[16,768]{1,0:T(8,128)} %get-tuple-element.116.v_ref), custom_call_target="tpu_custom_call" | custom-call | flops 11059200 | bytes 7077888 | tf_op jit(solution)/shard_map/pallas_call | solution.py:834
  225.5 0.7 shard_map.350
  226.2 15.4 %all-to-all-done.3.in_ref = bf16[16,12,3200]{2,1,0:T(8,128)(2,1)S(1)} async-done(((bf16[16,12,3200]{2,1,0:T(8,128)(2,1)}), bf16[16,12,3200]{2,1,0:T(8,128)(2,1)S(1)}, u32[]{:S(2)}, u32[]{:S(2)}) %all-to-all-start.3) | async-done | bytes 1228832 | tf_op jit(solution)/shard_map/all_to_all | solution.py:74
  242.0 1.4 collective-permute-done.16.o_ref.other_ref
  243.4 0.9 shard_map.353
  244.3 9.5 %all-to-all-start.4 = ((f32[64,8,128]{2,1,0:T(8,128)}), f32[64,8,128]{2,1,0:T(8,128)S(1)}, u32[]{:S(2)}, u32[]{:S(2)}) async-start(f32[64,8,128]{2,1,0:T(8,128)} %shard_map.353), calls=%async_computation.6 | async-start | bytes 524288 | tf_op jit(solution)/shard_map/all_to_all | solution.py:1093
  254.0 3.6 %shard_map.354 = bf16[576,768]{1,0:T(8,128)(2,1)} custom-call(f32[576,768]{1,0:T(8,128)} %get-tuple-element.149.after_ref, f32[576,768]{1,0:T(8,128)} %get-tuple-element.150.mlp_ref, f32[576,768]{1,0:T(8,128)} %collective-permute-done.17.mlpo_ref, f32[16,768]{1,0:T(8,128)} %get-tuple-element.116.v_ref), custom_call_target="tpu_custom_call" | custom-call | flops 1769472 | bytes 7077888 | tf_op jit(solution)/shard_map/pallas_call | solution.py:834
  257.6 6.9 %all-to-all-done.4.norm_ref = f32[64,8,128]{2,1,0:T(8,128)S(1)} async-done(((f32[64,8,128]{2,1,0:T(8,128)}), f32[64,8,128]{2,1,0:T(8,128)S(1)}, u32[]{:S(2)}, u32[]{:S(2)}) %all-to-all-start.4) | async-done | bytes 262176 | tf_op jit(solution)/shard_map/all_to_all | solution.py:1093
  264.7 3.8 %shard_map.355 = (f32[12,2304]{1,0:T(8,128)}, f32[12,2304]{1,0:T(8,128)}, f32[12,2304]{1,0:T(8,128)}, f32[12,768]{1,0:T(8,128)}, f32[12,768]{1,0:T(8,128)}, /*in...) custom-call(s32[5]{0:T(128)S(1)} %copy-done.13, ...), custom_call_target="tpu_custom_call" | custom-call | flops 2211840 | bytes 3000000 | tf_op jit(solution)/shard_map/pallas_call | solution.py:977
  (104 shorter events, 4.6 us)
Async XLA Ops:
  7.2 11.6 %copy-start.3 = (f32[12,768]{1,0:T(8,128)S(1)}, f32[12,768]{1,0:T(8,128)}, u32[]{:S(2)}) copy-start(f32[12,768]{1,0:T(8,128)} %refs_1_.1) | copy-start | bytes 110596
  7.2 11.6 %copy-start = (f32[12,3072]{1,0:T(8,128)S(1)}, f32[12,3072]{1,0:T(8,128)}, u32[]{:S(2)}) copy-start(f32[12,3072]{1,0:T(8,128)} %refs_2_.1) | copy-start | bytes 442372
  7.2 109.5 %all-gather.2.cloned.1.call-start = ((), (), s32[]{:S(2)}) async-start(), calls=%async_computation.7 | async-start | bytes 2396160 | tf_op jit(solution)/shard_map/all_gather | solution.py:1030
  10.5 19.6 %all-to-all-start = ((bf16[16,12,1280]{2,1,0:T(8,128)(2,1)}), bf16[16,12,1280]{2,1,0:T(8,128)(2,1)S(1)}, u32[]{:S(2)}, u32[]{:S(2)}) async-start(bf16[16,12,1280]{2,1,0:T(8,128)(2,1)} %get-tuple-element.96), calls=%async_computation | async-start | bytes 1310720 | tf_op jit(solution)/shard_map/all_to_all | solution.py:74
  18.6 33.6 %collective-permute-start.1 = (bf16[576,768]{1,0:T(8,128)(2,1)}, bf16[576,768]{1,0:T(8,128)(2,1)S(1)}, u32[]{:S(2)}, u32[]{:S(2)}) collective-permute-start(bf16[576,768]{1,0:T(8,128)(2,1)} %bitcast.40), channel_id=1, source_target_pairs={{0,64},{64,0},{1,65},{65,1},{2,66},{66,2},{3,67},{67,3},{4,68},{68... | collective-permute-start | bytes 2654216 | tf_op jit(solution)/shard_map/ppermute | solution.py:1020
  31.0 10.3 %collective-permute-start.2 = (bf16[192,1280]{1,0:T(8,128)(2,1)}, bf16[192,1280]{1,0:T(8,128)(2,1)S(1)}, u32[]{:S(2)}, u32[]{:S(2)}) collective-permute-start(bf16[192,1280]{1,0:T(8,128)(2,1)} %reshape.111.w0.v0), channel_id=1, source_target_pairs={{0,16},{16,32},{32,48},{48,0},{1,17},{17,33},{33,49},{49,1},{2,18}... | collective-permute-start | bytes 1474568 | tf_op jit(solution)/shard_map/ppermute | solution.py:70
  33.6 14.0 %copy-start.28 = (s32[1,1,576]{2,1,0:T(1,128)S(1)}, s32[1,1,576]{2,1,0:T(1,128)}, u32[]{:S(2)}) copy-start(s32[1,1,576]{2,1,0:T(1,128)} %param.24) | copy-start | bytes 6916
  33.6 14.0 %copy-start.29 = (s32[1,1,576]{2,1,0:T(1,128)S(1)}, s32[1,1,576]{2,1,0:T(1,128)}, u32[]{:S(2)}) copy-start(s32[1,1,576]{2,1,0:T(1,128)} %param.23) | copy-start | bytes 6916
  33.6 14.0 %copy-start.30 = (s32[1,1,2]{2,1,0:T(1,128)S(1)}, s32[1,1,2]{2,1,0:T(1,128)}, u32[]{:S(2)}) copy-start(s32[1,1,2]{2,1,0:T(1,128)} %param.22) | copy-start | bytes 28
  33.6 18.7 %collective-permute-start.4 = (bf16[192,1280]{1,0:T(8,128)(2,1)}, bf16[192,1280]{1,0:T(8,128)(2,1)S(1)}, u32[]{:S(2)}, u32[]{:S(2)}) collective-permute-start(bf16[192,1280]{1,0:T(8,128)(2,1)} %reshape.111.w0.v0), channel_id=1, source_target_pairs={{0,48},{16,0},{32,16},{48,32},{1,49},{17,1},{33,17},{49,33},{2,50}... | collective-permute-start | bytes 1474568 | tf_op jit(solution)/shard_map/ppermute | solution.py:70
  36.0 16.3 %collective-permute-start.3 = (bf16[192,1280]{1,0:T(8,128)(2,1)}, bf16[192,1280]{1,0:T(8,128)(2,1)}, u32[]{:S(2)}, u32[]{:S(2)}) collective-permute-start(bf16[192,1280]{1,0:T(8,128)(2,1)} %reshape.111.w0.v0), channel_id=1, source_target_pairs={{0,32},{16,48},{32,0},{48,16},{1,33},{17,49},{33,1},{49,17},{2,34}... | collective-permute-start | bytes 1474568 | tf_op jit(solution)/shard_map/ppermute | solution.py:70
  42.6 24.8 %all-to-all-start.1 = ((bf16[16,12,2304]{2,1,0:T(8,128)(2,1)}), bf16[16,12,2304]{2,1,0:T(8,128)(2,1)S(1)}, u32[]{:S(2)}, u32[]{:S(2)}) async-start(bf16[16,12,2304]{2,1,0:T(8,128)(2,1)} %broadcast_in_dim.10), calls=%async_computation.1 | async-start | bytes 2359296 | tf_op jit(solution)/shard_map/all_to_all | solution.py:74
  47.5 143.3 %reduce-scatter.3.cloned.1.call-start = ((), (), s32[]{:S(2)}) async-start(), calls=%async_computation.8 | async-start | bytes 2949120 | tf_op jit(solution)/shard_map/reduce_scatter | solution.py:1026
  47.7 1.6 collective-permute-start
  47.7 35.1 %collective-permute-start.7 = (bf16[576,768]{1,0:T(8,128)(2,1)}, bf16[576,768]{1,0:T(8,128)(2,1)}, u32[]{:S(2)}, u32[]{:S(2)}) collective-permute-start(bf16[576,768]{1,0:T(8,128)(2,1)} %bitcast.15.c_ref), channel_id=1, source_target_pairs={{0,64},{64,0},{1,65},{65,1},{2,66},{66,2},{3,67},{67,3},{4,68},{68... | collective-permute-start | bytes 2654216 | tf_op jit(solution)/shard_map/ppermute | solution.py:1020
  67.6 24.7 %copy-start.16 = (bf16[192,2304]{1,0:T(8,128)(2,1)}, bf16[192,2304]{1,0:T(8,128)(2,1)S(1)}, u32[]{:S(2)}) copy-start(bf16[192,2304]{1,0:T(8,128)(2,1)S(1)} %reshape.113.w0.w10.y0) | copy-start | bytes 2654212
  67.6 20.9 %collective-permute-start.6 = (bf16[192,2304]{1,0:T(8,128)(2,1)S(1)}, bf16[192,2304]{1,0:T(8,128)(2,1)S(1)}, u32[]{:S(2)}, u32[]{:S(2)}) collective-permute-start(bf16[192,2304]{1,0:T(8,128)(2,1)S(1)} %reshape.113.w0.w10.y0), channel_id=1, source_target_pairs={{0,48},{16,0},{32,16},{48,32},{1,49},{17,1},{33,17},{49,33},{2,50}... | collective-permute-start | bytes 2654216 | tf_op jit(solution)/shard_map/ppermute | solution.py:70
  71.6 20.6 %collective-permute-start.5 = (bf16[192,2304]{1,0:T(8,128)(2,1)S(1)}, bf16[192,2304]{1,0:T(8,128)(2,1)S(1)}, u32[]{:S(2)}, u32[]{:S(2)}) collective-permute-start(bf16[192,2304]{1,0:T(8,128)(2,1)S(1)} %reshape.113.w0.w10.y0), channel_id=1, source_target_pairs={{0,16},{16,32},{32,48},{48,0},{1,17},{17,33},{33,49},{49,1},{2,18}... | collective-permute-start | bytes 2654216 | tf_op jit(solution)/shard_map/ppermute | solution.py:70
  88.4 7.5 %copy-start.18 = (bf16[192,2304]{1,0:T(8,128)(2,1)}, bf16[192,2304]{1,0:T(8,128)(2,1)S(1)}, u32[]{:S(2)}) copy-start(bf16[192,2304]{1,0:T(8,128)(2,1)S(1)} %collective-permute-done.6.w3.w13.y3) | copy-start | bytes 2654212
  92.1 3.9 %collective-permute-start.8 = (bf16[2,576,384]{2,1,0:T(8,128)(2,1)}, bf16[2,576,384]{2,1,0:T(8,128)(2,1)S(1)}, u32[]{:S(2)}, u32[]{:S(2)}) collective-permute-start(bf16[2,576,384]{2,1,0:T(8,128)(2,1)} %get-tuple-element.105.mine_ref.o0.o1), channel_id=1, source_target_pairs={{0,64},{64,0},{1,65},{65,1},{2,66},{66,2},{3,67},{67,3},{4,68},{68... | collective-permute-start | bytes 2654216 | tf_op jit(solution)/shard_map/ppermute | solution.py:1020
  92.3 14.6 %collective-permute-start.9 = (bf16[192,2304]{1,0:T(8,128)(2,1)S(1)}, bf16[192,2304]{1,0:T(8,128)(2,1)S(1)}, u32[]{:S(2)}, u32[]{:S(2)}) collective-permute-start(bf16[192,2304]{1,0:T(8,128)(2,1)S(1)} %reshape.113.w0.w10.y0), channel_id=1, source_target_pairs={{0,32},{16,48},{32,0},{48,16},{1,33},{17,49},{33,1},{49,17},{2,34}... | collective-permute-start | bytes 2654216 | tf_op jit(solution)/shard_map/ppermute | solution.py:70
  96.0 11.0 %copy-start.20 = (bf16[2,576,384]{2,1,0:T(8,128)(2,1)}, bf16[2,576,384]{2,1,0:T(8,128)(2,1)S(1)}, u32[]{:S(2)}) copy-start(bf16[2,576,384]{2,1,0:T(8,128)(2,1)S(1)} %collective-permute-done.8.other_ref) | copy-start | bytes 2654212
  135.4 7.7 %collective-permute-start.10 = (bf16[1152,768]{1,0:T(8,128)(2,1)}, bf16[1152,768]{1,0:T(8,128)(2,1)S(1)}, u32[]{:S(2)}, u32[]{:S(2)}) collective-permute-start(bf16[1152,768]{1,0:T(8,128)(2,1)} %get-tuple-element.124.gh2_ref), channel_id=1, source_target_pairs={{0,64},{64,0},{1,65},{65,1},{2,66},{66,2},{3,67},{67,3},{4,68},{68... | collective-permute-start | bytes 5308424 | tf_op jit(solution)/shard_map/ppermute | solution.py:1020
  143.1 53.8 %reduce-scatter.5.cloned.1.call-start = ((), (), s32[]{:S(2)}) async-start(), calls=%async_computation.9 | async-start | bytes 2949120 | tf_op jit(solution)/shard_map/reduce_scatter | solution.py:1026
  185.5 25.4 %collective-permute-start.11 = (bf16[192,1664]{1,0:T(8,128)(2,1)}, bf16[192,1664]{1,0:T(8,128)(2,1)S(1)}, u32[]{:S(2)}, u32[]{:S(2)}) collective-permute-start(bf16[192,1664]{1,0:T(8,128)(2,1)} %get-tuple-element.131), channel_id=1, source_target_pairs={{0,16},{16,32},{32,48},{48,0},{1,17},{17,33},{33,49},{49,1},{2,18}... | collective-permute-start | bytes 1916936 | tf_op jit(solution)/shard_map/ppermute | solution.py:70
  185.6 25.3 %collective-permute-start.12 = (bf16[192,1664]{1,0:T(8,128)(2,1)}, bf16[192,1664]{1,0:T(8,128)(2,1)S(1)}, u32[]{:S(2)}, u32[]{:S(2)}) collective-permute-start(bf16[192,1664]{1,0:T(8,128)(2,1)} %get-tuple-element.132), channel_id=1, source_target_pairs={{0,32},{16,48},{32,0},{48,16},{1,33},{17,49},{33,1},{49,17},{2,34}... | collective-permute-start | bytes 1916936 | tf_op jit(solution)/shard_map/ppermute | solution.py:70
  187.0 24.0 %collective-permute-start.13 = (bf16[192,1664]{1,0:T(8,128)(2,1)}, bf16[192,1664]{1,0:T(8,128)(2,1)S(1)}, u32[]{:S(2)}, u32[]{:S(2)}) collective-permute-start(bf16[192,1664]{1,0:T(8,128)(2,1)} %get-tuple-element.133), channel_id=1, source_target_pairs={{0,48},{16,0},{32,16},{48,32},{1,49},{17,1},{33,17},{49,33},{2,50}... | collective-permute-start | bytes 1916936 | tf_op jit(solution)/shard_map/ppermute | solution.py:70
  188.8 32.3 %collective-permute-start.15 = (f32[576,768]{1,0:T(8,128)}, f32[576,768]{1,0:T(8,128)}, u32[]{:S(2)}, u32[]{:S(2)}) collective-permute-start(f32[576,768]{1,0:T(8,128)} %get-tuple-element.144), channel_id=1, source_target_pairs={{0,64},{64,0},{1,65},{65,1},{2,66},{66,2},{3,67},{67,3},{4,68},{68... | collective-permute-start | bytes 5308424 | tf_op jit(solution)/shard_map/ppermute | solution.py:1020
  190.8 20.2 %all-to-all-start.2 = ((bf16[16,24,768]{2,1,0:T(8,128)(2,1)}), bf16[16,24,768]{2,1,0:T(8,128)(2,1)S(1)}, u32[]{:S(2)}, u32[]{:S(2)}) async-start(bf16[16,24,768]{2,1,0:T(8,128)(2,1)} %bitcast.55), calls=%async_computation.3 | async-start | bytes 1179648 | tf_op jit(solution)/shard_map/all_to_all | solution.py:74
  196.0 57.9 %collective-permute-start.17 = (f32[576,768]{1,0:T(8,128)}, f32[576,768]{1,0:T(8,128)}, u32[]{:S(2)}, u32[]{:S(2)}) collective-permute-start(f32[576,768]{1,0:T(8,128)} %get-tuple-element.151), channel_id=1, source_target_pairs={{0,64},{64,0},{1,65},{65,1},{2,66},{66,2},{3,67},{67,3},{4,68},{68... | collective-permute-start | bytes 5308424 | tf_op jit(solution)/shard_map/ppermute | solution.py:1020
  215.6 26.0 %all-to-all-start.3 = ((bf16[16,12,3200]{2,1,0:T(8,128)(2,1)}), bf16[16,12,3200]{2,1,0:T(8,128)(2,1)S(1)}, u32[]{:S(2)}, u32[]{:S(2)}) async-start(bf16[16,12,3200]{2,1,0:T(8,128)(2,1)} %shard_map.348), calls=%async_computation.5 | async-start | bytes 3276800 | tf_op jit(solution)/shard_map/all_to_all | solution.py:74
  221.1 4.4 %collective-permute-start.14 = (f32[24,768]{1,0:T(8,128)S(1)}, f32[24,768]{1,0:T(8,128)S(1)}, u32[]{:S(2)}, u32[]{:S(2)}) collective-permute-start(f32[24,768]{1,0:T(8,128)S(1)} %shard_map.349.mine_ref), channel_id=1, source_target_pairs={{0,64},{64,0},{1,65},{65,1},{2,66},{66,2},{3,67},{67,3},{4,68},{68... | collective-permute-start | bytes 221192 | tf_op jit(solution)/shard_map/ppermute | solution.py:1020
  221.2 4.3 %copy-start.13 = (s32[5]{0:T(128)S(1)}, s32[5]{0:T(128)}, u32[]{:S(2)}) copy-start(s32[5]{0:T(128)} %pad_add_fusion.2.place_ref) | copy-start | bytes 64
  241.9 1.5 collective-permute-start.16
  244.3 20.2 %all-to-all-start.4 = ((f32[64,8,128]{2,1,0:T(8,128)}), f32[64,8,128]{2,1,0:T(8,128)S(1)}, u32[]{:S(2)}, u32[]{:S(2)}) async-start(f32[64,8,128]{2,1,0:T(8,128)} %shard_map.353), calls=%async_computation.6 | async-start | bytes 524288 | tf_op jit(solution)/shard_map/all_to_all | solution.py:1093
  253.9 10.7 %copy-start.1 = (f32[12,2304]{1,0:T(8,128)S(1)}, f32[12,2304]{1,0:T(8,128)}, u32[]{:S(2)}) copy-start(f32[12,2304]{1,0:T(8,128)} %refs_0_.1) | copy-start | bytes 331780
  253.9 10.7 %copy-start.2 = (f32[48,768]{1,0:T(8,128)S(1)}, f32[48,768]{1,0:T(8,128)}, u32[]{:S(2)}) copy-start(f32[48,768]{1,0:T(8,128)} %refs_3_.1) | copy-start | bytes 442372
  253.9 10.7 %copy-start.4 = (f32[12,3072]{1,0:T(8,128)S(1)}, f32[12,3072]{1,0:T(8,128)}, u32[]{:S(2)}) copy-start(f32[12,3072]{1,0:T(8,128)} %refs_7_.1) | copy-start | bytes 442372
  253.9 10.7 %copy-start.5 = (f32[12,3072]{1,0:T(8,128)S(1)}, f32[12,3072]{1,0:T(8,128)}, u32[]{:S(2)}) copy-start(f32[12,3072]{1,0:T(8,128)} %refs_12_.1) | copy-start | bytes 442372
  253.9 10.7 %copy-start.6 = (f32[12,2304]{1,0:T(8,128)S(1)}, f32[12,2304]{1,0:T(8,128)}, u32[]{:S(2)}) copy-start(f32[12,2304]{1,0:T(8,128)} %refs_5_.1) | copy-start | bytes 331780
  253.9 10.7 %copy-start.7 = (f32[48,768]{1,0:T(8,128)S(1)}, f32[48,768]{1,0:T(8,128)}, u32[]{:S(2)}) copy-start(f32[48,768]{1,0:T(8,128)} %refs_8_.1) | copy-start | bytes 442372
  253.9 10.7 %copy-start.8 = (f32[12,2304]{1,0:T(8,128)S(1)}, f32[12,2304]{1,0:T(8,128)}, u32[]{:S(2)}) copy-start(f32[12,2304]{1,0:T(8,128)} %refs_10_.1) | copy-start | bytes 331780
  254.0 10.7 %copy-start.9 = (f32[48,768]{1,0:T(8,128)S(1)}, f32[48,768]{1,0:T(8,128)}, u32[]{:S(2)}) copy-start(f32[48,768]{1,0:T(8,128)} %refs_13_.1) | copy-start | bytes 442372
  254.0 10.7 %copy-start.10 = (f32[12,768]{1,0:T(8,128)S(1)}, f32[12,768]{1,0:T(8,128)}, u32[]{:S(2)}) copy-start(f32[12,768]{1,0:T(8,128)} %refs_6_.1) | copy-start | bytes 110596
  254.0 10.7 %copy-start.11 = (f32[12,768]{1,0:T(8,128)S(1)}, f32[12,768]{1,0:T(8,128)}, u32[]{:S(2)}) copy-start(f32[12,768]{1,0:T(8,128)} %refs_11_.1) | copy-start | bytes 110596
  254.0 10.7 %copy-start.12 = (f32[14,12]{1,0:T(8,128)S(1)}, f32[14,12]{1,0:T(8,128)}, u32[]{:S(2)}) copy-start(f32[14,12]{1,0:T(8,128)} %refs_4_.1) | copy-start | bytes 2020
  254.0 10.7 %copy-start.14 = (f32[14,12]{1,0:T(8,128)S(1)}, f32[14,12]{1,0:T(8,128)}, u32[]{:S(2)}) copy-start(f32[14,12]{1,0:T(8,128)} %refs_9_.1) | copy-start | bytes 2020
  254.0 10.7 %copy-start.15 = (f32[14,12]{1,0:T(8,128)S(1)}, f32[14,12]{1,0:T(8,128)}, u32[]{:S(2)}) copy-start(f32[14,12]{1,0:T(8,128)} %refs_14_.1) | copy-start | bytes 2020
  (9 other events, 12.3 us)
Sparse Core Ops, SparseCore 0:
  11.5 79.8 all-gather.1
  143.2 23.9 reduce-scatter.2
  169.6 27.2 reduce-scatter.4

commit v5 on v4

--- a/solution.py
+++ b/solution.py
@@ -78,13 +78,18 @@
     return jnp.where(core == 0, SIDE * a + g, SIDE * g + a)
 
 
-def lay_out(place_ref, pieces, full_ref):
+def lay_out(place_ref, pieces, full_ref, cols=slice(None)):
     core, me = place_ref[0], place_ref[1]
     for d, piece in enumerate(pieces):
         a = (me + SIDE - d) & (SIDE - 1)
         for g in range(SIDE):
             at = pl.multiple_of(natural(core, a, g) * BLOCK, BLOCK)
-            full_ref[pl.ds(at, BLOCK), :] = piece[g * BLOCK : (g + 1) * BLOCK, :]
+            full_ref[pl.ds(at, BLOCK), :] = piece[g * BLOCK : (g + 1) * BLOCK, cols]
+
+
+QKV = slice(0, 3 * DC)
+PROJ = slice(3 * DC + 128, 3 * DC + 128 + D)
+SHARE = 3 * DC + 128 + D
 
 
 def usable_rows(place_ref, group, rows, base=0):
@@ -198,7 +203,7 @@
     return sine, cosine
 
 
-def share_kernel(place_ref, w_ref, v_ref, f_ref, out_ref, fc2_ref):
+def share_kernel(place_ref, w_ref, v_ref, p_ref, f_ref, out_ref, fc2_ref):
     core = place_ref[0]
     w = w_ref[...].astype(bf16)
     cols = []
@@ -209,32 +214,33 @@
     v = jnp.concatenate([v_ref[...], jnp.zeros((128 - v_ref.shape[0], KR), f32)], axis=0)
     v = jnp.concatenate([v, jnp.zeros((128, 128 - KR), f32)], axis=1)
     cols.append(v.T[:KR, :].astype(bf16))
+    cols.append(p_ref[...].astype(bf16))
     share = jnp.concatenate(cols, axis=1)
     for n in range(PLANE):
         out_ref[n] = share
     fc2_ref[...] = jnp.where(core == 0, f_ref[:FR, :], f_ref[FR:, :]).astype(bf16)
 
 
-def share_call(place, w, vectors, w_fc2):
+def share_call(place, w, vectors, w_proj, w_fc2):
     whole = lambda a: pl.BlockSpec(a.shape, lambda i, c: (0, 0))
     return pl.pallas_call(
         share_kernel,
         grid_spec=pltpu.PrefetchScalarGridSpec(
             num_scalar_prefetch=1,
             grid=(1,),
-            in_specs=[whole(w), whole(vectors), whole(w_fc2)],
+            in_specs=[whole(a) for a in (w, vectors, w_proj, w_fc2)],
             out_specs=[
-                pl.BlockSpec((PLANE, KR, 3 * DC + 128), lambda i, c: (0, 0, 0)),
+                pl.BlockSpec((PLANE, KR, SHARE), lambda i, c: (0, 0, 0)),
                 pl.BlockSpec((FR, D), lambda i, c: (0, 0)),
             ],
         ),
         out_shape=[
-            jax.ShapeDtypeStruct((PLANE, KR, 3 * DC + 128), bf16),
+            jax.ShapeDtypeStruct((PLANE, KR, SHARE), bf16),
             jax.ShapeDtypeStruct((FR, D), bf16),
         ],
         compiler_params=params(),
         cost_estimate=cost(KR * D * 3, 1e6),
-    )(place, w, vectors, w_fc2)
+    )(place, w, vectors, w_proj, w_fc2)
 
 
 def gy_kernel(place_ref, c_ref, co_ref, gy_ref):
@@ -417,7 +423,7 @@
 def proj_kernel(place_ref, mine_ref, other_ref, x_ref, xo_ref, w0, w1, w2, w3, v_ref, after_ref, n2_ref, r2_ref, h2_ref, w_s):
     @pl.when(pl.program_id(0) == 0)
     def _():
-        lay_out(place_ref, (w0, w1, w2, w3), w_s)
+        lay_out(place_ref, (w0, w1, w2, w3), w_s, PROJ)
 
     core = place_ref[0]
     at = lambda c: pl.ds(pl.multiple_of(c * DC, DC), DC)
@@ -451,7 +457,7 @@
                 pl.BlockSpec((rows, D), lambda i, c: (jnp.minimum(i, half - 1), 0)),
                 pl.BlockSpec((rows, D), lambda i, c: (jnp.maximum(i - half, 0), 0)),
             ]
-            + [pl.BlockSpec((QUARTER, D), lambda i, c: (0, FC // D))] * 4
+            + [whole(a) for a in pieces]
             + [whole(vec)],
             out_specs=[pl.BlockSpec((rows, D), lambda i, c: (jnp.minimum(i, half - 1), 0)), tile(D), tile(8), tile(D)],
             scratch_shapes=[pltpu.VMEM((D, D), bf16)],
@@ -656,7 +662,7 @@
     place_ref,
     q0, k0, v0, o0, p0, cos0, sin0, pos0,
     q1, k1, v1, o1, p1, cos1, sin1, pos1,
-    h1t_ref, ga_ref, cols_ref, mine_ref, other_ref, y0, y1, y2, y3, w0, w1, w2, w3,
+    h1t_ref, ga_ref, cols_ref, mine_ref, other_ref, w0, w1, w2, w3,
     x_ref, xo_ref, mid_ref, gb1_ref,
     gw0, gw1, gw2, gw3, gh_ref, gho_ref,
     gq_s, gk_s, gv_s, gw_s, y_s, do_s, gqkv_s, att_s, rows_s, full_s, w_s,
@@ -668,7 +674,7 @@
 
     @pl.when(pair == 0)
     def _():
-        lay_out(place_ref, (y0, y1, y2, y3), y_s)
+        lay_out(place_ref, (w0, w1, w2, w3), y_s, PROJ)
 
     wy = y_s[pl.ds(pl.multiple_of(core * DC + pair * 2 * HD, 2 * HD), 2 * HD), :]
     for frame in range(CORES):
@@ -737,7 +743,7 @@
 
     @pl.when(pair == PAIRS - 1)
     def _():
-        lay_out(place_ref, (w0, w1, w2, w3), w_s)
+        lay_out(place_ref, (w0, w1, w2, w3), w_s, QKV)
         rows_s[...] = jnp.zeros_like(rows_s)
         for frame, x, out in ((0, x_ref, gh_ref), (1, xo_ref, gho_ref)):
             for half in range(2):
@@ -772,7 +778,7 @@
 
 
 def attn_bwd_call(
-    place, q, k, v, ga, mine, other, p0, p1, cosine, sine, pos, h1t, pieces, proj_pieces, x, xo, mid, gb1
+    place, q, k, v, ga, mine, other, p0, p1, cosine, sine, pos, h1t, pieces, x, xo, mid, gb1
 ):
     q, k, v, cosine, sine, pos, ga = (a.reshape(CORES, S, -1) for a in (q, k, v, cosine, sine, pos, ga))
     block = lambda g: pl.BlockSpec((1, S, 2 * HD), lambda p, c: (g ^ c[0], 0, p))
@@ -796,8 +802,7 @@
             + [whole(h1t), whole(ga)]
             + [pl.BlockSpec((CORES, S, 2 * HD), lambda p, c: (0, 0, PAIRS * c[0] + p))]
             + [whole(mine), whole(other)]
-            + [pl.BlockSpec((QUARTER, D), lambda p, c: (0, FC // D))] * 4
-            + [keep(QUARTER, 3 * DC)] * 4
+            + [whole(a) for a in pieces]
             + [whole(a) for a in (x, xo, mid, gb1)],
             out_specs=[keep(QUARTER, PACK)] * 4 + [keep(S, D)] * 2,
             scratch_shapes=[pltpu.VMEM((S, 2 * HD), f32)] * 3
@@ -815,7 +820,7 @@
         place,
         q, k, v, mine, p0, cosine, sine, pos,
         q, k, v, mine, p1, cosine, sine, pos,
-        h1t, ga, ga, mine, other, *proj_pieces, *pieces, x, xo, mid, gb1,
+        h1t, ga, ga, mine, other, *pieces, x, xo, mid, gb1,
     )
 
 
@@ -1026,16 +1031,15 @@
         return lax.psum_scatter(whole, BOTH, scatter_dimension=0, axis_index_groups=lines(), tiled=True)
 
     me = jnp.stack([core, along]).astype(jnp.int32)
-    shares, share_fc2 = share_call(me, w_qkv, vectors, w_fc2)
+    shares, share_fc2 = share_call(me, w_qkv, vectors, w_proj, w_fc2)
     full_fc2 = lax.all_gather(share_fc2, "dp", axis=0, tiled=True)
-    quarter = plane_swap(shares).reshape(QUARTER, 3 * DC + 128)
+    quarter = plane_swap(shares).reshape(QUARTER, SHARE)
     qkv_pieces = along_line(quarter)
     fc1_b = w_fc1.astype(bf16).reshape(KR, CHIPS, CORES, FR)
     share_fc1 = jnp.where(first_core, fc1_b[:, :, 0], fc1_b[:, :, 1]).reshape(KR, FC)
-    share = jnp.concatenate([share_fc1, w_proj.astype(bf16)], axis=1)
-    share = jnp.broadcast_to(share[None], (PLANE,) + share.shape)
+    share = jnp.broadcast_to(share_fc1[None], (PLANE, KR, FC))
     share, qkv_pieces[1] = lax.optimization_barrier((share, qkv_pieces[1]))
-    quarter = plane_swap(share).reshape(QUARTER, FC + D)
+    quarter = plane_swap(share).reshape(QUARTER, FC)
 
     x_own = tokens.reshape(S, D)
     cot_own = cotangent.reshape(S, D)
@@ -1061,7 +1065,7 @@
     other = swap(mine)
     gy = gy_call(place, cot_own, cot_other)
     other, gy = lax.optimization_barrier((other, gy))
-    after, n2, r2, h2 = proj_call(place, mine, other, x_own, x_other, pieces, vec)
+    after, n2, r2, h2 = proj_call(place, mine, other, x_own, x_other, qkv_pieces, vec)
     mlp, mlp_part, gh2, act, gup, gb1 = mlp_call(place, h2, gy, pieces, full_fc2, b1)
     other_gh2 = swap(gh2)
     mlp_other = swap(mlp_part)
@@ -1072,17 +1076,17 @@
     gw1, ga, gab, sums_mid = mid_call(place, h2, gup, n2, r2, gy, gh2, other_gh2, vec)
     sum_fc1 = line_sum(gw1)
     *gw, gh1, gh1_part = attn_bwd_call(
-        place, q, k, v, gab, mine, other, p0, p1, cosine, sine, pos, h1t, qkv_pieces, pieces,
+        place, q, k, v, gab, mine, other, p0, p1, cosine, sine, pos, h1t, qkv_pieces,
         x_own, x_other, sums_mid, gb1,
     )
-    gh1_other = swap(gh1_part)
 
     got_fc2 = plane_swap(sum_fc2.reshape(PLANE, FR, D))
     parts = [gw[0]] + [shift(gw[d], d) for d in range(1, SIDE)]
     got_fc2, sum_fc1 = lax.optimization_barrier((got_fc2, sum_fc1))
     g_fc2 = sum_call(got_fc2)
     g2, squares = fc2_call(place, g_fc2, swap(g_fc2))
-    packed, gh1 = lax.optimization_barrier((pack_call(parts, sum_fc1), gh1))
+    packed, gh1, gh1_part = lax.optimization_barrier((pack_call(parts, sum_fc1), gh1, gh1_part))
+    gh1_other = swap(gh1_part)
     got = plane_swap(packed)
     gt = by_rows(last_kernel, f32, 25, x_own, ga, gh1, gh1_other, vec)
     got, g2, squares, gt = lax.optimization_barrier((got, g2, squares, gt))

time: 280 us -> 282 us (level); the launches traced: 275 us -> 283 us
  waiting for transfers between devices: 73.5 us -> 49.9 us
  blocking collectives: 0 us -> 23.2 us
  starting transfers between devices: 49.2 us -> 56.5 us
    all_to_all x0 -> x1, blocking collectives: none -> 23.2 us  [plane_swap(): return lax.all_to_all(value, BOTH, 0, 0, axis_index_groups=planes())]
    ppermute x9, waiting for transfers between devices: 24.3 us -> 10.6 us  [shift(): return lax.ppermute(value, BOTH, pairs)]
    all_to_all x4 -> x3, waiting for transfers between devices: 40.2 us -> 28.7 us  [plane_swap(): return lax.all_to_all(value, BOTH, 0, 0, axis_index_groups=planes())]
    ppermute x9, starting transfers between devices: 3.8 us -> 14.6 us  [swap(): return lax.ppermute(a, 'grp', [(0, 1), (1, 0)])]
    all_to_all x4 -> x3, starting transfers between devices: 23.6 us -> 17 us  [plane_swap(): return lax.all_to_all(value, BOTH, 0, 0, axis_index_groups=planes())]
    ppermute x9, starting transfers between devices: 11.9 us -> 15.7 us  [shift(): return lax.ppermute(value, BOTH, pairs)]
  transfers between devices with their start and end apart: 26 -> 25, of which waited for: 10 -> 9; matrix products, arithmetic and copies ran while one was open for 3% -> 3% of each run, Pallas kernels for 36% -> 34%
where the time goes in v5:
time: 282 us; the launch traced here: 283 us
  Pallas kernels  125 us (44%)
  starting transfers between devices  56.5 us (20%)
  waiting for transfers between devices  49.9 us (18%)
  blocking collectives  23.2 us (8%)
  between operations  15.9 us (6%)
  local copies, waits for them, and re-layouts  8.8 us (3%)
  other arithmetic  3.33 us (1%)
    all_to_all x3, waiting for transfers between devices, plane_swap(): return lax.all_to_all(value, BOTH, 0, 0, axis_index_groups=planes())  28.7 us
    pallas_call x1, Pallas kernels, attn_bwd_call(): pl.pallas_call(attn_bwd_kernel, grid_spec=pltpu.PrefetchScalarGridSpec(nu...  28.4 us
    all_to_all x1, blocking collectives, plane_swap(): return lax.all_to_all(value, BOTH, 0, 0, axis_index_groups=planes())  23.2 us
    pallas_call x1, Pallas kernels, mlp_call(): pl.pallas_call(mlp_kernel, grid_spec=pltpu.PrefetchScalarGridSpec(num_sca...  18.6 us
    all_to_all x3, starting transfers between devices, plane_swap(): return lax.all_to_all(value, BOTH, 0, 0, axis_index_groups=planes())  17 us
    ppermute x9, starting transfers between devices, shift(): return lax.ppermute(value, BOTH, pairs)  15.7 us
    ppermute x9, starting transfers between devices, swap(): return lax.ppermute(a, 'grp', [(0, 1), (1, 0)])  14.6 us
    pallas_call x1, Pallas kernels, qkv_call(): pl.pallas_call(qkv_kernel, grid_spec=pltpu.PrefetchScalarGridSpec(num_sca...  14 us
  transfers between devices with their start and end apart: 25, of which 9 were waited for; matrix products, arithmetic and copies ran while one was open for 3% of the time, Pallas kernels for 34%

profile of v5, /device:TPU:0, one launch (start us, length us, event | category | flops | bytes accessed | tf_op | source)
XLA Modules:
  0.0 283.1 jit_solution(9275711141495360781)
XLA Ops:
  7.9 2.7 shard_map.339
  10.7 23.2 %all_to_all.25 = bf16[16,12,2048]{2,1,0:T(8,128)(2,1)} all-to-all(bf16[16,12,2048]{2,1,0:T(8,128)(2,1)} %get-tuple-element.97), channel_id=1, replica_groups={{0,1,2,3,4,5,6,7,8,9,10,11,12,13,14,15},{16,17,18,19,20,21,22,23,24,25,..., dimensions={0} | all-to-all | bytes 1572864 | tf_op jit(solution)/shard_map/all_to_all | solution.py:74
  33.9 1.3 reshape.116.w0.v0
  35.3 1.4 collective-permute-start.2
  36.7 2.0 collective-permute-start.4
  38.6 1.6 collective-permute-start.3
  40.4 0.6 reshape.117
  41.0 1.4 fusion
  43.2 5.3 %collective-permute-done.2.w1.v1 = bf16[192,2048]{1,0:T(8,128)(2,1)S(1)} collective-permute-done((bf16[192,2048]{1,0:T(8,128)(2,1)S(1)}, bf16[192,2048]{1,0:T(8,128)(2,1)S(1)}, u32[]{:S(2)}, u32[]{:S(2)}) %collective-permute-start.2) | collective-permute-done | bytes 786464 | tf_op jit(solution)/shard_map/ppermute | solution.py:70
  48.6 1.1 broadcast_in_dim.9
  49.6 7.4 %all-to-all-start.1 = ((bf16[16,12,1536]{2,1,0:T(8,128)(2,1)}), bf16[16,12,1536]{2,1,0:T(8,128)(2,1)S(1)}, u32[]{:S(2)}, u32[]{:S(2)}) async-start(bf16[16,12,1536]{2,1,0:T(8,128)(2,1)} %broadcast_in_dim.9), calls=%async_computation.1 | async-start | bytes 1572864 | tf_op jit(solution)/shard_map/all_to_all | solution.py:74
  57.5 0.6 pad_add_fusion.ints_ref
  60.5 14.0 %shard_map.340 = (f32[16,768]{1,0:T(8,128)}, bf16[2,768,576]{2,1,0:T(8,128)(2,1)}, f32[1152,384]{1,0:T(8,128)}, f32[1152,384]{1,0:T(8,128)}, bf16[1152,384]{1,0:...) custom-call(s32[5]{0:T(128)} %pad_add_fusion.2.place_ref, ...), custom_call_target="tpu_custom_call" | custom-call | flops 2064973824 | bytes 13271040 | tf_op jit(solution)/shard_map/pallas_call | solution.py:328
  74.7 2.7 collective-permute-start.6
  77.4 11.3 %shard_map.341 = (bf16[2,576,384]{2,1,0:T(8,128)(2,1)}, bf16[6,2,208,208]{3,2,1,0:T(8,128)(2,1)}, bf16[6,576,576]{2,1,0:T(8,128)(2,1)}) custom-call(s32[5]{0:T(128)} %pad_add_fusion.2.place_ref, bf16[2,576,384]{2,1,0:T(8,128)(2,1)} %bitcast.28, bf16[2,576,384]{2,1,0:T(8,128)(2,1)} %bitcast.32, bf16[2,576,384]{2,1,0:T(8,128)(2,1)} %bitcast.36, ...), custom_call_target="tpu_custom_call" | custom-call | flops 1285029888 | bytes 12000000 | tf_op jit(solution)/shard_map/pallas_call | solution.py:401
  88.7 1.1 collective-permute-done.6.w13
  89.8 4.1 %collective-permute-done.5.w11 = bf16[192,1536]{1,0:T(8,128)(2,1)S(1)} collective-permute-done((bf16[192,1536]{1,0:T(8,128)(2,1)S(1)}, bf16[192,1536]{1,0:T(8,128)(2,1)S(1)}, u32[]{:S(2)}, u32[]{:S(2)}) %collective-permute-start.5) | collective-permute-done | bytes 589856 | tf_op jit(solution)/shard_map/ppermute | solution.py:70
  94.0 12.7 %collective-permute-start.8 = (bf16[2,576,384]{2,1,0:T(8,128)(2,1)}, bf16[2,576,384]{2,1,0:T(8,128)(2,1)S(1)}, u32[]{:S(2)}, u32[]{:S(2)}) collective-permute-start(bf16[2,576,384]{2,1,0:T(8,128)(2,1)} %get-tuple-element.106.mine_ref.o0.o1), channel_id=1, source_target_pairs={{0,64},{64,0},{1,65},{65,1},{2,66},{66,2},{3,67},{67,3},{4,68},{68... | collective-permute-start | bytes 2654216 | tf_op jit(solution)/shard_map/ppermute | solution.py:1025
  106.7 2.8 collective-permute-start.9
  109.5 3.5 %shard_map.342.gy_ref = bf16[1152,768]{1,0:T(8,128)(2,1)} custom-call(s32[5]{0:T(128)} %pad_add_fusion.2.place_ref, bf16[576,768]{1,0:T(8,128)(2,1)} %bitcast.56, bf16[576,768]{1,0:T(8,128)(2,1)} %collective-permute-done.7.co_ref), custom_call_target="tpu_custom_call" | custom-call | flops 3538944 | bytes 3538944 | tf_op jit(solution)/shard_map/pallas_call | solution.py:254
  113.1 0.9 copy-done.19
  114.0 9.3 %shard_map.343 = (f32[576,768]{1,0:T(8,128)}, f32[1152,768]{1,0:T(8,128)}, f32[1152,8]{1,0:T(8,128)}, bf16[1152,768]{1,0:T(8,128)(2,1)}) custom-call(s32[5]{0:T(128)} %pad_add_fusion.2.place_ref, bf16[2,576,384]{2,1,0:T(8,128)(2,1)} %get-tuple-element.106.mine_ref.o0.o1, bf16[2,576,384]{2,1,0:T(8,128)(2,1)} %copy-done.19, bf16[576,768]{1,0:T(8,128)(2,1)} %bitcast.41, ...), custom_call_target="tpu_custom_call" | custom-call | flops 1358954496 | bytes 10027008 | tf_op jit(solution)/shard_map/pallas_call | solution.py:449
  123.4 0.8 copy-done.30
  124.2 18.6 %shard_map.344 = (f32[576,768]{1,0:T(8,128)}, f32[576,768]{1,0:T(8,128)}, bf16[1152,768]{1,0:T(8,128)(2,1)}, bf16[1152,1536]{1,0:T(8,128)(2,1)}, bf16[1152,1536]{1,0:T(8,128)(2,1)}, /*index=5*/f32[1,1536]{1,0:T(1,128)}) custom-call(s32[5]{0:T(128)} %pad_add_fusion.2.place_ref, bf16[1152,768]{1,0:T(8,128)(2,1)} %get-tuple-element.116.h2_ref, ...), custom_call_target="tpu_custom_call" | custom-call | flops 10871635968 | bytes 30000000 | tf_op jit(solution)/shard_map/pallas_call | solution.py:523
  143.2 7.6 %shard_map.345 = bf16[1536,768]{1,0:T(8,128)(2,1)} custom-call(s32[5]{0:T(128)} %pad_add_fusion.2.place_ref, bf16[1152,1536]{1,0:T(8,128)(2,1)} %get-tuple-element.126.act_ref, bf16[1152,768]{1,0:T(8,128)(2,1)} %shard_map.342.gy_ref), custom_call_target="tpu_custom_call" | custom-call | flops 2717908992 | bytes 7667712 | tf_op jit(solution)/shard_map/pallas_call | solution.py:571
  150.9 1.2 copy-done.20
  152.1 12.9 %shard_map.346 = (bf16[768,1536]{1,0:T(8,128)(2,1)}, f32[576,768]{1,0:T(8,128)}, bf16[1152,768]{1,0:T(8,128)(2,1)}, f32[8,768]{1,0:T(8,128)}) custom-call(s32[5]{0:T(128)} %pad_add_fusion.2.place_ref, bf16[1152,768]{1,0:T(8,128)(2,1)} %get-tuple-element.116.h2_ref, bf16[1152,1536]{1,0:T(8,128)(2,1)} %get-tuple-element.122.gup_ref, ...), custom_call_target="tpu_custom_call" | custom-call | flops 2717908992 | bytes 21823488 | tf_op jit(solution)/shard_map/pallas_call | solution.py:622
  165.0 28.4 %shard_map.347 = (bf16[192,1664]{1,0:T(8,128)(2,1)}, bf16[192,1664]{1,0:T(8,128)(2,1)}, bf16[192,1664]{1,0:T(8,128)(2,1)}, bf16[192,1664]{1,0:T(8,128)(2,1)}, f32[576,768]{1,0:T(8,128)}, /*index=5*/f32[576,768]{1,0:T(8,128)}) custom-call(s32[5]{0:T(128)} %pad_add_fusion.2.place_ref, bf16[2,576,384]{2,1,0:T(8,128)(2,1)} %bitcast.30, ...), custom_call_target="tpu_custom_call" | custom-call | flops 7983857664 | bytes 36000000 | tf_op jit(solution)/shard_map/pallas_call | solution.py:789
  193.4 0.6 collective-permute-start.11
  194.1 2.1 collective-permute-start.12
  196.2 2.5 collective-permute-start.13
  198.7 4.8 %all-to-all-start.2 = ((bf16[16,24,768]{2,1,0:T(8,128)(2,1)}), bf16[16,24,768]{2,1,0:T(8,128)(2,1)S(1)}, u32[]{:S(2)}, u32[]{:S(2)}) async-start(bf16[16,24,768]{2,1,0:T(8,128)(2,1)} %bitcast.57), calls=%async_computation.3 | async-start | bytes 1179648 | tf_op jit(solution)/shard_map/all_to_all | solution.py:74
  203.5 0.9 reduce-scatter.5.cloned.1.call-done.f_ref
  204.5 14.4 %all-to-all-done.2.in_ref = bf16[16,24,768]{2,1,0:T(8,128)(2,1)S(1)} async-done(((bf16[16,24,768]{2,1,0:T(8,128)(2,1)}), bf16[16,24,768]{2,1,0:T(8,128)(2,1)S(1)}, u32[]{:S(2)}, u32[]{:S(2)}) %all-to-all-start.2) | async-done | bytes 589856 | tf_op jit(solution)/shard_map/all_to_all | solution.py:74
  218.9 0.8 copy-done.21
  220.2 3.4 %shard_map.348 = bf16[16,12,3200]{2,1,0:T(8,128)(2,1)} custom-call(bf16[192,1664]{1,0:T(8,128)(2,1)} %get-tuple-element.131.q0, bf16[192,1664]{1,0:T(8,128)(2,1)} %copy-done.21, bf16[192,1664]{1,0:T(8,128)(2,1)} %copy-done.22, bf16[192,1664]{1,0:T(8,128)(2,1)} %copy-done.23, bf16[192,1536]{1,0:T(8,128)(2,1)} %reduce-scatter.5.cloned.1.call-done.f_ref), custom_call_target="tpu_custom_call" | custom-call | flops 1277952 | bytes 3194880 | tf_op jit(solution)/shard_map/pallas_call | solution.py:863
  223.6 1.2 collective-permute-start.15
  224.8 4.9 %all-to-all-start.3 = ((bf16[16,12,3200]{2,1,0:T(8,128)(2,1)}), bf16[16,12,3200]{2,1,0:T(8,128)(2,1)S(1)}, u32[]{:S(2)}, u32[]{:S(2)}) async-start(bf16[16,12,3200]{2,1,0:T(8,128)(2,1)} %shard_map.348), calls=%async_computation.5 | async-start | bytes 3276800 | tf_op jit(solution)/shard_map/all_to_all | solution.py:74
  229.9 1.3 collective-permute-done.14.other_ref
  231.1 0.7 shard_map.350
  231.8 4.3 %shard_map.351 = f32[576,768]{1,0:T(8,128)} custom-call(bf16[576,768]{1,0:T(8,128)(2,1)} %bitcast.43, f32[576,768]{1,0:T(8,128)} %get-tuple-element.144.ga_ref, f32[576,768]{1,0:T(8,128)} %get-tuple-element.145.gh_ref, f32[576,768]{1,0:T(8,128)} %collective-permute-done.15.other_ref, f32[16,768]{1,0:T(8,128)} %get-tuple-element.115.v_ref), custom_call_target="tpu_custom_call" | custom-call | flops 11059200 | bytes 7077888 | tf_op jit(solution)/shard_map/pallas_call | solution.py:839
  236.1 14.2 %all-to-all-done.3.in_ref = bf16[16,12,3200]{2,1,0:T(8,128)(2,1)S(1)} async-done(((bf16[16,12,3200]{2,1,0:T(8,128)(2,1)}), bf16[16,12,3200]{2,1,0:T(8,128)(2,1)S(1)}, u32[]{:S(2)}, u32[]{:S(2)}) %all-to-all-start.3) | async-done | bytes 1228832 | tf_op jit(solution)/shard_map/all_to_all | solution.py:74
  250.7 1.4 collective-permute-done.16.o_ref.other_ref
  252.1 0.9 shard_map.353
  253.0 8.6 %all-to-all-start.4 = ((f32[64,8,128]{2,1,0:T(8,128)}), f32[64,8,128]{2,1,0:T(8,128)S(1)}, u32[]{:S(2)}, u32[]{:S(2)}) async-start(f32[64,8,128]{2,1,0:T(8,128)} %shard_map.353), calls=%async_computation.6 | async-start | bytes 524288 | tf_op jit(solution)/shard_map/all_to_all | solution.py:1097
  261.9 3.6 %shard_map.354 = bf16[576,768]{1,0:T(8,128)(2,1)} custom-call(f32[576,768]{1,0:T(8,128)} %get-tuple-element.151.after_ref, f32[576,768]{1,0:T(8,128)} %get-tuple-element.152.mlp_ref, f32[576,768]{1,0:T(8,128)} %collective-permute-done.17.mlpo_ref, f32[16,768]{1,0:T(8,128)} %get-tuple-element.115.v_ref), custom_call_target="tpu_custom_call" | custom-call | flops 1769472 | bytes 7077888 | tf_op jit(solution)/shard_map/pallas_call | solution.py:839
  265.5 6.9 %all-to-all-done.4.norm_ref = f32[64,8,128]{2,1,0:T(8,128)S(1)} async-done(((f32[64,8,128]{2,1,0:T(8,128)}), f32[64,8,128]{2,1,0:T(8,128)S(1)}, u32[]{:S(2)}, u32[]{:S(2)}) %all-to-all-start.4) | async-done | bytes 262176 | tf_op jit(solution)/shard_map/all_to_all | solution.py:1097
  272.5 3.8 %shard_map.355 = (f32[12,2304]{1,0:T(8,128)}, f32[12,2304]{1,0:T(8,128)}, f32[12,2304]{1,0:T(8,128)}, f32[12,768]{1,0:T(8,128)}, f32[12,768]{1,0:T(8,128)}, /*in...) custom-call(s32[5]{0:T(128)S(1)} %copy-done.12, ...), custom_call_target="tpu_custom_call" | custom-call | flops 2211840 | bytes 3000000 | tf_op jit(solution)/shard_map/pallas_call | solution.py:982
  (101 shorter events, 5.0 us)
Async XLA Ops:
  7.2 116.2 %all-gather.2.cloned.1.call-start = ((), (), s32[]{:S(2)}) async-start(), calls=%async_computation.7 | async-start | bytes 2396160 | tf_op jit(solution)/shard_map/all_gather | solution.py:1035
  10.6 26.0 %copy-start.17 = (bf16[1,1,576,768]{3,2,1,0:T(8,128)(2,1)S(1)}, bf16[1,1,576,768]{3,2,1,0:T(8,128)(2,1)}, u32[]{:S(2)}) copy-start(bf16[1,1,576,768]{3,2,1,0:T(8,128)(2,1)} %param.20) | copy-start | bytes 2654212
  10.6 29.6 %copy-start.25 = (s32[1,1,576]{2,1,0:T(1,128)S(1)}, s32[1,1,576]{2,1,0:T(1,128)}, u32[]{:S(2)}) copy-start(s32[1,1,576]{2,1,0:T(1,128)} %param.24) | copy-start | bytes 6916
  10.7 29.6 %copy-start.26 = (s32[1,1,576]{2,1,0:T(1,128)S(1)}, s32[1,1,576]{2,1,0:T(1,128)}, u32[]{:S(2)}) copy-start(s32[1,1,576]{2,1,0:T(1,128)} %param.23) | copy-start | bytes 6916
  10.7 29.6 %copy-start.27 = (s32[1,1,2]{2,1,0:T(1,128)S(1)}, s32[1,1,2]{2,1,0:T(1,128)}, u32[]{:S(2)}) copy-start(s32[1,1,2]{2,1,0:T(1,128)} %param.22) | copy-start | bytes 28
  10.7 29.7 %copy-start = (f32[12,3072]{1,0:T(8,128)S(1)}, f32[12,3072]{1,0:T(8,128)}, u32[]{:S(2)}) copy-start(f32[12,3072]{1,0:T(8,128)} %refs_2_.1) | copy-start | bytes 442372
  35.2 14.4 %copy-start.16 = (bf16[192,2048]{1,0:T(8,128)(2,1)}, bf16[192,2048]{1,0:T(8,128)(2,1)S(1)}, u32[]{:S(2)}) copy-start(bf16[192,2048]{1,0:T(8,128)(2,1)S(1)} %reshape.116.w0.v0) | copy-start | bytes 2359300
  35.3 13.3 %collective-permute-start.2 = (bf16[192,2048]{1,0:T(8,128)(2,1)S(1)}, bf16[192,2048]{1,0:T(8,128)(2,1)S(1)}, u32[]{:S(2)}, u32[]{:S(2)}) collective-permute-start(bf16[192,2048]{1,0:T(8,128)(2,1)S(1)} %reshape.116.w0.v0), channel_id=1, source_target_pairs={{0,16},{16,32},{32,48},{48,0},{1,17},{17,33},{33,49},{49,1},{2,18}... | collective-permute-start | bytes 2359304 | tf_op jit(solution)/shard_map/ppermute | solution.py:70
  36.6 23.9 %collective-permute-start.1 = (bf16[576,768]{1,0:T(8,128)(2,1)S(1)}, bf16[576,768]{1,0:T(8,128)(2,1)}, u32[]{:S(2)}, u32[]{:S(2)}) collective-permute-start(bf16[576,768]{1,0:T(8,128)(2,1)S(1)} %bitcast.44), channel_id=1, source_target_pairs={{0,64},{64,0},{1,65},{65,1},{2,66},{66,2},{3,67},{67,3},{4,68},{68... | collective-permute-start | bytes 2654216 | tf_op jit(solution)/shard_map/ppermute | solution.py:1025
  36.7 23.8 %collective-permute-start.4 = (bf16[192,2048]{1,0:T(8,128)(2,1)S(1)}, bf16[192,2048]{1,0:T(8,128)(2,1)}, u32[]{:S(2)}, u32[]{:S(2)}) collective-permute-start(bf16[192,2048]{1,0:T(8,128)(2,1)S(1)} %reshape.116.w0.v0), channel_id=1, source_target_pairs={{0,48},{16,0},{32,16},{48,32},{1,49},{17,1},{33,17},{49,33},{2,50}... | collective-permute-start | bytes 2359304 | tf_op jit(solution)/shard_map/ppermute | solution.py:70
  38.6 21.9 %collective-permute-start.3 = (bf16[192,2048]{1,0:T(8,128)(2,1)S(1)}, bf16[192,2048]{1,0:T(8,128)(2,1)}, u32[]{:S(2)}, u32[]{:S(2)}) collective-permute-start(bf16[192,2048]{1,0:T(8,128)(2,1)S(1)} %reshape.116.w0.v0), channel_id=1, source_target_pairs={{0,32},{16,48},{32,0},{48,16},{1,33},{17,49},{33,1},{49,17},{2,34}... | collective-permute-start | bytes 2359304 | tf_op jit(solution)/shard_map/ppermute | solution.py:70
  40.3 17.1 %collective-permute-start = (s32[8,576]{1,0:T(8,128)S(1)}, s32[8,576]{1,0:T(8,128)S(1)}, u32[]{:S(2)}, u32[]{:S(2)}) collective-permute-start(s32[8,576]{1,0:T(8,128)S(1)} %get-tuple-element.176), channel_id=1, source_target_pairs={{0,64},{64,0},{1,65},{65,1},{2,66},{66,2},{3,67},{67,3},{4,68},{68... | collective-permute-start | bytes 55304 | tf_op jit(solution)/shard_map/ppermute | solution.py:1025
  48.6 12.0 %copy-start.18 = (bf16[192,2048]{1,0:T(8,128)(2,1)}, bf16[192,2048]{1,0:T(8,128)(2,1)S(1)}, u32[]{:S(2)}) copy-start(bf16[192,2048]{1,0:T(8,128)(2,1)S(1)} %collective-permute-done.2.w1.v1) | copy-start | bytes 2359300
  48.6 40.1 %collective-permute-start.7 = (bf16[576,768]{1,0:T(8,128)(2,1)}, bf16[576,768]{1,0:T(8,128)(2,1)}, u32[]{:S(2)}, u32[]{:S(2)}) collective-permute-start(bf16[576,768]{1,0:T(8,128)(2,1)} %bitcast.55), channel_id=1, source_target_pairs={{0,64},{64,0},{1,65},{65,1},{2,66},{66,2},{3,67},{67,3},{4,68},{68... | collective-permute-start | bytes 2654216 | tf_op jit(solution)/shard_map/ppermute | solution.py:1025
  49.6 24.9 %all-to-all-start.1 = ((bf16[16,12,1536]{2,1,0:T(8,128)(2,1)}), bf16[16,12,1536]{2,1,0:T(8,128)(2,1)S(1)}, u32[]{:S(2)}, u32[]{:S(2)}) async-start(bf16[16,12,1536]{2,1,0:T(8,128)(2,1)} %broadcast_in_dim.9), calls=%async_computation.1 | async-start | bytes 1572864 | tf_op jit(solution)/shard_map/all_to_all | solution.py:74
  57.0 141.7 %reduce-scatter.3.cloned.1.call-start = ((), (), s32[]{:S(2)}) async-start(), calls=%async_computation.8 | async-start | bytes 2949120 | tf_op jit(solution)/shard_map/reduce_scatter | solution.py:1031
  74.7 32.0 %copy-start.24 = (bf16[192,1536]{1,0:T(8,128)(2,1)}, bf16[192,1536]{1,0:T(8,128)(2,1)S(1)}, u32[]{:S(2)}) copy-start(bf16[192,1536]{1,0:T(8,128)(2,1)S(1)} %reshape.118.w10) | copy-start | bytes 1769476
  74.7 15.1 %collective-permute-start.6 = (bf16[192,1536]{1,0:T(8,128)(2,1)S(1)}, bf16[192,1536]{1,0:T(8,128)(2,1)S(1)}, u32[]{:S(2)}, u32[]{:S(2)}) collective-permute-start(bf16[192,1536]{1,0:T(8,128)(2,1)S(1)} %reshape.118.w10), channel_id=1, source_target_pairs={{0,48},{16,0},{32,16},{48,32},{1,49},{17,1},{33,17},{49,33},{2,50}... | collective-permute-start | bytes 1769480 | tf_op jit(solution)/shard_map/ppermute | solution.py:70
  77.4 16.6 %collective-permute-start.5 = (bf16[192,1536]{1,0:T(8,128)(2,1)S(1)}, bf16[192,1536]{1,0:T(8,128)(2,1)S(1)}, u32[]{:S(2)}, u32[]{:S(2)}) collective-permute-start(bf16[192,1536]{1,0:T(8,128)(2,1)S(1)} %reshape.118.w10), channel_id=1, source_target_pairs={{0,16},{16,32},{32,48},{48,0},{1,17},{17,33},{33,49},{49,1},{2,18}... | collective-permute-start | bytes 1769480 | tf_op jit(solution)/shard_map/ppermute | solution.py:70
  89.8 23.2 %copy-start.28 = (bf16[192,1536]{1,0:T(8,128)(2,1)}, bf16[192,1536]{1,0:T(8,128)(2,1)S(1)}, u32[]{:S(2)}) copy-start(bf16[192,1536]{1,0:T(8,128)(2,1)S(1)} %collective-permute-done.6.w13) | copy-start | bytes 1769476
  94.0 19.1 %copy-start.29 = (bf16[192,1536]{1,0:T(8,128)(2,1)}, bf16[192,1536]{1,0:T(8,128)(2,1)S(1)}, u32[]{:S(2)}) copy-start(bf16[192,1536]{1,0:T(8,128)(2,1)S(1)} %collective-permute-done.5.w11) | copy-start | bytes 1769476
  94.0 19.1 %collective-permute-start.8 = (bf16[2,576,384]{2,1,0:T(8,128)(2,1)}, bf16[2,576,384]{2,1,0:T(8,128)(2,1)S(1)}, u32[]{:S(2)}, u32[]{:S(2)}) collective-permute-start(bf16[2,576,384]{2,1,0:T(8,128)(2,1)} %get-tuple-element.106.mine_ref.o0.o1), channel_id=1, source_target_pairs={{0,64},{64,0},{1,65},{65,1},{2,66},{66,2},{3,67},{67,3},{4,68},{68... | collective-permute-start | bytes 2654216 | tf_op jit(solution)/shard_map/ppermute | solution.py:1025
  106.7 16.6 %collective-permute-start.9 = (bf16[192,1536]{1,0:T(8,128)(2,1)S(1)}, bf16[192,1536]{1,0:T(8,128)(2,1)S(1)}, u32[]{:S(2)}, u32[]{:S(2)}) collective-permute-start(bf16[192,1536]{1,0:T(8,128)(2,1)S(1)} %reshape.118.w10), channel_id=1, source_target_pairs={{0,32},{16,48},{32,0},{48,16},{1,33},{17,49},{33,1},{49,17},{2,34}... | collective-permute-start | bytes 1769480 | tf_op jit(solution)/shard_map/ppermute | solution.py:70
  142.8 8.1 %collective-permute-start.10 = (bf16[1152,768]{1,0:T(8,128)(2,1)}, bf16[1152,768]{1,0:T(8,128)(2,1)S(1)}, u32[]{:S(2)}, u32[]{:S(2)}) collective-permute-start(bf16[1152,768]{1,0:T(8,128)(2,1)} %get-tuple-element.125.gh2_ref), channel_id=1, source_target_pairs={{0,64},{64,0},{1,65},{65,1},{2,66},{66,2},{3,67},{67,3},{4,68},{68... | collective-permute-start | bytes 5308424 | tf_op jit(solution)/shard_map/ppermute | solution.py:1025
  150.9 53.6 %reduce-scatter.5.cloned.1.call-start = ((), (), s32[]{:S(2)}) async-start(), calls=%async_computation.9 | async-start | bytes 2949120 | tf_op jit(solution)/shard_map/reduce_scatter | solution.py:1031
  193.4 25.4 %collective-permute-start.11 = (bf16[192,1664]{1,0:T(8,128)(2,1)}, bf16[192,1664]{1,0:T(8,128)(2,1)S(1)}, u32[]{:S(2)}, u32[]{:S(2)}) collective-permute-start(bf16[192,1664]{1,0:T(8,128)(2,1)} %get-tuple-element.132), channel_id=1, source_target_pairs={{0,16},{16,32},{32,48},{48,0},{1,17},{17,33},{33,49},{49,1},{2,18}... | collective-permute-start | bytes 1916936 | tf_op jit(solution)/shard_map/ppermute | solution.py:70
  194.1 24.8 %collective-permute-start.12 = (bf16[192,1664]{1,0:T(8,128)(2,1)}, bf16[192,1664]{1,0:T(8,128)(2,1)S(1)}, u32[]{:S(2)}, u32[]{:S(2)}) collective-permute-start(bf16[192,1664]{1,0:T(8,128)(2,1)} %get-tuple-element.133), channel_id=1, source_target_pairs={{0,32},{16,48},{32,0},{48,16},{1,33},{17,49},{33,1},{49,17},{2,34}... | collective-permute-start | bytes 1916936 | tf_op jit(solution)/shard_map/ppermute | solution.py:70
  196.2 22.7 %collective-permute-start.13 = (bf16[192,1664]{1,0:T(8,128)(2,1)}, bf16[192,1664]{1,0:T(8,128)(2,1)S(1)}, u32[]{:S(2)}, u32[]{:S(2)}) collective-permute-start(bf16[192,1664]{1,0:T(8,128)(2,1)} %get-tuple-element.134), channel_id=1, source_target_pairs={{0,48},{16,0},{32,16},{48,32},{1,49},{17,1},{33,17},{49,33},{2,50}... | collective-permute-start | bytes 1916936 | tf_op jit(solution)/shard_map/ppermute | solution.py:70
  198.7 20.1 %all-to-all-start.2 = ((bf16[16,24,768]{2,1,0:T(8,128)(2,1)}), bf16[16,24,768]{2,1,0:T(8,128)(2,1)S(1)}, u32[]{:S(2)}, u32[]{:S(2)}) async-start(bf16[16,24,768]{2,1,0:T(8,128)(2,1)} %bitcast.57), calls=%async_computation.3 | async-start | bytes 1179648 | tf_op jit(solution)/shard_map/all_to_all | solution.py:74
  223.6 8.3 %collective-permute-start.15 = (f32[576,768]{1,0:T(8,128)}, f32[576,768]{1,0:T(8,128)}, u32[]{:S(2)}, u32[]{:S(2)}) collective-permute-start(f32[576,768]{1,0:T(8,128)} %get-tuple-element.146), channel_id=1, source_target_pairs={{0,64},{64,0},{1,65},{65,1},{2,66},{66,2},{3,67},{67,3},{4,68},{68... | collective-permute-start | bytes 5308424 | tf_op jit(solution)/shard_map/ppermute | solution.py:1025
  224.8 36.9 %collective-permute-start.17 = (f32[576,768]{1,0:T(8,128)}, f32[576,768]{1,0:T(8,128)}, u32[]{:S(2)}, u32[]{:S(2)}) collective-permute-start(f32[576,768]{1,0:T(8,128)} %get-tuple-element.153), channel_id=1, source_target_pairs={{0,64},{64,0},{1,65},{65,1},{2,66},{66,2},{3,67},{67,3},{4,68},{68... | collective-permute-start | bytes 5308424 | tf_op jit(solution)/shard_map/ppermute | solution.py:1025
  224.8 25.6 %all-to-all-start.3 = ((bf16[16,12,3200]{2,1,0:T(8,128)(2,1)}), bf16[16,12,3200]{2,1,0:T(8,128)(2,1)S(1)}, u32[]{:S(2)}, u32[]{:S(2)}) async-start(bf16[16,12,3200]{2,1,0:T(8,128)(2,1)} %shard_map.348), calls=%async_computation.5 | async-start | bytes 3276800 | tf_op jit(solution)/shard_map/all_to_all | solution.py:74
  229.8 1.3 collective-permute-start.14
  250.6 1.5 collective-permute-start.16
  253.0 19.4 %all-to-all-start.4 = ((f32[64,8,128]{2,1,0:T(8,128)}), f32[64,8,128]{2,1,0:T(8,128)S(1)}, u32[]{:S(2)}, u32[]{:S(2)}) async-start(f32[64,8,128]{2,1,0:T(8,128)} %shard_map.353), calls=%async_computation.6 | async-start | bytes 524288 | tf_op jit(solution)/shard_map/all_to_all | solution.py:1097
  261.7 10.7 %copy-start.1 = (f32[12,2304]{1,0:T(8,128)S(1)}, f32[12,2304]{1,0:T(8,128)}, u32[]{:S(2)}) copy-start(f32[12,2304]{1,0:T(8,128)} %refs_0_.1) | copy-start | bytes 331780
  261.7 10.7 %copy-start.2 = (f32[48,768]{1,0:T(8,128)S(1)}, f32[48,768]{1,0:T(8,128)}, u32[]{:S(2)}) copy-start(f32[48,768]{1,0:T(8,128)} %refs_3_.1) | copy-start | bytes 442372
  261.7 10.7 %copy-start.3 = (f32[12,768]{1,0:T(8,128)S(1)}, f32[12,768]{1,0:T(8,128)}, u32[]{:S(2)}) copy-start(f32[12,768]{1,0:T(8,128)} %refs_1_.1) | copy-start | bytes 110596
  261.7 10.7 %copy-start.4 = (f32[12,3072]{1,0:T(8,128)S(1)}, f32[12,3072]{1,0:T(8,128)}, u32[]{:S(2)}) copy-start(f32[12,3072]{1,0:T(8,128)} %refs_7_.1) | copy-start | bytes 442372
  261.7 10.7 %copy-start.5 = (f32[12,3072]{1,0:T(8,128)S(1)}, f32[12,3072]{1,0:T(8,128)}, u32[]{:S(2)}) copy-start(f32[12,3072]{1,0:T(8,128)} %refs_12_.1) | copy-start | bytes 442372
  261.8 10.7 %copy-start.6 = (f32[12,2304]{1,0:T(8,128)S(1)}, f32[12,2304]{1,0:T(8,128)}, u32[]{:S(2)}) copy-start(f32[12,2304]{1,0:T(8,128)} %refs_5_.1) | copy-start | bytes 331780
  261.8 10.7 %copy-start.7 = (f32[48,768]{1,0:T(8,128)S(1)}, f32[48,768]{1,0:T(8,128)}, u32[]{:S(2)}) copy-start(f32[48,768]{1,0:T(8,128)} %refs_8_.1) | copy-start | bytes 442372
  261.8 10.7 %copy-start.8 = (f32[12,2304]{1,0:T(8,128)S(1)}, f32[12,2304]{1,0:T(8,128)}, u32[]{:S(2)}) copy-start(f32[12,2304]{1,0:T(8,128)} %refs_10_.1) | copy-start | bytes 331780
  261.8 10.7 %copy-start.9 = (f32[48,768]{1,0:T(8,128)S(1)}, f32[48,768]{1,0:T(8,128)}, u32[]{:S(2)}) copy-start(f32[48,768]{1,0:T(8,128)} %refs_13_.1) | copy-start | bytes 442372
  261.8 10.7 %copy-start.10 = (f32[12,768]{1,0:T(8,128)S(1)}, f32[12,768]{1,0:T(8,128)}, u32[]{:S(2)}) copy-start(f32[12,768]{1,0:T(8,128)} %refs_6_.1) | copy-start | bytes 110596
  261.8 10.7 %copy-start.11 = (f32[12,768]{1,0:T(8,128)S(1)}, f32[12,768]{1,0:T(8,128)}, u32[]{:S(2)}) copy-start(f32[12,768]{1,0:T(8,128)} %refs_11_.1) | copy-start | bytes 110596
  261.8 10.7 %copy-start.13 = (f32[14,12]{1,0:T(8,128)S(1)}, f32[14,12]{1,0:T(8,128)}, u32[]{:S(2)}) copy-start(f32[14,12]{1,0:T(8,128)} %refs_4_.1) | copy-start | bytes 2020
  261.8 10.7 %copy-start.14 = (f32[14,12]{1,0:T(8,128)S(1)}, f32[14,12]{1,0:T(8,128)}, u32[]{:S(2)}) copy-start(f32[14,12]{1,0:T(8,128)} %refs_9_.1) | copy-start | bytes 2020
  (8 other events, 23.2 us)
Sparse Core Ops, SparseCore 0:
  11.4 81.2 all-gather.1
  151.0 23.8 reduce-scatter.2
  177.4 27.0 reduce-scatter.4

commit v6 on v5

--- a/solution.py
+++ b/solution.py
@@ -1061,7 +1061,7 @@
     q, quarter = lax.optimization_barrier((q, quarter))
     pieces = along_line(quarter)
     mine, p0, p1 = attn_fwd_call(place, q, k, v)
-    mine, pieces[1], pieces[3], cot_other = lax.optimization_barrier((mine, pieces[1], pieces[3], cot_other))
+    mine, pieces[1], cot_other = lax.optimization_barrier((mine, pieces[1], cot_other))
     other = swap(mine)
     gy = gy_call(place, cot_own, cot_other)
     other, gy = lax.optimization_barrier((other, gy))

time: 282 us -> 276 us (0.979); the launches traced: 283 us -> 271 us
  starting transfers between devices: 56.5 us -> 45.9 us
    ppermute x9, starting transfers between devices: 14.6 us -> 3.53 us  [swap(): return lax.ppermute(a, 'grp', [(0, 1), (1, 0)])]
  transfers between devices with their start and end apart: 25 -> 25, of which waited for: 9 -> 8; matrix products, arithmetic and copies ran while one was open for 3% -> 3% of each run, Pallas kernels for 34% -> 36%
where the time goes in v6:
time: 276 us; the launch traced here: 271 us
  Pallas kernels  126 us (46%)
  waiting for transfers between devices  47.6 us (17%)
  starting transfers between devices  45.9 us (17%)
  blocking collectives  23.2 us (8%)
  between operations  15.8 us (6%)
  local copies, waits for them, and re-layouts  8.55 us (3%)
  other arithmetic  3.33 us (1%)
    pallas_call x1, Pallas kernels, attn_bwd_call(): pl.pallas_call(attn_bwd_kernel, grid_spec=pltpu.PrefetchScalarGridSpec(nu...  28.4 us
    all_to_all x3, waiting for transfers between devices, plane_swap(): return lax.all_to_all(value, BOTH, 0, 0, axis_index_groups=planes())  28.3 us
    all_to_all x1, blocking collectives, plane_swap(): return lax.all_to_all(value, BOTH, 0, 0, axis_index_groups=planes())  23.2 us
    pallas_call x1, Pallas kernels, mlp_call(): pl.pallas_call(mlp_kernel, grid_spec=pltpu.PrefetchScalarGridSpec(num_sca...  18.6 us
    all_to_all x3, starting transfers between devices, plane_swap(): return lax.all_to_all(value, BOTH, 0, 0, axis_index_groups=planes())  17.6 us
    ppermute x9, starting transfers between devices, shift(): return lax.ppermute(value, BOTH, pairs)  15.5 us
    pallas_call x1, Pallas kernels, qkv_call(): pl.pallas_call(qkv_kernel, grid_spec=pltpu.PrefetchScalarGridSpec(num_sca...  14 us
    pallas_call x1, Pallas kernels, mid_call(): pl.pallas_call(mid_kernel, grid_spec=pltpu.PrefetchScalarGridSpec(num_sca...  13.4 us
  transfers between devices with their start and end apart: 25, of which 8 were waited for; matrix products, arithmetic and copies ran while one was open for 3% of the time, Pallas kernels for 36%

profile of v6, /device:TPU:0, one launch (start us, length us, event | category | flops | bytes accessed | tf_op | source)
XLA Modules:
  0.0 270.5 jit_solution(11857814887833255128)
XLA Ops:
  7.9 2.7 %shard_map.339 = (bf16[16,12,2048]{2,1,0:T(8,128)(2,1)}, bf16[24,768]{1,0:T(8,128)(2,1)}) custom-call(s32[2]{0:T(128)} %pad_add_fusion.3.place_ref, f32[12,2304]{1,0:T(8,128)} %refs_0_.1, f32[14,12]{1,0:T(8,128)} %refs_4_.1, f32[12,768]{1,0:T(8,128)} %refs_1_.1, f32[48,768]{1,0:T(8,128)} %refs_3_.1), custom_call_target="tpu_custom_call" | custom-call | flops 27648 | bytes 1000000 | tf_op jit(solution)/shard_map/pallas_call | solution.py:226
  10.7 23.2 %all_to_all.25 = bf16[16,12,2048]{2,1,0:T(8,128)(2,1)} all-to-all(bf16[16,12,2048]{2,1,0:T(8,128)(2,1)} %get-tuple-element.96), channel_id=1, replica_groups={{0,1,2,3,4,5,6,7,8,9,10,11,12,13,14,15},{16,17,18,19,20,21,22,23,24,25,..., dimensions={0} | all-to-all | bytes 1572864 | tf_op jit(solution)/shard_map/all_to_all | solution.py:74
  33.9 1.3 reshape.116.w0.v0
  35.3 1.4 collective-permute-start.2
  36.7 2.0 collective-permute-start.4
  38.6 1.6 collective-permute-start.3
  40.4 0.6 reshape.117
  41.0 1.4 fusion
  43.2 5.3 %collective-permute-done.2.w1.v1 = bf16[192,2048]{1,0:T(8,128)(2,1)S(1)} collective-permute-done((bf16[192,2048]{1,0:T(8,128)(2,1)S(1)}, bf16[192,2048]{1,0:T(8,128)(2,1)S(1)}, u32[]{:S(2)}, u32[]{:S(2)}) %collective-permute-start.2) | collective-permute-done | bytes 786464 | tf_op jit(solution)/shard_map/ppermute | solution.py:70
  48.6 1.1 broadcast_in_dim.9
  49.6 7.4 %all-to-all-start.1 = ((bf16[16,12,1536]{2,1,0:T(8,128)(2,1)}), bf16[16,12,1536]{2,1,0:T(8,128)(2,1)S(1)}, u32[]{:S(2)}, u32[]{:S(2)}) async-start(bf16[16,12,1536]{2,1,0:T(8,128)(2,1)} %broadcast_in_dim.9), calls=%async_computation.1 | async-start | bytes 1572864 | tf_op jit(solution)/shard_map/all_to_all | solution.py:74
  57.2 0.6 pad_add_fusion.ints_ref
  59.7 0.6 pad_add_fusion.2.place_ref
  60.3 14.0 %shard_map.340 = (f32[16,768]{1,0:T(8,128)}, bf16[2,768,576]{2,1,0:T(8,128)(2,1)}, f32[1152,384]{1,0:T(8,128)}, f32[1152,384]{1,0:T(8,128)}, bf16[1152,384]{1,0:...) custom-call(s32[5]{0:T(128)} %pad_add_fusion.2.place_ref, ...), custom_call_target="tpu_custom_call" | custom-call | flops 2064973824 | bytes 13271040 | tf_op jit(solution)/shard_map/pallas_call | solution.py:328
  74.5 2.1 collective-permute-start.5
  76.6 11.3 %shard_map.341 = (bf16[2,576,384]{2,1,0:T(8,128)(2,1)}, bf16[6,2,208,208]{3,2,1,0:T(8,128)(2,1)}, bf16[6,576,576]{2,1,0:T(8,128)(2,1)}) custom-call(s32[5]{0:T(128)} %pad_add_fusion.2.place_ref, bf16[2,576,384]{2,1,0:T(8,128)(2,1)} %bitcast.28, bf16[2,576,384]{2,1,0:T(8,128)(2,1)} %bitcast.32, bf16[2,576,384]{2,1,0:T(8,128)(2,1)} %bitcast.36, ...), custom_call_target="tpu_custom_call" | custom-call | flops 1285029888 | bytes 12000000 | tf_op jit(solution)/shard_map/pallas_call | solution.py:401
  87.9 3.0 %collective-permute-done.5.w11 = bf16[192,1536]{1,0:T(8,128)(2,1)S(1)} collective-permute-done((bf16[192,1536]{1,0:T(8,128)(2,1)S(1)}, bf16[192,1536]{1,0:T(8,128)(2,1)S(1)}, u32[]{:S(2)}, u32[]{:S(2)}) %collective-permute-start.5) | collective-permute-done | bytes 589856 | tf_op jit(solution)/shard_map/ppermute | solution.py:70
  90.9 2.3 collective-permute-start.7
  93.2 2.8 %collective-permute-start.9 = (bf16[192,1536]{1,0:T(8,128)(2,1)S(1)}, bf16[192,1536]{1,0:T(8,128)(2,1)S(1)}, u32[]{:S(2)}, u32[]{:S(2)}) collective-permute-start(bf16[192,1536]{1,0:T(8,128)(2,1)S(1)} %reshape.118.w10), channel_id=1, source_target_pairs={{0,48},{16,0},{32,16},{48,32},{1,49},{17,1},{33,17},{49,33},{2,50}... | collective-permute-start | bytes 1769480 | tf_op jit(solution)/shard_map/ppermute | solution.py:70
  96.0 0.8 collective-permute-start.8
  96.8 3.5 %shard_map.342.gy_ref = bf16[1152,768]{1,0:T(8,128)(2,1)} custom-call(s32[5]{0:T(128)} %pad_add_fusion.2.place_ref, bf16[576,768]{1,0:T(8,128)(2,1)} %bitcast.56, bf16[576,768]{1,0:T(8,128)(2,1)} %collective-permute-done.6.co_ref), custom_call_target="tpu_custom_call" | custom-call | flops 3538944 | bytes 3538944 | tf_op jit(solution)/shard_map/pallas_call | solution.py:254
  100.4 0.9 copy-done.19
  101.3 9.3 %shard_map.343 = (f32[576,768]{1,0:T(8,128)}, f32[1152,768]{1,0:T(8,128)}, f32[1152,8]{1,0:T(8,128)}, bf16[1152,768]{1,0:T(8,128)(2,1)}) custom-call(s32[5]{0:T(128)} %pad_add_fusion.2.place_ref, bf16[2,576,384]{2,1,0:T(8,128)(2,1)} %get-tuple-element.105.mine_ref.o0.o1, bf16[2,576,384]{2,1,0:T(8,128)(2,1)} %copy-done.19, bf16[576,768]{1,0:T(8,128)(2,1)} %bitcast.41, ...), custom_call_target="tpu_custom_call" | custom-call | flops 1358954496 | bytes 10027008 | tf_op jit(solution)/shard_map/pallas_call | solution.py:449
  110.7 0.8 copy-done.29
  111.7 18.6 %shard_map.344 = (f32[576,768]{1,0:T(8,128)}, f32[576,768]{1,0:T(8,128)}, bf16[1152,768]{1,0:T(8,128)(2,1)}, bf16[1152,1536]{1,0:T(8,128)(2,1)}, bf16[1152,1536]{1,0:T(8,128)(2,1)}, /*index=5*/f32[1,1536]{1,0:T(1,128)}) custom-call(s32[5]{0:T(128)} %pad_add_fusion.2.place_ref, bf16[1152,768]{1,0:T(8,128)(2,1)} %get-tuple-element.115.h2_ref, ...), custom_call_target="tpu_custom_call" | custom-call | flops 10871635968 | bytes 30000000 | tf_op jit(solution)/shard_map/pallas_call | solution.py:523
  130.4 7.6 %shard_map.345 = bf16[1536,768]{1,0:T(8,128)(2,1)} custom-call(s32[5]{0:T(128)} %pad_add_fusion.2.place_ref, bf16[1152,1536]{1,0:T(8,128)(2,1)} %get-tuple-element.124.act_ref, bf16[1152,768]{1,0:T(8,128)(2,1)} %shard_map.342.gy_ref), custom_call_target="tpu_custom_call" | custom-call | flops 2717908992 | bytes 7667712 | tf_op jit(solution)/shard_map/pallas_call | solution.py:571
  138.5 0.8 copy-done.20
  139.3 13.4 %shard_map.346 = (bf16[768,1536]{1,0:T(8,128)(2,1)}, f32[576,768]{1,0:T(8,128)}, bf16[1152,768]{1,0:T(8,128)(2,1)}, f32[8,768]{1,0:T(8,128)}) custom-call(s32[5]{0:T(128)} %pad_add_fusion.2.place_ref, bf16[1152,768]{1,0:T(8,128)(2,1)} %get-tuple-element.115.h2_ref, bf16[1152,1536]{1,0:T(8,128)(2,1)} %get-tuple-element.120.gup_ref, ...), custom_call_target="tpu_custom_call" | custom-call | flops 2717908992 | bytes 21823488 | tf_op jit(solution)/shard_map/pallas_call | solution.py:622
  152.7 28.4 %shard_map.347 = (bf16[192,1664]{1,0:T(8,128)(2,1)}, bf16[192,1664]{1,0:T(8,128)(2,1)}, bf16[192,1664]{1,0:T(8,128)(2,1)}, bf16[192,1664]{1,0:T(8,128)(2,1)}, f32[576,768]{1,0:T(8,128)}, /*index=5*/f32[576,768]{1,0:T(8,128)}) custom-call(s32[5]{0:T(128)} %pad_add_fusion.2.place_ref, bf16[2,576,384]{2,1,0:T(8,128)(2,1)} %bitcast.30, ...), custom_call_target="tpu_custom_call" | custom-call | flops 7983857664 | bytes 36000000 | tf_op jit(solution)/shard_map/pallas_call | solution.py:789
  181.6 3.8 %collective-permute-start.12 = (bf16[192,1664]{1,0:T(8,128)(2,1)}, bf16[192,1664]{1,0:T(8,128)(2,1)S(1)}, u32[]{:S(2)}, u32[]{:S(2)}) collective-permute-start(bf16[192,1664]{1,0:T(8,128)(2,1)} %get-tuple-element.131), channel_id=1, source_target_pairs={{0,32},{16,48},{32,0},{48,16},{1,33},{17,49},{33,1},{49,17},{2,34}... | collective-permute-start | bytes 1916936 | tf_op jit(solution)/shard_map/ppermute | solution.py:70
  185.4 0.6 collective-permute-start.13
  186.0 5.3 %all-to-all-start.2 = ((bf16[16,24,768]{2,1,0:T(8,128)(2,1)}), bf16[16,24,768]{2,1,0:T(8,128)(2,1)S(1)}, u32[]{:S(2)}, u32[]{:S(2)}) async-start(bf16[16,24,768]{2,1,0:T(8,128)(2,1)} %bitcast.57), calls=%async_computation.3 | async-start | bytes 1179648 | tf_op jit(solution)/shard_map/all_to_all | solution.py:74
  191.4 1.3 reduce-scatter.5.cloned.1.call-done.f_ref
  192.7 14.0 %all-to-all-done.2.in_ref = bf16[16,24,768]{2,1,0:T(8,128)(2,1)S(1)} async-done(((bf16[16,24,768]{2,1,0:T(8,128)(2,1)}), bf16[16,24,768]{2,1,0:T(8,128)(2,1)S(1)}, u32[]{:S(2)}, u32[]{:S(2)}) %all-to-all-start.2) | async-done | bytes 589856 | tf_op jit(solution)/shard_map/all_to_all | solution.py:74
  206.8 0.8 copy-done.21
  208.0 3.4 %shard_map.348 = bf16[16,12,3200]{2,1,0:T(8,128)(2,1)} custom-call(bf16[192,1664]{1,0:T(8,128)(2,1)} %get-tuple-element.129.q0, bf16[192,1664]{1,0:T(8,128)(2,1)} %copy-done.21, bf16[192,1664]{1,0:T(8,128)(2,1)} %copy-done.22, bf16[192,1664]{1,0:T(8,128)(2,1)} %copy-done.23, bf16[192,1536]{1,0:T(8,128)(2,1)} %reduce-scatter.5.cloned.1.call-done.f_ref), custom_call_target="tpu_custom_call" | custom-call | flops 1277952 | bytes 3194880 | tf_op jit(solution)/shard_map/pallas_call | solution.py:863
  211.4 0.7 collective-permute-start.15
  212.3 4.9 %all-to-all-start.3 = ((bf16[16,12,3200]{2,1,0:T(8,128)(2,1)}), bf16[16,12,3200]{2,1,0:T(8,128)(2,1)S(1)}, u32[]{:S(2)}, u32[]{:S(2)}) async-start(bf16[16,12,3200]{2,1,0:T(8,128)(2,1)} %shard_map.348), calls=%async_computation.5 | async-start | bytes 3276800 | tf_op jit(solution)/shard_map/all_to_all | solution.py:74
  217.3 1.3 collective-permute-done.14.other_ref
  218.6 0.7 shard_map.350
  219.3 4.3 %shard_map.351 = f32[576,768]{1,0:T(8,128)} custom-call(bf16[576,768]{1,0:T(8,128)(2,1)} %bitcast.43, f32[576,768]{1,0:T(8,128)} %get-tuple-element.142.ga_ref, f32[576,768]{1,0:T(8,128)} %get-tuple-element.143.gh_ref, f32[576,768]{1,0:T(8,128)} %collective-permute-done.15.other_ref, f32[16,768]{1,0:T(8,128)} %get-tuple-element.114.v_ref), custom_call_target="tpu_custom_call" | custom-call | flops 11059200 | bytes 7077888 | tf_op jit(solution)/shard_map/pallas_call | solution.py:839
  223.6 14.3 %all-to-all-done.3.in_ref = bf16[16,12,3200]{2,1,0:T(8,128)(2,1)S(1)} async-done(((bf16[16,12,3200]{2,1,0:T(8,128)(2,1)}), bf16[16,12,3200]{2,1,0:T(8,128)(2,1)S(1)}, u32[]{:S(2)}, u32[]{:S(2)}) %all-to-all-start.3) | async-done | bytes 1228832 | tf_op jit(solution)/shard_map/all_to_all | solution.py:74
  238.2 1.4 collective-permute-done.16.o_ref.other_ref
  239.6 0.9 shard_map.353
  240.5 8.6 %all-to-all-start.4 = ((f32[64,8,128]{2,1,0:T(8,128)}), f32[64,8,128]{2,1,0:T(8,128)S(1)}, u32[]{:S(2)}, u32[]{:S(2)}) async-start(f32[64,8,128]{2,1,0:T(8,128)} %shard_map.353), calls=%async_computation.6 | async-start | bytes 524288 | tf_op jit(solution)/shard_map/all_to_all | solution.py:1097
  249.3 3.6 %shard_map.354 = bf16[576,768]{1,0:T(8,128)(2,1)} custom-call(f32[576,768]{1,0:T(8,128)} %get-tuple-element.149.after_ref, f32[576,768]{1,0:T(8,128)} %get-tuple-element.150.mlp_ref, f32[576,768]{1,0:T(8,128)} %collective-permute-done.17.mlpo_ref, f32[16,768]{1,0:T(8,128)} %get-tuple-element.114.v_ref), custom_call_target="tpu_custom_call" | custom-call | flops 1769472 | bytes 7077888 | tf_op jit(solution)/shard_map/pallas_call | solution.py:839
  252.9 6.9 %all-to-all-done.4.norm_ref = f32[64,8,128]{2,1,0:T(8,128)S(1)} async-done(((f32[64,8,128]{2,1,0:T(8,128)}), f32[64,8,128]{2,1,0:T(8,128)S(1)}, u32[]{:S(2)}, u32[]{:S(2)}) %all-to-all-start.4) | async-done | bytes 262176 | tf_op jit(solution)/shard_map/all_to_all | solution.py:1097
  260.0 3.8 %shard_map.355 = (f32[12,2304]{1,0:T(8,128)}, f32[12,2304]{1,0:T(8,128)}, f32[12,2304]{1,0:T(8,128)}, f32[12,768]{1,0:T(8,128)}, f32[12,768]{1,0:T(8,128)}, /*in...) custom-call(s32[5]{0:T(128)S(1)} %copy-done.12, ...), custom_call_target="tpu_custom_call" | custom-call | flops 2211840 | bytes 3000000 | tf_op jit(solution)/shard_map/pallas_call | solution.py:982
  (101 shorter events, 5.0 us)
Async XLA Ops:
  7.2 103.5 %all-gather.2.cloned.1.call-start = ((), (), s32[]{:S(2)}) async-start(), calls=%async_computation.7 | async-start | bytes 2396160 | tf_op jit(solution)/shard_map/all_gather | solution.py:1035
  10.6 26.0 %copy-start.17 = (bf16[1,1,576,768]{3,2,1,0:T(8,128)(2,1)S(1)}, bf16[1,1,576,768]{3,2,1,0:T(8,128)(2,1)}, u32[]{:S(2)}) copy-start(bf16[1,1,576,768]{3,2,1,0:T(8,128)(2,1)} %param.20) | copy-start | bytes 2654212
  10.6 29.6 %copy-start.25 = (s32[1,1,576]{2,1,0:T(1,128)S(1)}, s32[1,1,576]{2,1,0:T(1,128)}, u32[]{:S(2)}) copy-start(s32[1,1,576]{2,1,0:T(1,128)} %param.24) | copy-start | bytes 6916
  10.7 29.6 %copy-start.26 = (s32[1,1,576]{2,1,0:T(1,128)S(1)}, s32[1,1,576]{2,1,0:T(1,128)}, u32[]{:S(2)}) copy-start(s32[1,1,576]{2,1,0:T(1,128)} %param.23) | copy-start | bytes 6916
  10.7 29.6 %copy-start.27 = (s32[1,1,2]{2,1,0:T(1,128)S(1)}, s32[1,1,2]{2,1,0:T(1,128)}, u32[]{:S(2)}) copy-start(s32[1,1,2]{2,1,0:T(1,128)} %param.22) | copy-start | bytes 28
  10.7 29.7 %copy-start = (f32[12,3072]{1,0:T(8,128)S(1)}, f32[12,3072]{1,0:T(8,128)}, u32[]{:S(2)}) copy-start(f32[12,3072]{1,0:T(8,128)} %refs_2_.1) | copy-start | bytes 442372
  35.2 14.4 %copy-start.16 = (bf16[192,2048]{1,0:T(8,128)(2,1)}, bf16[192,2048]{1,0:T(8,128)(2,1)S(1)}, u32[]{:S(2)}) copy-start(bf16[192,2048]{1,0:T(8,128)(2,1)S(1)} %reshape.116.w0.v0) | copy-start | bytes 2359300
  35.3 13.3 %collective-permute-start.2 = (bf16[192,2048]{1,0:T(8,128)(2,1)S(1)}, bf16[192,2048]{1,0:T(8,128)(2,1)S(1)}, u32[]{:S(2)}, u32[]{:S(2)}) collective-permute-start(bf16[192,2048]{1,0:T(8,128)(2,1)S(1)} %reshape.116.w0.v0), channel_id=1, source_target_pairs={{0,16},{16,32},{32,48},{48,0},{1,17},{17,33},{33,49},{49,1},{2,18}... | collective-permute-start | bytes 2359304 | tf_op jit(solution)/shard_map/ppermute | solution.py:70
  36.6 23.7 %collective-permute-start.1 = (bf16[576,768]{1,0:T(8,128)(2,1)S(1)}, bf16[576,768]{1,0:T(8,128)(2,1)}, u32[]{:S(2)}, u32[]{:S(2)}) collective-permute-start(bf16[576,768]{1,0:T(8,128)(2,1)S(1)} %bitcast.44), channel_id=1, source_target_pairs={{0,64},{64,0},{1,65},{65,1},{2,66},{66,2},{3,67},{67,3},{4,68},{68... | collective-permute-start | bytes 2654216 | tf_op jit(solution)/shard_map/ppermute | solution.py:1025
  36.7 23.6 %collective-permute-start.4 = (bf16[192,2048]{1,0:T(8,128)(2,1)S(1)}, bf16[192,2048]{1,0:T(8,128)(2,1)}, u32[]{:S(2)}, u32[]{:S(2)}) collective-permute-start(bf16[192,2048]{1,0:T(8,128)(2,1)S(1)} %reshape.116.w0.v0), channel_id=1, source_target_pairs={{0,48},{16,0},{32,16},{48,32},{1,49},{17,1},{33,17},{49,33},{2,50}... | collective-permute-start | bytes 2359304 | tf_op jit(solution)/shard_map/ppermute | solution.py:70
  38.6 21.7 %collective-permute-start.3 = (bf16[192,2048]{1,0:T(8,128)(2,1)S(1)}, bf16[192,2048]{1,0:T(8,128)(2,1)}, u32[]{:S(2)}, u32[]{:S(2)}) collective-permute-start(bf16[192,2048]{1,0:T(8,128)(2,1)S(1)} %reshape.116.w0.v0), channel_id=1, source_target_pairs={{0,32},{16,48},{32,0},{48,16},{1,33},{17,49},{33,1},{49,17},{2,34}... | collective-permute-start | bytes 2359304 | tf_op jit(solution)/shard_map/ppermute | solution.py:70
  40.3 16.9 %collective-permute-start = (s32[8,576]{1,0:T(8,128)S(1)}, s32[8,576]{1,0:T(8,128)S(1)}, u32[]{:S(2)}, u32[]{:S(2)}) collective-permute-start(s32[8,576]{1,0:T(8,128)S(1)} %get-tuple-element.174), channel_id=1, source_target_pairs={{0,64},{64,0},{1,65},{65,1},{2,66},{66,2},{3,67},{67,3},{4,68},{68... | collective-permute-start | bytes 55304 | tf_op jit(solution)/shard_map/ppermute | solution.py:1025
  48.6 11.8 %copy-start.18 = (bf16[192,2048]{1,0:T(8,128)(2,1)}, bf16[192,2048]{1,0:T(8,128)(2,1)S(1)}, u32[]{:S(2)}) copy-start(bf16[192,2048]{1,0:T(8,128)(2,1)S(1)} %collective-permute-done.2.w1.v1) | copy-start | bytes 2359300
  48.6 39.3 %collective-permute-start.6 = (bf16[576,768]{1,0:T(8,128)(2,1)}, bf16[576,768]{1,0:T(8,128)(2,1)}, u32[]{:S(2)}, u32[]{:S(2)}) collective-permute-start(bf16[576,768]{1,0:T(8,128)(2,1)} %bitcast.55), channel_id=1, source_target_pairs={{0,64},{64,0},{1,65},{65,1},{2,66},{66,2},{3,67},{67,3},{4,68},{68... | collective-permute-start | bytes 2654216 | tf_op jit(solution)/shard_map/ppermute | solution.py:1025
  49.6 24.7 %all-to-all-start.1 = ((bf16[16,12,1536]{2,1,0:T(8,128)(2,1)}), bf16[16,12,1536]{2,1,0:T(8,128)(2,1)S(1)}, u32[]{:S(2)}, u32[]{:S(2)}) async-start(bf16[16,12,1536]{2,1,0:T(8,128)(2,1)} %broadcast_in_dim.9), calls=%async_computation.1 | async-start | bytes 1572864 | tf_op jit(solution)/shard_map/all_to_all | solution.py:74
  57.0 129.0 %reduce-scatter.3.cloned.1.call-start = ((), (), s32[]{:S(2)}) async-start(), calls=%async_computation.8 | async-start | bytes 2949120 | tf_op jit(solution)/shard_map/reduce_scatter | solution.py:1031
  74.5 21.5 %copy-start.24 = (bf16[192,1536]{1,0:T(8,128)(2,1)}, bf16[192,1536]{1,0:T(8,128)(2,1)S(1)}, u32[]{:S(2)}) copy-start(bf16[192,1536]{1,0:T(8,128)(2,1)S(1)} %reshape.118.w10) | copy-start | bytes 1769476
  74.5 16.4 %collective-permute-start.5 = (bf16[192,1536]{1,0:T(8,128)(2,1)S(1)}, bf16[192,1536]{1,0:T(8,128)(2,1)S(1)}, u32[]{:S(2)}, u32[]{:S(2)}) collective-permute-start(bf16[192,1536]{1,0:T(8,128)(2,1)S(1)} %reshape.118.w10), channel_id=1, source_target_pairs={{0,16},{16,32},{32,48},{48,0},{1,17},{17,33},{33,49},{49,1},{2,18}... | collective-permute-start | bytes 1769480 | tf_op jit(solution)/shard_map/ppermute | solution.py:70
  90.9 9.5 %copy-start.28 = (bf16[192,1536]{1,0:T(8,128)(2,1)}, bf16[192,1536]{1,0:T(8,128)(2,1)S(1)}, u32[]{:S(2)}) copy-start(bf16[192,1536]{1,0:T(8,128)(2,1)S(1)} %collective-permute-done.5.w11) | copy-start | bytes 1769476
  90.9 9.5 %collective-permute-start.7 = (bf16[2,576,384]{2,1,0:T(8,128)(2,1)}, bf16[2,576,384]{2,1,0:T(8,128)(2,1)S(1)}, u32[]{:S(2)}, u32[]{:S(2)}) collective-permute-start(bf16[2,576,384]{2,1,0:T(8,128)(2,1)} %get-tuple-element.105.mine_ref.o0.o1), channel_id=1, source_target_pairs={{0,64},{64,0},{1,65},{65,1},{2,66},{66,2},{3,67},{67,3},{4,68},{68... | collective-permute-start | bytes 2654216 | tf_op jit(solution)/shard_map/ppermute | solution.py:1025
  93.2 17.5 %collective-permute-start.9 = (bf16[192,1536]{1,0:T(8,128)(2,1)S(1)}, bf16[192,1536]{1,0:T(8,128)(2,1)S(1)}, u32[]{:S(2)}, u32[]{:S(2)}) collective-permute-start(bf16[192,1536]{1,0:T(8,128)(2,1)S(1)} %reshape.118.w10), channel_id=1, source_target_pairs={{0,48},{16,0},{32,16},{48,32},{1,49},{17,1},{33,17},{49,33},{2,50}... | collective-permute-start | bytes 1769480 | tf_op jit(solution)/shard_map/ppermute | solution.py:70
  96.0 14.7 %collective-permute-start.8 = (bf16[192,1536]{1,0:T(8,128)(2,1)S(1)}, bf16[192,1536]{1,0:T(8,128)(2,1)S(1)}, u32[]{:S(2)}, u32[]{:S(2)}) collective-permute-start(bf16[192,1536]{1,0:T(8,128)(2,1)S(1)} %reshape.118.w10), channel_id=1, source_target_pairs={{0,32},{16,48},{32,0},{48,16},{1,33},{17,49},{33,1},{49,17},{2,34}... | collective-permute-start | bytes 1769480 | tf_op jit(solution)/shard_map/ppermute | solution.py:70
  130.3 7.7 %collective-permute-start.10 = (bf16[1152,768]{1,0:T(8,128)(2,1)}, bf16[1152,768]{1,0:T(8,128)(2,1)S(1)}, u32[]{:S(2)}, u32[]{:S(2)}) collective-permute-start(bf16[1152,768]{1,0:T(8,128)(2,1)} %get-tuple-element.123.gh2_ref), channel_id=1, source_target_pairs={{0,64},{64,0},{1,65},{65,1},{2,66},{66,2},{3,67},{67,3},{4,68},{68... | collective-permute-start | bytes 5308424 | tf_op jit(solution)/shard_map/ppermute | solution.py:1025
  138.0 54.7 %reduce-scatter.5.cloned.1.call-start = ((), (), s32[]{:S(2)}) async-start(), calls=%async_computation.9 | async-start | bytes 2949120 | tf_op jit(solution)/shard_map/reduce_scatter | solution.py:1031
  181.1 25.6 %collective-permute-start.11 = (bf16[192,1664]{1,0:T(8,128)(2,1)}, bf16[192,1664]{1,0:T(8,128)(2,1)S(1)}, u32[]{:S(2)}, u32[]{:S(2)}) collective-permute-start(bf16[192,1664]{1,0:T(8,128)(2,1)} %get-tuple-element.130), channel_id=1, source_target_pairs={{0,16},{16,32},{32,48},{48,0},{1,17},{17,33},{33,49},{49,1},{2,18}... | collective-permute-start | bytes 1916936 | tf_op jit(solution)/shard_map/ppermute | solution.py:70
  181.6 25.1 %collective-permute-start.12 = (bf16[192,1664]{1,0:T(8,128)(2,1)}, bf16[192,1664]{1,0:T(8,128)(2,1)S(1)}, u32[]{:S(2)}, u32[]{:S(2)}) collective-permute-start(bf16[192,1664]{1,0:T(8,128)(2,1)} %get-tuple-element.131), channel_id=1, source_target_pairs={{0,32},{16,48},{32,0},{48,16},{1,33},{17,49},{33,1},{49,17},{2,34}... | collective-permute-start | bytes 1916936 | tf_op jit(solution)/shard_map/ppermute | solution.py:70
  185.4 21.3 %collective-permute-start.13 = (bf16[192,1664]{1,0:T(8,128)(2,1)}, bf16[192,1664]{1,0:T(8,128)(2,1)S(1)}, u32[]{:S(2)}, u32[]{:S(2)}) collective-permute-start(bf16[192,1664]{1,0:T(8,128)(2,1)} %get-tuple-element.132), channel_id=1, source_target_pairs={{0,48},{16,0},{32,16},{48,32},{1,49},{17,1},{33,17},{49,33},{2,50}... | collective-permute-start | bytes 1916936 | tf_op jit(solution)/shard_map/ppermute | solution.py:70
  186.0 20.7 %all-to-all-start.2 = ((bf16[16,24,768]{2,1,0:T(8,128)(2,1)}), bf16[16,24,768]{2,1,0:T(8,128)(2,1)S(1)}, u32[]{:S(2)}, u32[]{:S(2)}) async-start(bf16[16,24,768]{2,1,0:T(8,128)(2,1)} %bitcast.57), calls=%async_computation.3 | async-start | bytes 1179648 | tf_op jit(solution)/shard_map/all_to_all | solution.py:74
  211.4 7.9 %collective-permute-start.15 = (f32[576,768]{1,0:T(8,128)}, f32[576,768]{1,0:T(8,128)}, u32[]{:S(2)}, u32[]{:S(2)}) collective-permute-start(f32[576,768]{1,0:T(8,128)} %get-tuple-element.144), channel_id=1, source_target_pairs={{0,64},{64,0},{1,65},{65,1},{2,66},{66,2},{3,67},{67,3},{4,68},{68... | collective-permute-start | bytes 5308424 | tf_op jit(solution)/shard_map/ppermute | solution.py:1025
  212.1 37.0 %collective-permute-start.17 = (f32[576,768]{1,0:T(8,128)}, f32[576,768]{1,0:T(8,128)}, u32[]{:S(2)}, u32[]{:S(2)}) collective-permute-start(f32[576,768]{1,0:T(8,128)} %get-tuple-element.151), channel_id=1, source_target_pairs={{0,64},{64,0},{1,65},{65,1},{2,66},{66,2},{3,67},{67,3},{4,68},{68... | collective-permute-start | bytes 5308424 | tf_op jit(solution)/shard_map/ppermute | solution.py:1025
  212.3 25.6 %all-to-all-start.3 = ((bf16[16,12,3200]{2,1,0:T(8,128)(2,1)}), bf16[16,12,3200]{2,1,0:T(8,128)(2,1)S(1)}, u32[]{:S(2)}, u32[]{:S(2)}) async-start(bf16[16,12,3200]{2,1,0:T(8,128)(2,1)} %shard_map.348), calls=%async_computation.5 | async-start | bytes 3276800 | tf_op jit(solution)/shard_map/all_to_all | solution.py:74
  217.2 1.3 collective-permute-start.14
  238.1 1.5 collective-permute-start.16
  240.5 19.3 %all-to-all-start.4 = ((f32[64,8,128]{2,1,0:T(8,128)}), f32[64,8,128]{2,1,0:T(8,128)S(1)}, u32[]{:S(2)}, u32[]{:S(2)}) async-start(f32[64,8,128]{2,1,0:T(8,128)} %shard_map.353), calls=%async_computation.6 | async-start | bytes 524288 | tf_op jit(solution)/shard_map/all_to_all | solution.py:1097
  249.1 10.7 %copy-start.1 = (f32[12,2304]{1,0:T(8,128)S(1)}, f32[12,2304]{1,0:T(8,128)}, u32[]{:S(2)}) copy-start(f32[12,2304]{1,0:T(8,128)} %refs_0_.1) | copy-start | bytes 331780
  249.2 10.7 %copy-start.2 = (f32[48,768]{1,0:T(8,128)S(1)}, f32[48,768]{1,0:T(8,128)}, u32[]{:S(2)}) copy-start(f32[48,768]{1,0:T(8,128)} %refs_3_.1) | copy-start | bytes 442372
  249.2 10.7 %copy-start.3 = (f32[12,768]{1,0:T(8,128)S(1)}, f32[12,768]{1,0:T(8,128)}, u32[]{:S(2)}) copy-start(f32[12,768]{1,0:T(8,128)} %refs_1_.1) | copy-start | bytes 110596
  249.2 10.7 %copy-start.4 = (f32[12,3072]{1,0:T(8,128)S(1)}, f32[12,3072]{1,0:T(8,128)}, u32[]{:S(2)}) copy-start(f32[12,3072]{1,0:T(8,128)} %refs_7_.1) | copy-start | bytes 442372
  249.2 10.7 %copy-start.5 = (f32[12,3072]{1,0:T(8,128)S(1)}, f32[12,3072]{1,0:T(8,128)}, u32[]{:S(2)}) copy-start(f32[12,3072]{1,0:T(8,128)} %refs_12_.1) | copy-start | bytes 442372
  249.2 10.7 %copy-start.6 = (f32[12,2304]{1,0:T(8,128)S(1)}, f32[12,2304]{1,0:T(8,128)}, u32[]{:S(2)}) copy-start(f32[12,2304]{1,0:T(8,128)} %refs_5_.1) | copy-start | bytes 331780
  249.2 10.7 %copy-start.7 = (f32[48,768]{1,0:T(8,128)S(1)}, f32[48,768]{1,0:T(8,128)}, u32[]{:S(2)}) copy-start(f32[48,768]{1,0:T(8,128)} %refs_8_.1) | copy-start | bytes 442372
  249.2 10.7 %copy-start.8 = (f32[12,2304]{1,0:T(8,128)S(1)}, f32[12,2304]{1,0:T(8,128)}, u32[]{:S(2)}) copy-start(f32[12,2304]{1,0:T(8,128)} %refs_10_.1) | copy-start | bytes 331780
  249.2 10.7 %copy-start.9 = (f32[48,768]{1,0:T(8,128)S(1)}, f32[48,768]{1,0:T(8,128)}, u32[]{:S(2)}) copy-start(f32[48,768]{1,0:T(8,128)} %refs_13_.1) | copy-start | bytes 442372
  249.2 10.7 %copy-start.10 = (f32[12,768]{1,0:T(8,128)S(1)}, f32[12,768]{1,0:T(8,128)}, u32[]{:S(2)}) copy-start(f32[12,768]{1,0:T(8,128)} %refs_6_.1) | copy-start | bytes 110596
  249.3 10.7 %copy-start.11 = (f32[12,768]{1,0:T(8,128)S(1)}, f32[12,768]{1,0:T(8,128)}, u32[]{:S(2)}) copy-start(f32[12,768]{1,0:T(8,128)} %refs_11_.1) | copy-start | bytes 110596
  249.3 10.7 %copy-start.13 = (f32[14,12]{1,0:T(8,128)S(1)}, f32[14,12]{1,0:T(8,128)}, u32[]{:S(2)}) copy-start(f32[14,12]{1,0:T(8,128)} %refs_4_.1) | copy-start | bytes 2020
  249.3 10.7 %copy-start.14 = (f32[14,12]{1,0:T(8,128)S(1)}, f32[14,12]{1,0:T(8,128)}, u32[]{:S(2)}) copy-start(f32[14,12]{1,0:T(8,128)} %refs_9_.1) | copy-start | bytes 2020
  249.3 10.7 %copy-start.15 = (f32[14,12]{1,0:T(8,128)S(1)}, f32[14,12]{1,0:T(8,128)}, u32[]{:S(2)}) copy-start(f32[14,12]{1,0:T(8,128)} %refs_14_.1) | copy-start | bytes 2020
  (8 other events, 13.6 us)
Sparse Core Ops, SparseCore 0:
  11.4 81.0 all-gather.1
  138.1 24.7 reduce-scatter.2
  165.3 27.3 reduce-scatter.4
